TPU v7x, 256 devices: a whole 4x4x8 slice. The times are simulated.
256 devices in a mesh: brick: 128 (over z, x_lo, y, core), orb: 2 (over x_hi).
Axes of the slice: x: 4 (x_hi: 2, x_lo: 2; x = x_hi * 2 + x_lo), y: 4, z: 8, core: 2. Of those that a mesh axis runs over, the one named last changes fastest.
Arguments:
- orbitals: float32 [64, 128, 6, 6, 128], P('orb', 'brick'), may hold values from -24 to 24
- potential: float32 [128, 6, 6, 128], P('brick'), may hold values from 0 to 2
Outputs:
- filtered: float32 [64, 128, 6, 6, 128], P('orb', 'brick')
- hamiltonian: float32 [64, 64], P('orb')
- margin: float32 [64, 64], P('orb')
All inputs are finite; a program needn't handle non-finite values.
Results may differ from a plain program's by a relative error of at most 0.00005.
Values sent between devices are 32-bit elements; how exact they have to be, the bound alone decides.
No kernel may reach another device: no remote copies, remote signals or barrier semaphores. Data moves between devices by JAX's collectives and lax.ppermute only.
A program may use at most 64 MiB of HBM per device.

v0:
```python
import jax
import jax.numpy as jnp
from jax import lax
from jax.sharding import PartitionSpec as P

BX = 16
DEGREE = 3


stencil_weights = (
    -5369.0 / 1800.0,
    12.0 / 7.0,
    -15.0 / 56.0,
    10.0 / 189.0,
    -1.0 / 112.0,
    2.0 / 825.0,
    -1.0 / 4752.0,
)
lower_edge = 0.0
cut_edge = 3.0
upper_edge = 13.0


def shifted(shard, axis, by):
    devices = lax.axis_size(axis)
    pairs = [(i, i + by) for i in range(devices) if 0 <= i + by < devices]
    return lax.ppermute(shard, axis, pairs)


def along_axis(extended, axis_number, length):
    summed = None
    for offset in range(1, 7):
        ahead_part = lax.slice_in_dim(extended, 6 + offset, 6 + offset + length, axis=axis_number)
        behind_part = lax.slice_in_dim(extended, 6 - offset, 6 - offset + length, axis=axis_number)
        weighted = stencil_weights[offset] * (ahead_part + behind_part)
        summed = weighted if summed is None else summed + weighted
    return summed


def apply_hamiltonian(values, local_potential, keep_below, keep_above, stride_x):
    width_x = values.shape[1]
    width_y = values.shape[2]
    planes_z = values.shape[3]
    below_x = shifted(values, "brick", stride_x)
    above_x = shifted(values, "brick", -stride_x)
    padded_x = jnp.concatenate([below_x, values, above_x], axis=1)
    below_y = shifted(padded_x, "brick", 1) * keep_below
    above_y = shifted(padded_x, "brick", -1) * keep_above
    padded_both = jnp.concatenate([below_y, padded_x, above_y], axis=2)
    padded_y = padded_both[:, 6 : 6 + width_x]
    padded_z = jnp.pad(values, ((0, 0), (0, 0), (0, 0), (6, 6)))
    laplace = (
        3.0 * stencil_weights[0] * values
        + along_axis(padded_x, 1, width_x)
        + along_axis(padded_y, 2, width_y)
        + along_axis(padded_z, 3, planes_z)
    )
    return -0.5 * laplace + local_potential * values


def local(orbitals, potential):
    values = orbitals[:, 0]
    local_potential = potential[0]
    stride_x = lax.axis_size("brick") // BX
    position_y = lax.axis_index("brick") % stride_x
    keep_below = (position_y > 0).astype(jnp.float32)
    keep_above = (position_y < stride_x - 1).astype(jnp.float32)

    def hamiltonian_of(field_values):
        return apply_hamiltonian(field_values, local_potential, keep_below, keep_above, stride_x)

    half_width = (upper_edge - cut_edge) / 2.0
    centre = (upper_edge + cut_edge) / 2.0
    sigma_first = half_width / (lower_edge - centre)
    tau_value = 2.0 / sigma_first
    previous = values
    current = sigma_first / half_width * (hamiltonian_of(values) - centre * values)
    sigma_now = sigma_first
    for section in range(DEGREE - 1):
        sigma_next = 1.0 / (tau_value - sigma_now)
        following = (
            2.0 * sigma_next / half_width * (hamiltonian_of(current) - centre * current)
            - sigma_now * sigma_next * previous
        )
        previous, current, sigma_now = (current, following, sigma_next)
    applied = hamiltonian_of(current)
    mine = current.reshape(current.shape[0], -1)
    mine_applied = applied.reshape(applied.shape[0], -1)
    cell_count = mine.shape[1] * lax.axis_size("brick")
    every, every_applied = (
        lax.all_gather(mine, "orb", axis=0, tiled=True),
        lax.all_gather(mine_applied, "orb", axis=0, tiled=True),
    )
    margin_rows = jnp.einsum("ic,jc->ij", mine, every, precision=lax.Precision.HIGHEST)
    energy_rows = jnp.einsum("ic,jc->ij", mine, every_applied, precision=lax.Precision.HIGHEST)
    margin, energy = lax.psum((margin_rows / cell_count, energy_rows / cell_count), "brick")
    return (current[:, None], energy, margin)


def solution(mesh):
    return jax.shard_map(
        local,
        mesh=mesh,
        in_specs=(P("orb", "brick", None, None, None), P("brick", None, None, None)),
        out_specs=(P("orb", "brick", None, None, None), P("orb", None), P("orb", None)),
        check_vma=False,
    )
```

profile of v0, /device:TPU:4, one launch (start us, length us, event | category | flops | bytes accessed | tf_op | source)
XLA Modules:
  0.0 874.9 jit_solution(7188999823969921141)
XLA Ops:
  7.2 0.0 all-gather.5.cloned.1.call-start
  7.2 1.1 copy.16
  8.3 1.3 collective-permute-start
  9.6 4.6 collective-permute-start.1
  14.2 11.1 %collective-permute-done = f32[32,6,6,128]{3,0,2,1:T(8,128)S(1)} collective-permute-done((f32[32,6,6,128]{3,0,2,1:T(8,128)S(1)}, f32[32,6,6,128]{3,0,2,1:T(8,128)S(1)}, u32[]{:S(2)}, u32[]{:S(2)}) %collective-permute-start) | collective-permute-done | bytes 589856 | tf_op jit(solution)/shard_map/ppermute | solution.py:27
  25.3 12.3 %collective-permute-done.1 = f32[32,6,6,128]{3,0,2,1:T(8,128)S(1)} collective-permute-done((f32[32,6,6,128]{3,0,2,1:T(8,128)S(1)}, f32[32,6,6,128]{3,0,2,1:T(8,128)S(1)}, u32[]{:S(2)}, u32[]{:S(2)}) %collective-permute-start.1) | collective-permute-done | bytes 589856 | tf_op jit(solution)/shard_map/ppermute | solution.py:27
  37.6 0.2 pad_maximum_fusion
  37.8 1.3 collective-permute-start.2
  39.1 4.3 collective-permute-start.3
  43.4 0.7 copy.17
  44.1 0.0 collective-permute-done.2
  44.1 1.7 broadcast_multiply_fusion.7
  45.8 1.7 broadcast_multiply_fusion.3
  47.6 5.6 broadcast_multiply_fusion.8
  53.1 0.0 copy-start.4
  53.1 1.3 collective-permute-start.4
  54.4 26.6 %collective-permute-start.5 = (f32[32,6,6,128]{3,0,2,1:T(8,128)S(1)}, f32[32,6,6,128]{3,0,2,1:T(8,128)S(1)}, u32[]{:S(2)}, u32[]{:S(2)}) collective-permute-start(f32[32,6,6,128]{3,0,2,1:T(8,128)S(1)} %get-tuple-element.8), channel_id=1, source_target_pairs={{0,16},{2,18},{4,20},{6,22},{8,24},{10,26},{12,28},{14,30},{16,32}... | collective-permute-start | bytes 1769480 | tf_op jit(solution)/shard_map/ppermute | solution.py:27
  81.0 7.9 collective-permute-done.4
  88.9 12.8 %collective-permute-done.5 = f32[32,6,6,128]{3,0,2,1:T(8,128)S(1)} collective-permute-done((f32[32,6,6,128]{3,0,2,1:T(8,128)S(1)}, f32[32,6,6,128]{3,0,2,1:T(8,128)S(1)}, u32[]{:S(2)}, u32[]{:S(2)}) %collective-permute-start.5) | collective-permute-done | bytes 589856 | tf_op jit(solution)/shard_map/ppermute | solution.py:27
  101.7 0.1 pad_maximum_fusion.1
  101.9 1.3 collective-permute-start.6
  103.2 3.1 collective-permute-start.7
  106.3 1.1 collective-permute-done.6
  107.4 0.2 broadcast_multiply_fusion.6
  107.7 0.0 copy-start.1
  107.7 1.8 collective-permute-done.7
  109.5 0.2 broadcast_multiply_fusion.2
  109.7 5.7 fusion.68
  115.4 1.3 collective-permute-start.8
  116.7 28.3 %collective-permute-start.9 = (f32[32,6,6,128]{3,0,2,1:T(8,128)S(1)}, f32[32,6,6,128]{3,0,2,1:T(8,128)S(1)}, u32[]{:S(2)}, u32[]{:S(2)}) collective-permute-start(f32[32,6,6,128]{3,0,2,1:T(8,128)S(1)} %fusion.68), channel_id=1, source_target_pairs={{0,16},{2,18},{4,20},{6,22},{8,24},{10,26},{12,28},{14,30},{16,32}... | collective-permute-start | bytes 1769480 | tf_op jit(solution)/shard_map/ppermute | solution.py:27
  145.0 5.9 collective-permute-done.8
  150.9 12.8 %collective-permute-done.9 = f32[32,6,6,128]{3,0,2,1:T(8,128)S(1)} collective-permute-done((f32[32,6,6,128]{3,0,2,1:T(8,128)S(1)}, f32[32,6,6,128]{3,0,2,1:T(8,128)S(1)}, u32[]{:S(2)}, u32[]{:S(2)}) %collective-permute-start.9) | collective-permute-done | bytes 589856 | tf_op jit(solution)/shard_map/ppermute | solution.py:27
  163.6 0.1 pad_maximum_fusion.2
  163.8 1.3 collective-permute-start.10
  165.1 3.1 collective-permute-start.11
  168.2 1.1 collective-permute-done.10
  169.4 0.2 broadcast_multiply_fusion.5
  169.5 1.9 collective-permute-done.11
  171.4 0.2 broadcast_multiply_fusion.1
  171.6 5.5 fusion.39
  177.2 1.3 collective-permute-start.12
  178.5 29.7 %collective-permute-start.13 = (f32[32,6,6,128]{3,0,2,1:T(8,128)S(1)}, f32[32,6,6,128]{3,0,2,1:T(8,128)S(1)}, u32[]{:S(2)}, u32[]{:S(2)}) collective-permute-start(f32[32,6,6,128]{3,0,2,1:T(8,128)S(1)} %fusion.39), channel_id=1, source_target_pairs={{0,16},{2,18},{4,20},{6,22},{8,24},{10,26},{12,28},{14,30},{16,32}... | collective-permute-start | bytes 1769480 | tf_op jit(solution)/shard_map/ppermute | solution.py:27
  208.2 5.9 collective-permute-done.12
  214.1 11.1 %collective-permute-done.13 = f32[32,6,6,128]{3,0,2,1:T(8,128)S(1)} collective-permute-done((f32[32,6,6,128]{3,0,2,1:T(8,128)S(1)}, f32[32,6,6,128]{3,0,2,1:T(8,128)S(1)}, u32[]{:S(2)}, u32[]{:S(2)}) %collective-permute-start.13) | collective-permute-done | bytes 589856 | tf_op jit(solution)/shard_map/ppermute | solution.py:27
  225.2 1.5 pad_maximum_fusion.3
  226.7 1.3 collective-permute-start.14
  228.0 4.2 collective-permute-start.15
  232.2 0.4 copy.6
  232.6 1.0 reshape.12
  233.5 0.0 all-gather.5.cloned.1.call-update
  233.5 0.2 all-gather.3.cloned.1.call-start
  233.8 1.7 broadcast_multiply_fusion.4
  235.5 0.0 copy-start.3
  235.5 1.7 broadcast_multiply_fusion
  237.2 5.4 fusion.10
  242.6 0.4 copy.7
  243.0 1.0 reshape.13
  244.0 0.0 all-gather.3.cloned.1.call-update
  244.0 1.4 copy.8
  245.4 28.1 %all-gather.5.cloned.1.call-done = f32[64,4608]{1,0:T(8,128)} async-done(((f32[32,4608]{1,0:T(8,128)}), f32[64,4608]{1,0:T(8,128)}) %all-gather.5.cloned.1.call-update) | async-done | bytes 1179664 | tf_op jit(solution)/shard_map/all_gather | solution.py:91
  273.6 2.3 convolution_multiply_fusion
  275.9 34.7 %all-gather.3.cloned.1.call-done = f32[64,4608]{1,0:T(8,128)} async-done(((f32[32,4608]{1,0:T(8,128)}), f32[64,4608]{1,0:T(8,128)}) %all-gather.3.cloned.1.call-update) | async-done | bytes 1179664 | tf_op jit(solution)/shard_map/all_gather | solution.py:92
  310.6 2.3 convolution_multiply_fusion.1
  313.0 555.1 %all-reduce.4 = (f32[32,64]{1,0:T(8,128)}, f32[32,64]{1,0:T(8,128)}) all-reduce(f32[32,64]{1,0:T(8,128)S(1)} %convolution_multiply_fusion.1, f32[32,64]{1,0:T(8,128)S(1)} %convolution_multiply_fusion), channel_id=1, replica_groups=mesh['brick'=128,'orb'=2] {'brick'}, use_global_device_ids=true, to_apply=%region_0.1 | all-reduce | flops 4096 | bytes 32768 | tf_op jit(solution)/shard_map/psum | solution.py:96
  (11 shorter events, 0.0 us)
Async XLA Ops:
  7.2 266.4 %all-gather.5.cloned.1.call-start = ((), (), s32[]{:S(2)}) async-start(), calls=%async_computation.1 | async-start | bytes 1769472 | tf_op jit(solution)/shard_map/all_gather | solution.py:91
  8.3 17.0 %collective-permute-start = (f32[32,6,6,128]{3,0,2,1:T(8,128)S(1)}, f32[32,6,6,128]{3,0,2,1:T(8,128)S(1)}, u32[]{:S(2)}, u32[]{:S(2)}) collective-permute-start(f32[32,6,6,128]{3,0,2,1:T(8,128)S(1)} %bitcast.16), channel_id=1, source_target_pairs={{16,0},{18,2},{20,4},{22,6},{24,8},{26,10},{28,12},{30,14},{32,16}... | collective-permute-start | bytes 1769480 | tf_op jit(solution)/shard_map/ppermute | solution.py:27
  9.6 27.9 %collective-permute-start.1 = (f32[32,6,6,128]{3,0,2,1:T(8,128)S(1)}, f32[32,6,6,128]{3,0,2,1:T(8,128)S(1)}, u32[]{:S(2)}, u32[]{:S(2)}) collective-permute-start(f32[32,6,6,128]{3,0,2,1:T(8,128)S(1)} %bitcast.17), channel_id=1, source_target_pairs={{0,16},{2,18},{4,20},{6,22},{8,24},{10,26},{12,28},{14,30},{16,32}... | collective-permute-start | bytes 1769480 | tf_op jit(solution)/shard_map/ppermute | solution.py:27
  37.8 6.3 collective-permute-start.2
  39.1 6.8 collective-permute-start.3
  44.1 127.5 %copy-start.2 = (f32[1,6,6,128]{3,2,0,1:T(8,128)}, f32[1,6,6,128]{3,2,0,1:T(8,128)S(1)}, u32[]{:S(2)}) copy-start(f32[1,6,6,128]{3,2,0,1:T(8,128)S(1)} %copy.17) | copy-start | bytes 55300
  53.1 53.2 %copy-start.4 = (f32[1,6,6,128]{3,0,2,1:T(1,128)S(1)}, f32[1,6,6,128]{3,0,2,1:T(1,128)}, u32[]{:S(2)}) copy-start(f32[1,6,6,128]{3,0,2,1:T(1,128)} %param.3) | copy-start | bytes 55300
  53.1 35.8 %collective-permute-start.4 = (f32[32,6,6,128]{3,0,2,1:T(8,128)S(1)}, f32[32,6,6,128]{3,0,2,1:T(8,128)S(1)}, u32[]{:S(2)}, u32[]{:S(2)}) collective-permute-start(f32[32,6,6,128]{3,0,2,1:T(8,128)S(1)} %get-tuple-element.8), channel_id=1, source_target_pairs={{16,0},{18,2},{20,4},{22,6},{24,8},{26,10},{28,12},{30,14},{32,16}... | collective-permute-start | bytes 1769480 | tf_op jit(solution)/shard_map/ppermute | solution.py:27
  54.4 47.3 %collective-permute-start.5 = (f32[32,6,6,128]{3,0,2,1:T(8,128)S(1)}, f32[32,6,6,128]{3,0,2,1:T(8,128)S(1)}, u32[]{:S(2)}, u32[]{:S(2)}) collective-permute-start(f32[32,6,6,128]{3,0,2,1:T(8,128)S(1)} %get-tuple-element.8), channel_id=1, source_target_pairs={{0,16},{2,18},{4,20},{6,22},{8,24},{10,26},{12,28},{14,30},{16,32}... | collective-permute-start | bytes 1769480 | tf_op jit(solution)/shard_map/ppermute | solution.py:27
  101.9 5.6 collective-permute-start.6
  103.2 6.3 collective-permute-start.7
  107.7 2.0 copy-start.1
  115.4 35.5 %collective-permute-start.8 = (f32[32,6,6,128]{3,0,2,1:T(8,128)S(1)}, f32[32,6,6,128]{3,0,2,1:T(8,128)S(1)}, u32[]{:S(2)}, u32[]{:S(2)}) collective-permute-start(f32[32,6,6,128]{3,0,2,1:T(8,128)S(1)} %fusion.68), channel_id=1, source_target_pairs={{16,0},{18,2},{20,4},{22,6},{24,8},{26,10},{28,12},{30,14},{32,16}... | collective-permute-start | bytes 1769480 | tf_op jit(solution)/shard_map/ppermute | solution.py:27
  116.7 47.0 %collective-permute-start.9 = (f32[32,6,6,128]{3,0,2,1:T(8,128)S(1)}, f32[32,6,6,128]{3,0,2,1:T(8,128)S(1)}, u32[]{:S(2)}, u32[]{:S(2)}) collective-permute-start(f32[32,6,6,128]{3,0,2,1:T(8,128)S(1)} %fusion.68), channel_id=1, source_target_pairs={{0,16},{2,18},{4,20},{6,22},{8,24},{10,26},{12,28},{14,30},{16,32}... | collective-permute-start | bytes 1769480 | tf_op jit(solution)/shard_map/ppermute | solution.py:27
  163.8 5.6 collective-permute-start.10
  165.1 6.3 collective-permute-start.11
  177.2 36.9 %collective-permute-start.12 = (f32[32,6,6,128]{3,0,2,1:T(8,128)S(1)}, f32[32,6,6,128]{3,0,2,1:T(8,128)S(1)}, u32[]{:S(2)}, u32[]{:S(2)}) collective-permute-start(f32[32,6,6,128]{3,0,2,1:T(8,128)S(1)} %fusion.39), channel_id=1, source_target_pairs={{16,0},{18,2},{20,4},{22,6},{24,8},{26,10},{28,12},{30,14},{32,16}... | collective-permute-start | bytes 1769480 | tf_op jit(solution)/shard_map/ppermute | solution.py:27
  178.5 46.7 %collective-permute-start.13 = (f32[32,6,6,128]{3,0,2,1:T(8,128)S(1)}, f32[32,6,6,128]{3,0,2,1:T(8,128)S(1)}, u32[]{:S(2)}, u32[]{:S(2)}) collective-permute-start(f32[32,6,6,128]{3,0,2,1:T(8,128)S(1)} %fusion.39), channel_id=1, source_target_pairs={{0,16},{2,18},{4,20},{6,22},{8,24},{10,26},{12,28},{14,30},{16,32}... | collective-permute-start | bytes 1769480 | tf_op jit(solution)/shard_map/ppermute | solution.py:27
  226.7 7.1 collective-permute-start.14
  228.0 7.5 collective-permute-start.15
  233.5 77.1 %all-gather.3.cloned.1.call-start = ((), (), s32[]{:S(2)}) async-start(), calls=%async_computation | async-start | bytes 1769472 | tf_op jit(solution)/shard_map/all_gather | solution.py:92
  235.5 1.7 copy-start.3
  243.0 30.6 %copy-start = (f32[32,4608]{1,0:T(8,128)S(1)}, f32[32,4608]{1,0:T(8,128)}, u32[]{:S(2)}) copy-start(f32[32,4608]{1,0:T(8,128)} %reshape.12) | copy-start | bytes 1769476
Sparse Core Ops, SparseCore 0:
  233.7 39.8 all-gather.4
  275.3 35.2 all-gather.2
where the time goes:
time: 876 us; the launch traced here: 875 us
  blocking collectives  555 us (63%)
  waiting for transfers between devices  149 us (17%)
  starting transfers between devices  115 us (13%)
  other arithmetic  31.7 us (4%)
  between operations  14.4 us (2%)
    psum x1, blocking collectives, local(): lax.psum((margin_rows / cell_count, energy_rows / cell_count), 'brick')  555 us
    ppermute x16, starting transfers between devices, shifted(): return lax.ppermute(shard, axis, pairs)  114 us
    ppermute x16, waiting for transfers between devices, shifted(): return lax.ppermute(shard, axis, pairs)  85.6 us
    all_gather x1, waiting for transfers between devices, local(): lax.all_gather(mine_applied, 'orb', axis=0, tiled=True)  34.7 us
    all_gather x1, waiting for transfers between devices, local(): lax.all_gather(mine, 'orb', axis=0, tiled=True)  28.1 us
  transfers between devices with their start and end apart: 18, of which 14 were waited for; matrix products, arithmetic and copies ran while one was open for 2% of the time, Pallas kernels for 0%

commit v1 on v0

v1 whole, which is shorter than its diff:
```python
import jax
import jax.numpy as jnp
from jax import lax
from jax.experimental import pallas as pl
from jax.experimental.pallas import tpu as pltpu
from jax.sharding import Mesh, PartitionSpec as P

weights = (
    -5369.0 / 1800.0,
    12.0 / 7.0,
    -15.0 / 56.0,
    10.0 / 189.0,
    -1.0 / 112.0,
    2.0 / 825.0,
    -1.0 / 4752.0,
)
lower_edge = 0.0
cut_edge = 3.0
upper_edge = 13.0
CELLS = 96 * 48 * 128

VM = pl.BlockSpec(memory_space=pltpu.VMEM)
SM = pl.BlockSpec(memory_space=pltpu.SMEM)
PARAMS = pltpu.CompilerParams(vmem_limit_bytes=32 * 1024 * 1024)
F32 = jnp.float32

HALF = jax.ShapeDtypeStruct((6, 2, 6, 8, 128), F32)
RAW = jax.ShapeDtypeStruct((1152, 128), F32)


def call(body, outs, inputs, specs=None, flops=1_000_000):
    return pl.pallas_call(
        body,
        out_shape=outs,
        in_specs=specs or [VM] * len(inputs),
        out_specs=jax.tree.map(lambda _: VM, outs),
        compiler_params=PARAMS,
        cost_estimate=pl.CostEstimate(flops=flops, bytes_accessed=2_000_000, transcendentals=0),
    )(*inputs)


def unpack_body(raw, low, high):
    for half, ref in ((0, low), (1, high)):
        for o in range(2):
            for xi in range(6):
                for yi in range(6):
                    start = half * 576 + o * 36 + xi * 6 + yi
                    ref[xi, o, yi] = raw[pl.ds(start, 8, stride=72), :]


def interior_body(alpha, shift, beta, has_previous, *refs):
    if has_previous:
        low, high, potential, previous_low, previous_high, acc_low, acc_high = refs
    else:
        low, high, potential, acc_low, acc_high = refs
    halves = (low, high)
    accs = (acc_low, acc_high)
    scaled = [-0.5 * alpha * w for w in weights]
    row = lax.broadcasted_iota(jnp.int32, (128, 128), 0)
    column = lax.broadcasted_iota(jnp.int32, (128, 128), 1)
    distance = jnp.abs(row - column)
    band = jnp.zeros((128, 128), F32)
    for k in range(1, 7):
        band = jnp.where(distance == k, F32(scaled[k]), band)
    band = jnp.where(distance == 0, F32(3.0 * scaled[0] - alpha * shift), band)
    sub = lax.broadcasted_iota(jnp.int32, (8, 128), 0)
    for x in range(12):
        here = halves[x // 6][x % 6]
        along = jnp.dot(
            here.reshape(96, 128), band, precision=lax.Precision.HIGHEST, preferred_element_type=F32
        ).reshape(2, 6, 8, 128)
        for o in range(2):
            own = [here[o, yi] for yi in range(6)]
            behind = [jnp.where(sub == 0, 0.0, pltpu.roll(v, 1, 0)) for v in own]
            ahead = [jnp.where(sub == 7, 0.0, pltpu.roll(v, 7, 0)) for v in own]
            line = behind + own + ahead
            for yi in range(6):
                start = (x // 6) * 288 + (x % 6) * 6 + yi
                local = potential[pl.ds(start, 8, stride=36), :] * F32(alpha)
                total = along[o, yi] + local * own[yi]
                for k in range(1, 7):
                    pair = line[6 + yi + k] + line[6 + yi - k]
                    if x + k < 12:
                        pair = pair + halves[(x + k) // 6][(x + k) % 6, o, yi]
                    if x - k >= 0:
                        pair = pair + halves[(x - k) // 6][(x - k) % 6, o, yi]
                    total = total + F32(scaled[k]) * pair
                if has_previous:
                    old = (previous_low, previous_high)[x // 6][x % 6, o, yi]
                    total = total - F32(beta) * old
                accs[x // 6][x % 6, o, yi] = total


def halo_terms(alpha, inside, acc_low, acc_high, before, after, emit):
    scaled = [-0.5 * alpha * w for w in weights]
    from_before = [inside[0] * F32(s) for s in scaled]
    from_after = [inside[1] * F32(s) for s in scaled]
    for o in range(2):
        for yi in range(6):
            lows = [before[j, o, yi] for j in range(6)]
            highs = [after[j, o, yi] for j in range(6)]
            for x in range(6):
                total = acc_low[x, o, yi]
                for k in range(x + 1, 7):
                    total = total + from_before[k] * lows[6 + x - k]
                emit(0, x, o, yi, total)
                total = acc_high[5 - x, o, yi]
                for k in range(x + 1, 7):
                    total = total + from_after[k] * highs[k - x - 1]
                emit(1, 5 - x, o, yi, total)


def edge_body(alpha, inside, acc_low, acc_high, before, after, out_low, out_high):
    outs = (out_low, out_high)

    def emit(half, x, o, yi, value):
        outs[half][x, o, yi] = value

    halo_terms(alpha, inside, acc_low, acc_high, before, after, emit)


def edge_both_body(alpha, inside, acc_low, acc_high, before, after, out_low, out_high, raw):
    outs = (out_low, out_high)

    def emit(half, x, o, yi, value):
        outs[half][x, o, yi] = value
        raw[pl.ds(half * 576 + o * 36 + x * 6 + yi, 8, stride=72), :] = value

    halo_terms(alpha, inside, acc_low, acc_high, before, after, emit)


def edge_raw_body(alpha, inside, acc_low, acc_high, before, after, raw):
    def emit(half, x, o, yi, value):
        raw[pl.ds(half * 576 + o * 36 + x * 6 + yi, 8, stride=72), :] = value

    halo_terms(alpha, inside, acc_low, acc_high, before, after, emit)


def gram_body(mine, other, applied, copies):
    total = jnp.zeros((64, 64), F32)
    for r in range(36):
        rows = pl.ds(r, 32, stride=36)
        own = mine[rows, :]
        left = jnp.concatenate([own, applied[rows, :]], axis=0)
        right = jnp.concatenate([own, other[rows, :]], axis=0)
        total = total + lax.dot_general(
            left,
            right,
            (((1,), (1,)), ((), ())),
            precision=lax.Precision.HIGHEST,
            preferred_element_type=F32,
        )
    packed = jnp.concatenate([total[:32], total[32:]], axis=1)
    for n in range(16):
        copies[n] = packed


def sum_body(parts, copies):
    total = parts[0]
    for n in range(1, 16):
        total = total + parts[n]
    for n in range(8):
        copies[n] = total


def finish_body(side, parts, energy, margin):
    total = parts[0]
    for n in range(1, 8):
        total = total + parts[n]
    total = total * F32(1.0 / CELLS)
    swapped = jnp.concatenate(
        [total[:, 32:64], total[:, 0:32], total[:, 96:128], total[:, 64:96]], axis=1
    )
    total = jnp.where(side[0] == 0, total, swapped)
    margin[...] = total[:, :64]
    energy[...] = total[:, 64:]


SLAB = ("xl", "y", "core")


def local(orbitals, potential):
    position = lax.axis_index("z")
    inside = jnp.stack([position > 0, position < 7]).astype(F32)
    side = lax.axis_index("xh").astype(jnp.int32).reshape(1)
    field = lax.all_gather(potential.reshape(36, 128), SLAB, axis=0, tiled=True)
    raw = lax.all_to_all(
        orbitals.reshape(16, 72, 128), SLAB, split_axis=0, concat_axis=0, tiled=True
    ).reshape(1152, 128)
    current = call(unpack_body, [HALF, HALF], [raw])
    up = [(i, (i + 1) % 8) for i in range(8)]
    down = [(i, (i + 7) % 8) for i in range(8)]

    def hamiltonian_part(alpha, shift, beta, values, previous, body, outs):
        before = lax.ppermute(values[1], "z", up)
        after = lax.ppermute(values[0], "z", down)

        def interior(*refs):
            interior_body(alpha, shift, beta, previous is not None, *refs)

        accs = call(interior, [HALF, HALF], [*values, field] + list(previous or []), flops=20_000_000)

        def edge(*refs):
            body(alpha, *refs)

        return call(edge, outs, [inside, *accs, before, after], [SM] + [VM] * 4)

    half_width = (upper_edge - cut_edge) / 2.0
    centre = (upper_edge + cut_edge) / 2.0
    sigma_first = half_width / (lower_edge - centre)
    tau_value = 2.0 / sigma_first
    previous = current
    current = hamiltonian_part(
        sigma_first / half_width, centre, 0.0, current, None, edge_body, [HALF, HALF]
    )
    sigma_second = 1.0 / (tau_value - sigma_first)
    previous, current = current, hamiltonian_part(
        2.0 * sigma_second / half_width,
        centre,
        sigma_first * sigma_second,
        current,
        previous,
        edge_body,
        [HALF, HALF],
    )
    sigma_third = 1.0 / (tau_value - sigma_second)
    low, high, filtered_raw = hamiltonian_part(
        2.0 * sigma_third / half_width,
        centre,
        sigma_second * sigma_third,
        current,
        previous,
        edge_both_body,
        [HALF, HALF, RAW],
    )

    def to_bricks(values):
        return lax.all_to_all(
            values.reshape(16, 72, 128), SLAB, split_axis=0, concat_axis=0, tiled=True
        ).reshape(1152, 128)

    filtered = to_bricks(filtered_raw)
    other = lax.ppermute(filtered, "xh", [(0, 1), (1, 0)])
    applied_raw = hamiltonian_part(1.0, 0.0, 0.0, [low, high], None, edge_raw_body, RAW)
    applied = to_bricks(applied_raw)
    copies = call(gram_body, jax.ShapeDtypeStruct((16, 32, 128), F32), [filtered, other, applied])
    parts = lax.all_to_all(copies, SLAB, split_axis=0, concat_axis=0, tiled=True)
    copies = call(sum_body, jax.ShapeDtypeStruct((8, 32, 128), F32), [parts])
    parts = lax.all_to_all(copies, "z", split_axis=0, concat_axis=0, tiled=True)
    energy, margin = call(
        finish_body,
        [jax.ShapeDtypeStruct((32, 64), F32)] * 2,
        [side, parts],
        [SM, VM],
    )
    return filtered.reshape(32, 1, 6, 6, 128), energy, margin


def solution(mesh):
    fine = Mesh(mesh.devices.reshape(8, 2, 4, 2, 2), ("z", "xl", "y", "core", "xh"))
    brick = ("z", "xl", "y", "core")
    return jax.shard_map(
        local,
        mesh=fine,
        in_specs=(P("xh", brick, None, None, None), P(brick, None, None, None)),
        out_specs=(P("xh", brick, None, None, None), P("xh", None), P("xh", None)),
        check_vma=False,
    )
```

time: 876 us -> 136 us (0.16)
  blocking collectives: 555 us -> 65.8 us
  waiting for transfers between devices: 149 us -> 34 us
  starting transfers between devices: 115 us -> 21.2 us
  other arithmetic: 31.7 us -> 0.08 us
  between operations: 14.4 us -> 0.76 us
  Pallas kernels: 0 us -> 11.8 us
    psum x1 -> x0, blocking collectives: 555 us -> none  [local(): lax.psum((margin_rows / cell_count, energy_rows / cell_count), 'brick')]
    ppermute x16 -> x9, starting transfers between devices: 114 us -> 14.2 us  [the longest x4 9.94 us: hamiltonian_part(): after = lax.ppermute(values[0], 'z', down)]
    ppermute x16 -> x9, waiting for transfers between devices: 85.6 us -> 15.5 us  [the longest x4 10.6 us: hamiltonian_part(): after = lax.ppermute(values[0], 'z', down)]
    all_gather x2 -> x0, waiting for transfers between devices: 62.9 us -> none  [the longest x1 34.7 us: local(): lax.all_gather(mine_applied, 'orb', axis=0, tiled=True)]
    all_to_all x0 -> x3, blocking collectives: none -> 47.7 us  [the longest x1 19.5 us: to_bricks(): lax.all_to_all(values.reshape(16, 72, 128), SLAB, split_axis=0, concat_ax...]
    all_to_all x0 -> x2, waiting for transfers between devices: none -> 18.5 us  [the longest x1 9.47 us: to_bricks(): lax.all_to_all(values.reshape(16, 72, 128), SLAB, split_axis=0, concat_ax...]
    all_gather x0 -> x1, blocking collectives: none -> 18.1 us  [local(): field = lax.all_gather(potential.reshape(36, 128), SLAB, axis=0, tiled=True)]
    mul x10 -> x0, other arithmetic: 13.2 us -> none  [the longest x1 5.56 us: local(): sigma_first / half_width * (hamiltonian_of(values) - centre * values)]
  transfers between devices with their start and end apart: 18 -> 11, of which waited for: 14 -> 6; matrix products, arithmetic and copies ran while one was open for 2% -> 0% of each run, Pallas kernels for 0% -> 4%
where the time goes in v1:
time: 136 us; the launch traced here: 134 us
  blocking collectives  65.8 us (48%)
  waiting for transfers between devices  34 us (25%)
  starting transfers between devices  21.2 us (16%)
  Pallas kernels  11.8 us (9%)
    all_to_all x1, blocking collectives, to_bricks(): lax.all_to_all(values.reshape(16, 72, 128), SLAB, split_axis=0, concat_ax...  19.5 us
    all_gather x1, blocking collectives, local(): field = lax.all_gather(potential.reshape(36, 128), SLAB, axis=0, tiled=True)  18.1 us
    all_to_all x1, blocking collectives, local(): lax.all_to_all(orbitals.reshape(16, 72, 128), SLAB, split_axis=0, concat_...  16.8 us
    pallas_call x12, Pallas kernels, call(): pl.pallas_call(body, out_shape=outs, in_specs=specs or [VM] * len(inputs)...  11.8 us
    all_to_all x1, blocking collectives, local(): lax.all_to_all(copies, SLAB, split_axis=0, concat_axis=0, tiled=True)  11.4 us
    ppermute x4, waiting for transfers between devices, hamiltonian_part(): after = lax.ppermute(values[0], 'z', down)  10.6 us
    ppermute x4, starting transfers between devices, hamiltonian_part(): after = lax.ppermute(values[0], 'z', down)  9.94 us
    all_to_all x1, waiting for transfers between devices, to_bricks(): lax.all_to_all(values.reshape(16, 72, 128), SLAB, split_axis=0, concat_ax...  9.47 us
  transfers between devices with their start and end apart: 11, of which 6 were waited for; matrix products, arithmetic and copies ran while one was open for 0% of the time, Pallas kernels for 4%

profile of v1, /device:TPU:4, one launch (start us, length us, event | category | flops | bytes accessed | tf_op | source)
XLA Modules:
  0.0 134.4 jit_solution(3562915679574738971)
XLA Ops:
  0.6 16.8 %all_to_all.25 = f32[16,72,128]{2,1,0:T(8,128)S(1)} all-to-all(f32[16,72,128]{2,1,0:T(8,128)} %bitcast.17), channel_id=1, replica_groups=mesh['z'=8,'xl'=2,'y'=4,'core'=2,'xh'=2] {'xl','y','core'}, dimensions={0} | all-to-all | bytes 1179648 | tf_op jit(solution)/shard_map/all_to_all | solution.py:187
  17.4 0.0 copy-start
  17.4 0.1 shard_map.49
  17.6 5.9 %collective-permute-start.1 = (f32[6,2,6,8,128]{4,3,2,1,0:T(8,128)S(1)}, f32[6,2,6,8,128]{4,3,2,1,0:T(8,128)S(1)}, u32[]{:S(2)}, u32[]{:S(2)}) collective-permute-start(f32[6,2,6,8,128]{4,3,2,1,0:T(8,128)S(1)} %get-tuple-element.22.refs_0_.refs_3_), channel_id=1, source_target_pairs={{0,224},{32,0},{64,32},{96,64},{128,96},{160,128},{192,160},{224,1... | collective-permute-start | bytes 884744 | tf_op jit(solution)/shard_map/ppermute | solution.py:196
  23.5 0.0 collective-permute-start
  23.5 0.0 copy-done
  23.5 18.1 %all-gather = f32[16,36,128]{2,1,0:T(8,128)S(1)} all-gather(f32[1,36,128]{2,1,0:T(8,128)S(1)} %copy.7), channel_id=1, replica_groups=mesh['z'=8,'xl'=2,'y'=4,'core'=2,'xh'=2] {'xl','y','core'}, dimensions={0}, use_global_device_ids=true | all-gather | bytes 313344 | tf_op jit(solution)/shard_map/all_gather | solution.py:186
  41.6 0.1 add_convert_fusion.refs_0_
  41.7 1.1 shard_map.50
  42.8 0.0 collective-permute-done.1.refs_4_
  42.8 0.0 collective-permute-done.refs_3_
  42.8 0.7 shard_map.51
  43.5 3.3 %collective-permute-start.3 = (f32[6,2,6,8,128]{4,3,2,1,0:T(8,128)S(1)}, f32[6,2,6,8,128]{4,3,2,1,0:T(8,128)S(1)}, u32[]{:S(2)}, u32[]{:S(2)}) collective-permute-start(f32[6,2,6,8,128]{4,3,2,1,0:T(8,128)S(1)} %get-tuple-element.26.refs_0_.refs_3_), channel_id=1, source_target_pairs={{0,224},{32,0},{64,32},{96,64},{128,96},{160,128},{192,160},{224,1... | collective-permute-start | bytes 884744 | tf_op jit(solution)/shard_map/ppermute | solution.py:196
  46.8 0.0 collective-permute-start.2
  46.8 1.1 shard_map.52
  47.9 5.6 %collective-permute-done.3.refs_4_ = f32[6,2,6,8,128]{4,3,2,1,0:T(8,128)S(1)} collective-permute-done((f32[6,2,6,8,128]{4,3,2,1,0:T(8,128)S(1)}, f32[6,2,6,8,128]{4,3,2,1,0:T(8,128)S(1)}, u32[]{:S(2)}, u32[]{:S(2)}) %collective-permute-start.3) | collective-permute-done | bytes 294944 | tf_op jit(solution)/shard_map/ppermute | solution.py:196
  53.6 3.4 %collective-permute-done.2.refs_3_ = f32[6,2,6,8,128]{4,3,2,1,0:T(8,128)S(1)} collective-permute-done((f32[6,2,6,8,128]{4,3,2,1,0:T(8,128)S(1)}, f32[6,2,6,8,128]{4,3,2,1,0:T(8,128)S(1)}, u32[]{:S(2)}, u32[]{:S(2)}) %collective-permute-start.2) | collective-permute-done | bytes 294944 | tf_op jit(solution)/shard_map/ppermute | solution.py:195
  57.0 0.7 shard_map.53
  57.7 0.4 collective-permute-start.5
  58.0 1.7 %collective-permute-start.4 = (f32[6,2,6,8,128]{4,3,2,1,0:T(8,128)S(1)}, f32[6,2,6,8,128]{4,3,2,1,0:T(8,128)S(1)}, u32[]{:S(2)}, u32[]{:S(2)}) collective-permute-start(f32[6,2,6,8,128]{4,3,2,1,0:T(8,128)S(1)} %get-tuple-element.31.refs_1_), channel_id=1, source_target_pairs={{0,32},{32,64},{64,96},{96,128},{128,160},{160,192},{192,224},{224... | collective-permute-start | bytes 884744 | tf_op jit(solution)/shard_map/ppermute | solution.py:195
  59.8 1.1 shard_map.54
  60.9 5.0 %collective-permute-done.5.refs_4_ = f32[6,2,6,8,128]{4,3,2,1,0:T(8,128)S(1)} collective-permute-done((f32[6,2,6,8,128]{4,3,2,1,0:T(8,128)S(1)}, f32[6,2,6,8,128]{4,3,2,1,0:T(8,128)S(1)}, u32[]{:S(2)}, u32[]{:S(2)}) %collective-permute-start.5) | collective-permute-done | bytes 294944 | tf_op jit(solution)/shard_map/ppermute | solution.py:196
  65.9 1.5 %collective-permute-done.4.refs_3_ = f32[6,2,6,8,128]{4,3,2,1,0:T(8,128)S(1)} collective-permute-done((f32[6,2,6,8,128]{4,3,2,1,0:T(8,128)S(1)}, f32[6,2,6,8,128]{4,3,2,1,0:T(8,128)S(1)}, u32[]{:S(2)}, u32[]{:S(2)}) %collective-permute-start.4) | collective-permute-done | bytes 294944 | tf_op jit(solution)/shard_map/ppermute | solution.py:195
  67.4 1.6 %shard_map.55 = (f32[6,2,6,8,128]{4,3,2,1,0:T(8,128)S(1)}, f32[6,2,6,8,128]{4,3,2,1,0:T(8,128)S(1)}, f32[1152,128]{1,0:T(8,128)}) custom-call(f32[2]{0:T(128)S(1)} %add_convert_fusion.refs_0_, f32[6,2,6,8,128]{4,3,2,1,0:T(8,128)S(1)} %get-tuple-element.32.refs_1_, f32[6,2,6,8,128]{4,3,2,1,0:T(8,128)S(1)} %get-tuple-element.33.refs_2_, ...), custom_call_target="tpu_custom_call" | custom-call | flops 1000000 | bytes 2000000 | tf_op jit(solution)/shard_map/pallas_call | solution.py:32
  69.0 3.6 %all-to-all-start.1 = ((f32[16,72,128]{2,1,0:T(8,128)}), f32[16,72,128]{2,1,0:T(8,128)S(1)}, u32[]{:S(2)}, u32[]{:S(2)}) async-start(f32[16,72,128]{2,1,0:T(8,128)} %bitcast.5), calls=%async_computation.1 | async-start | bytes 1179648 | tf_op jit(solution)/shard_map/all_to_all | solution.py:238
  72.6 0.4 collective-permute-start.8
  72.9 1.7 %collective-permute-start.7 = (f32[6,2,6,8,128]{4,3,2,1,0:T(8,128)S(1)}, f32[6,2,6,8,128]{4,3,2,1,0:T(8,128)S(1)}, u32[]{:S(2)}, u32[]{:S(2)}) collective-permute-start(f32[6,2,6,8,128]{4,3,2,1,0:T(8,128)S(1)} %get-tuple-element.36.refs_1_), channel_id=1, source_target_pairs={{0,32},{32,64},{64,96},{96,128},{128,160},{160,192},{192,224},{224... | collective-permute-start | bytes 884744 | tf_op jit(solution)/shard_map/ppermute | solution.py:195
  74.7 9.5 %all-to-all-done.1 = f32[16,72,128]{2,1,0:T(8,128)S(1)} async-done(((f32[16,72,128]{2,1,0:T(8,128)}), f32[16,72,128]{2,1,0:T(8,128)S(1)}, u32[]{:S(2)}, u32[]{:S(2)}) %all-to-all-start.1) | async-done | bytes 589856 | tf_op jit(solution)/shard_map/all_to_all | solution.py:238
  84.2 0.8 collective-permute-start.6
  85.0 1.1 shard_map.56
  86.1 0.0 collective-permute-done.8.refs_4_
  86.1 0.0 collective-permute-done.7.refs_3_
  86.1 0.7 shard_map.57
  86.8 19.5 %all_to_all.26 = f32[16,72,128]{2,1,0:T(8,128)S(1)} all-to-all(f32[16,72,128]{2,1,0:T(8,128)S(1)} %bitcast.15), channel_id=1, replica_groups=mesh['z'=8,'xl'=2,'y'=4,'core'=2,'xh'=2] {'xl','y','core'}, dimensions={0} | all-to-all | bytes 1179648 | tf_op jit(solution)/shard_map/all_to_all | solution.py:238
  106.3 0.0 collective-permute-done.6.other
  106.3 2.0 %shard_map.58 = f32[16,32,128]{2,1,0:T(8,128)S(1)} custom-call(f32[1152,128]{1,0:T(8,128)S(1)} %bitcast.12, f32[1152,128]{1,0:T(8,128)S(1)} %collective-permute-done.6.other, f32[1152,128]{1,0:T(8,128)S(1)} %bitcast.16), custom_call_target="tpu_custom_call" | custom-call | flops 1000000 | bytes 2000000 | tf_op jit(solution)/shard_map/pallas_call | solution.py:32
  108.3 11.4 %all_to_all.27.parts = f32[16,32,128]{2,1,0:T(8,128)S(1)} all-to-all(f32[16,32,128]{2,1,0:T(8,128)S(1)} %shard_map.58), channel_id=1, replica_groups=mesh['z'=8,'xl'=2,'y'=4,'core'=2,'xh'=2] {'xl','y','core'}, dimensions={0} | all-to-all | bytes 524288 | tf_op jit(solution)/shard_map/all_to_all | solution.py:247
  119.8 0.7 shard_map.59
  120.4 3.4 %all-to-all-start.4 = ((f32[8,32,128]{2,1,0:T(8,128)}), f32[8,32,128]{2,1,0:T(8,128)S(1)}, u32[]{:S(2)}, u32[]{:S(2)}) async-start(f32[8,32,128]{2,1,0:T(8,128)} %shard_map.59), calls=%async_computation.4 | async-start | bytes 262144 | tf_op jit(solution)/shard_map/all_to_all | solution.py:249
  123.8 9.0 %all-to-all-done.4.parts = f32[8,32,128]{2,1,0:T(8,128)S(1)} async-done(((f32[8,32,128]{2,1,0:T(8,128)}), f32[8,32,128]{2,1,0:T(8,128)S(1)}, u32[]{:S(2)}, u32[]{:S(2)}) %all-to-all-start.4) | async-done | bytes 131104 | tf_op jit(solution)/shard_map/all_to_all | solution.py:249
  132.8 0.8 shard_map.60
  133.6 0.8 copy.9
  (2 shorter events, 0.0 us)
Async XLA Ops:
  17.4 6.1 %copy-start = (f32[1,6,6,128]{3,0,2,1:T(1,128)S(1)}, f32[1,6,6,128]{3,0,2,1:T(1,128)}, u32[]{:S(2)}) copy-start(f32[1,6,6,128]{3,0,2,1:T(1,128)} %param.3) | copy-start | bytes 55300
  17.6 25.2 %collective-permute-start.1 = (f32[6,2,6,8,128]{4,3,2,1,0:T(8,128)S(1)}, f32[6,2,6,8,128]{4,3,2,1,0:T(8,128)S(1)}, u32[]{:S(2)}, u32[]{:S(2)}) collective-permute-start(f32[6,2,6,8,128]{4,3,2,1,0:T(8,128)S(1)} %get-tuple-element.22.refs_0_.refs_3_), channel_id=1, source_target_pairs={{0,224},{32,0},{64,32},{96,64},{128,96},{160,128},{192,160},{224,1... | collective-permute-start | bytes 884744 | tf_op jit(solution)/shard_map/ppermute | solution.py:196
  23.5 19.3 %collective-permute-start = (f32[6,2,6,8,128]{4,3,2,1,0:T(8,128)S(1)}, f32[6,2,6,8,128]{4,3,2,1,0:T(8,128)S(1)}, u32[]{:S(2)}, u32[]{:S(2)}) collective-permute-start(f32[6,2,6,8,128]{4,3,2,1,0:T(8,128)S(1)} %get-tuple-element.23.refs_1_.refs_4_), channel_id=1, source_target_pairs={{0,32},{32,64},{64,96},{96,128},{128,160},{160,192},{192,224},{224... | collective-permute-start | bytes 884744 | tf_op jit(solution)/shard_map/ppermute | solution.py:195
  43.5 10.1 %collective-permute-start.3 = (f32[6,2,6,8,128]{4,3,2,1,0:T(8,128)S(1)}, f32[6,2,6,8,128]{4,3,2,1,0:T(8,128)S(1)}, u32[]{:S(2)}, u32[]{:S(2)}) collective-permute-start(f32[6,2,6,8,128]{4,3,2,1,0:T(8,128)S(1)} %get-tuple-element.26.refs_0_.refs_3_), channel_id=1, source_target_pairs={{0,224},{32,0},{64,32},{96,64},{128,96},{160,128},{192,160},{224,1... | collective-permute-start | bytes 884744 | tf_op jit(solution)/shard_map/ppermute | solution.py:196
  46.8 10.2 %collective-permute-start.2 = (f32[6,2,6,8,128]{4,3,2,1,0:T(8,128)S(1)}, f32[6,2,6,8,128]{4,3,2,1,0:T(8,128)S(1)}, u32[]{:S(2)}, u32[]{:S(2)}) collective-permute-start(f32[6,2,6,8,128]{4,3,2,1,0:T(8,128)S(1)} %get-tuple-element.27.refs_1_.refs_4_), channel_id=1, source_target_pairs={{0,32},{32,64},{64,96},{96,128},{128,160},{160,192},{192,224},{224... | collective-permute-start | bytes 884744 | tf_op jit(solution)/shard_map/ppermute | solution.py:195
  57.7 8.2 %collective-permute-start.5 = (f32[6,2,6,8,128]{4,3,2,1,0:T(8,128)S(1)}, f32[6,2,6,8,128]{4,3,2,1,0:T(8,128)S(1)}, u32[]{:S(2)}, u32[]{:S(2)}) collective-permute-start(f32[6,2,6,8,128]{4,3,2,1,0:T(8,128)S(1)} %get-tuple-element.30.refs_0_), channel_id=1, source_target_pairs={{0,224},{32,0},{64,32},{96,64},{128,96},{160,128},{192,160},{224,1... | collective-permute-start | bytes 884744 | tf_op jit(solution)/shard_map/ppermute | solution.py:196
  58.0 9.4 %collective-permute-start.4 = (f32[6,2,6,8,128]{4,3,2,1,0:T(8,128)S(1)}, f32[6,2,6,8,128]{4,3,2,1,0:T(8,128)S(1)}, u32[]{:S(2)}, u32[]{:S(2)}) collective-permute-start(f32[6,2,6,8,128]{4,3,2,1,0:T(8,128)S(1)} %get-tuple-element.31.refs_1_), channel_id=1, source_target_pairs={{0,32},{32,64},{64,96},{96,128},{128,160},{160,192},{192,224},{224... | collective-permute-start | bytes 884744 | tf_op jit(solution)/shard_map/ppermute | solution.py:195
  69.0 15.2 %all-to-all-start.1 = ((f32[16,72,128]{2,1,0:T(8,128)}), f32[16,72,128]{2,1,0:T(8,128)S(1)}, u32[]{:S(2)}, u32[]{:S(2)}) async-start(f32[16,72,128]{2,1,0:T(8,128)} %bitcast.5), calls=%async_computation.1 | async-start | bytes 1179648 | tf_op jit(solution)/shard_map/all_to_all | solution.py:238
  72.6 13.5 %collective-permute-start.8 = (f32[6,2,6,8,128]{4,3,2,1,0:T(8,128)S(1)}, f32[6,2,6,8,128]{4,3,2,1,0:T(8,128)S(1)}, u32[]{:S(2)}, u32[]{:S(2)}) collective-permute-start(f32[6,2,6,8,128]{4,3,2,1,0:T(8,128)S(1)} %get-tuple-element.35.refs_0_), channel_id=1, source_target_pairs={{0,224},{32,0},{64,32},{96,64},{128,96},{160,128},{192,160},{224,1... | collective-permute-start | bytes 884744 | tf_op jit(solution)/shard_map/ppermute | solution.py:196
  72.9 13.1 %collective-permute-start.7 = (f32[6,2,6,8,128]{4,3,2,1,0:T(8,128)S(1)}, f32[6,2,6,8,128]{4,3,2,1,0:T(8,128)S(1)}, u32[]{:S(2)}, u32[]{:S(2)}) collective-permute-start(f32[6,2,6,8,128]{4,3,2,1,0:T(8,128)S(1)} %get-tuple-element.36.refs_1_), channel_id=1, source_target_pairs={{0,32},{32,64},{64,96},{96,128},{128,160},{160,192},{192,224},{224... | collective-permute-start | bytes 884744 | tf_op jit(solution)/shard_map/ppermute | solution.py:195
  84.2 22.1 %collective-permute-start.6 = (f32[1152,128]{1,0:T(8,128)S(1)}, f32[1152,128]{1,0:T(8,128)S(1)}, u32[]{:S(2)}, u32[]{:S(2)}) collective-permute-start(f32[1152,128]{1,0:T(8,128)S(1)} %bitcast.11), channel_id=1, source_target_pairs={{0,1},{1,0},{2,3},{3,2},{4,5},{5,4},{6,7},{7,6},{8,9},{9,8},{10,11... | collective-permute-start | bytes 1769480 | tf_op jit(solution)/shard_map/ppermute | solution.py:243
  120.4 12.4 %all-to-all-start.4 = ((f32[8,32,128]{2,1,0:T(8,128)}), f32[8,32,128]{2,1,0:T(8,128)S(1)}, u32[]{:S(2)}, u32[]{:S(2)}) async-start(f32[8,32,128]{2,1,0:T(8,128)} %shard_map.59), calls=%async_computation.4 | async-start | bytes 262144 | tf_op jit(solution)/shard_map/all_to_all | solution.py:249

commit v2 on v1

v2 whole, which is shorter than its diff:
```python
import jax
import jax.numpy as jnp
from jax import lax
from jax.experimental import pallas as pl
from jax.experimental.pallas import tpu as pltpu
from jax.sharding import Mesh, PartitionSpec as P

weights = (
    -5369.0 / 1800.0,
    12.0 / 7.0,
    -15.0 / 56.0,
    10.0 / 189.0,
    -1.0 / 112.0,
    2.0 / 825.0,
    -1.0 / 4752.0,
)
lower_edge = 0.0
cut_edge = 3.0
upper_edge = 13.0
CELLS = 96 * 48 * 128

VM = pl.BlockSpec(memory_space=pltpu.VMEM)
SM = pl.BlockSpec(memory_space=pltpu.SMEM)
PARAMS = pltpu.CompilerParams(vmem_limit_bytes=32 * 1024 * 1024)
F32 = jnp.float32

HALF = jax.ShapeDtypeStruct((6, 12, 8, 128), F32)
RAW = jax.ShapeDtypeStruct((1152, 128), F32)
WIDE = jax.ShapeDtypeStruct((15, 12, 8, 128), F32)


def call(body, outs, inputs, specs=None, out_specs=None, scratch=(), flops=1_000_000):
    return pl.pallas_call(
        body,
        out_shape=outs,
        in_specs=specs or [VM] * len(inputs),
        out_specs=out_specs or jax.tree.map(lambda _: VM, outs),
        scratch_shapes=scratch,
        compiler_params=PARAMS,
        cost_estimate=pl.CostEstimate(flops=flops, bytes_accessed=2_000_000, transcendentals=0),
    )(*inputs)


def unpack_body(raw, to_up, to_down):
    for half in range(2):
        for xi in range(6):
            for yi in range(6):
                for o in range(2):
                    rows = raw[pl.ds(half * 896 + o * 36 + xi * 6 + yi, 8, stride=112), :]
                    to_up[half * 6 + xi, o * 6 + yi] = rows
                    to_down[half * 6 + xi, o * 6 + yi] = rows
                rows = raw[pl.ds(half * 896 + 72 + xi * 6 + yi, 8, stride=112), :]
                (to_down, to_up)[half][12 + xi // 2, (xi % 2) * 6 + yi] = rows


class Step:
    def __init__(self, alpha, shift):
        self.alpha = alpha
        self.scaled = [-0.5 * alpha * w for w in weights]
        row = lax.broadcasted_iota(jnp.int32, (128, 128), 0)
        column = lax.broadcasted_iota(jnp.int32, (128, 128), 1)
        distance = jnp.abs(row - column)
        band = jnp.zeros((128, 128), F32)
        for k in range(1, 7):
            band = jnp.where(distance == k, F32(self.scaled[k]), band)
        self.band = jnp.where(distance == 0, F32(3.0 * self.scaled[0] - alpha * shift), band)
        self.sub = lax.broadcasted_iota(jnp.int32, (8, 128), 0)

    def plane(self, x, layer, local, emit):
        ref, index = layer(x)
        here = ref[index]
        along = jnp.dot(
            here.reshape(96, 128), self.band, precision=lax.Precision.HIGHEST, preferred_element_type=F32
        ).reshape(12, 8, 128)
        near = [(k, [p for p in (layer(x + k), layer(x - k)) if p is not None]) for k in range(1, 7)]
        for o in range(2):
            own = [ref[index, o * 6 + yi] for yi in range(6)]
            behind = [jnp.where(self.sub == 0, 0.0, pltpu.roll(v, 1, 0)) for v in own]
            ahead = [jnp.where(self.sub == 7, 0.0, pltpu.roll(v, 7, 0)) for v in own]
            line = behind + own + ahead
            for yi in range(6):
                n = o * 6 + yi
                total = along[n] + local(yi) * F32(self.alpha) * own[yi]
                for k, planes in near:
                    pair = line[6 + yi + k] + line[6 + yi - k]
                    for other, place in planes:
                        pair = pair + other[place, n]
                    total = total + F32(self.scaled[k]) * pair
                emit(n, total)


def field_of(to_up, to_down):
    def rows(x, yi):
        source = to_down if x < 6 else to_up
        return source[12 + (x % 6) // 2, (x % 2) * 6 + yi]

    return rows


def first_body(alpha, shift, to_up, to_down, acc):
    step = Step(alpha, shift)
    field = field_of(to_up, to_down)
    for x in range(12):

        def emit(n, value, x=x):
            acc[x, n] = value

        step.plane(
            x,
            lambda i: (to_up, i) if 0 <= i < 12 else None,
            lambda yi, x=x: field(x, yi),
            emit,
        )


def two_steps_body(first, second, inside, to_up, to_down, before, after, acc, y1_low, y1_high, y2_low, y2_high, wide):
    step = Step(first[0], first[1])
    field = field_of(to_up, to_down)
    mask = (inside[0], inside[1])
    terms_before = [mask[0] * F32(s) for s in step.scaled]
    terms_after = [mask[1] * F32(s) for s in step.scaled]
    for n in range(12):
        lows = [before[6 + j, n] for j in range(6)]
        highs = [after[j, n] for j in range(6)]
        for x in range(6):
            total = acc[x, n]
            for k in range(x + 1, 7):
                total = total + terms_before[k] * lows[6 + x - k]
            wide[6 + x, n] = total
            y1_low[x, n] = total
            total = acc[11 - x, n]
            for k in range(x + 1, 7):
                total = total + terms_after[k] * highs[k - x - 1]
            wide[17 - x, n] = total
            y1_high[5 - x, n] = total

    def layer(i):
        if i < 0:
            return before, 12 + i
        return (to_up, i) if i < 12 else (after, i - 12)

    for j in range(6):
        for x, source, side in ((j - 6, before, 0), (12 + j, after, 1)):

            def emit(n, value, x=x, side=side):
                wide[6 + x, n] = value * mask[side]

            step.plane(
                x,
                layer,
                lambda yi, j=j, source=source: source[12 + j // 2, (j % 2) * 6 + yi],
                emit,
            )
    step = Step(second[0], second[1])
    beta = second[2]
    for x in range(12):

        def emit(n, value, x=x):
            (y2_low, y2_high)[x // 6][x % 6, n] = value - F32(beta) * to_up[x, n]

        step.plane(x, lambda i: (wide, 6 + i), lambda yi, x=x: field(x, yi), emit)


def interior_body(alpha, shift, beta, low, high, to_up, to_down, *refs):
    if len(refs) == 2:
        acc_low, acc_high = refs
    else:
        previous_low, previous_high, acc_low, acc_high = refs
    step = Step(alpha, shift)
    field = field_of(to_up, to_down)
    for x in range(12):

        def emit(n, value, x=x):
            if len(refs) == 4:
                value = value - F32(beta) * (previous_low, previous_high)[x // 6][x % 6, n]
            (acc_low, acc_high)[x // 6][x % 6, n] = value

        step.plane(
            x,
            lambda i: ((low, high)[i // 6], i % 6) if 0 <= i < 12 else None,
            lambda yi, x=x: field(x, yi),
            emit,
        )


def halo_terms(alpha, inside, acc_low, acc_high, before, after, emit):
    scaled = [-0.5 * alpha * w for w in weights]
    terms_before = [inside[0] * F32(s) for s in scaled]
    terms_after = [inside[1] * F32(s) for s in scaled]
    for n in range(12):
        lows = [before[j, n] for j in range(6)]
        highs = [after[j, n] for j in range(6)]
        for x in range(6):
            total = acc_low[x, n]
            for k in range(x + 1, 7):
                total = total + terms_before[k] * lows[6 + x - k]
            emit(0, x, n, total)
            total = acc_high[5 - x, n]
            for k in range(x + 1, 7):
                total = total + terms_after[k] * highs[k - x - 1]
            emit(1, 5 - x, n, total)


def brick_rows(half, x, n):
    return pl.ds(half * 576 + (n // 6) * 36 + x * 6 + n % 6, 8, stride=72)


def edge_both_body(alpha, inside, acc_low, acc_high, before, after, out_low, out_high, raw):
    outs = (out_low, out_high)

    def emit(half, x, n, value):
        outs[half][x, n] = value
        raw[brick_rows(half, x, n), :] = value

    halo_terms(alpha, inside, acc_low, acc_high, before, after, emit)


def edge_raw_body(alpha, inside, acc_low, acc_high, before, after, raw):
    def emit(half, x, n, value):
        raw[brick_rows(half, x, n), :] = value

    halo_terms(alpha, inside, acc_low, acc_high, before, after, emit)


def gram_body(mine, other, applied, copies, out, sem):
    write = pltpu.make_async_copy(mine, out, sem)
    write.start()
    total = jnp.zeros((64, 64), F32)
    for r in range(36):
        rows = pl.ds(r, 32, stride=36)
        own = mine[rows, :]
        left = jnp.concatenate([own, applied[rows, :]], axis=0)
        right = jnp.concatenate([own, other[rows, :]], axis=0)
        total = total + lax.dot_general(
            left,
            right,
            (((1,), (1,)), ((), ())),
            precision=lax.Precision.HIGHEST,
            preferred_element_type=F32,
        )
    packed = jnp.concatenate([total[:32], total[32:]], axis=1)
    for n in range(16):
        copies[n] = packed
    write.wait()


def sum_body(parts, copies):
    total = parts[0]
    for n in range(1, 16):
        total = total + parts[n]
    for n in range(8):
        copies[n] = total


def finish_body(side, parts, energy, margin):
    total = parts[0]
    for n in range(1, 8):
        total = total + parts[n]
    total = total * F32(1.0 / CELLS)
    swapped = jnp.concatenate(
        [total[:, 32:64], total[:, 0:32], total[:, 96:128], total[:, 64:96]], axis=1
    )
    total = jnp.where(side[0] == 0, total, swapped)
    margin[...] = total[:, :64]
    energy[...] = total[:, 64:]


SLAB = ("xl", "y", "core")
UP = [(i, (i + 1) % 8) for i in range(8)]
DOWN = [(i, (i + 7) % 8) for i in range(8)]


def to_slabs(values):
    return lax.all_to_all(values, SLAB, split_axis=0, concat_axis=0, tiled=True)


def local(orbitals, potential):
    position = lax.axis_index("z")
    inside = jnp.stack([position > 0, position < 7]).astype(F32)
    side = lax.axis_index("xh").astype(jnp.int32).reshape(1)

    half_width = (upper_edge - cut_edge) / 2.0
    centre = (upper_edge + cut_edge) / 2.0
    sigma_first = half_width / (lower_edge - centre)
    tau_value = 2.0 / sigma_first
    sigma_second = 1.0 / (tau_value - sigma_first)
    sigma_third = 1.0 / (tau_value - sigma_second)
    first = (sigma_first / half_width, centre, 0.0)
    second = (2.0 * sigma_second / half_width, centre, sigma_first * sigma_second)
    third = (2.0 * sigma_third / half_width, centre, sigma_second * sigma_third)

    field = jnp.pad(potential.reshape(1, 36, 128), ((0, 0), (0, 4), (0, 0)))
    field = jnp.broadcast_to(field, (16, 40, 128))
    joined = jnp.concatenate([orbitals.reshape(16, 72, 128), field], axis=1)
    raw = to_slabs(joined).reshape(1792, 128)
    packed = call(unpack_body, [WIDE, WIDE], [raw])

    before = lax.ppermute(packed[0], "z", UP)
    after = lax.ppermute(packed[1], "z", DOWN)

    def first_part(*refs):
        first_body(first[0], first[1], *refs)

    acc = call(first_part, jax.ShapeDtypeStruct((12, 12, 8, 128), F32), packed, flops=400_000_000)

    def two_steps(*refs):
        two_steps_body(first, second, *refs)

    y1_low, y1_high, y2_low, y2_high = call(
        two_steps,
        [HALF] * 4,
        [inside, *packed, before, after, acc],
        [SM] + [VM] * 5,
        scratch=[pltpu.VMEM((24, 12, 8, 128), F32)],
    )

    def one_step(numbers, values, previous, body, outs):
        alpha, shift, beta = numbers
        before = lax.ppermute(values[1], "z", UP)
        after = lax.ppermute(values[0], "z", DOWN)

        def interior(*refs):
            interior_body(alpha, shift, beta, *refs)

        accs = call(interior, [HALF, HALF], [*values, *packed, *previous], flops=400_000_000)

        def edge(*refs):
            body(alpha, *refs)

        return call(edge, outs, [inside, *accs, before, after], [SM] + [VM] * 4)

    low, high, filtered_raw = one_step(
        third, (y2_low, y2_high), (y1_low, y1_high), edge_both_body, [HALF, HALF, RAW]
    )
    filtered = to_slabs(filtered_raw.reshape(16, 72, 128)).reshape(1152, 128)
    other = lax.ppermute(filtered, "xh", [(0, 1), (1, 0)])
    applied_raw = one_step((1.0, 0.0, 0.0), (low, high), (), edge_raw_body, RAW)
    applied = to_slabs(applied_raw.reshape(16, 72, 128)).reshape(1152, 128)
    copies, result = call(
        gram_body,
        [jax.ShapeDtypeStruct((16, 32, 128), F32), RAW],
        [filtered, other, applied],
        out_specs=[VM, pl.BlockSpec(memory_space=pl.ANY)],
        scratch=[pltpu.SemaphoreType.DMA],
    )
    parts = to_slabs(copies)
    copies = call(sum_body, jax.ShapeDtypeStruct((8, 32, 128), F32), [parts])
    parts = lax.all_to_all(copies, "z", split_axis=0, concat_axis=0, tiled=True)
    energy, margin = call(
        finish_body,
        [jax.ShapeDtypeStruct((32, 64), F32)] * 2,
        [side, parts],
        [SM, VM],
    )
    return result.reshape(32, 1, 6, 6, 128), energy, margin


def solution(mesh):
    fine = Mesh(mesh.devices.reshape(8, 2, 4, 2, 2), ("z", "xl", "y", "core", "xh"))
    brick = ("z", "xl", "y", "core")
    return jax.shard_map(
        local,
        mesh=fine,
        in_specs=(P("xh", brick, None, None, None), P(brick, None, None, None)),
        out_specs=(P("xh", brick, None, None, None), P("xh", None), P("xh", None)),
        check_vma=False,
    )
```

time: 136 us -> 130 us (0.956)
  blocking collectives: 65.8 us -> 50.7 us
  waiting for transfers between devices: 34 us -> 40.5 us
    all_gather x1 -> x0, blocking collectives: 18.1 us -> none  [local(): field = lax.all_gather(potential.reshape(36, 128), SLAB, axis=0, tiled=True)]
    ppermute x8 -> x6, waiting for transfers between devices: 15.5 us -> 21.9 us  [the longest x1 14.7 us: local(): before = lax.ppermute(packed[0], 'z', UP)]
    all_to_all x3, blocking collectives: 47.7 us -> 50.7 us  [to_slabs(): return lax.all_to_all(values, SLAB, split_axis=0, concat_axis=0, tiled=True)]
    ppermute x8 -> x6, starting transfers between devices: 13.4 us -> 11.2 us  [the longest x1 4.03 us: local(): after = lax.ppermute(packed[1], 'z', DOWN)]
    all_to_all x1, starting transfers between devices: 3.37 us -> 5.16 us  [local(): parts = lax.all_to_all(copies, 'z', split_axis=0, concat_axis=0, tiled=True)]
    pallas_call x12 -> x10, Pallas kernels: 11.8 us -> 12.3 us  [call(): pl.pallas_call(body, out_shape=outs, in_specs=specs or [VM] * len(inputs)...]
  transfers between devices with their start and end apart: 11 -> 9, of which waited for: 6 -> 5; matrix products, arithmetic and copies ran while one was open for 0% -> 0% of each run, Pallas kernels for 4% -> 3%
where the time goes in v2:
time: 130 us; the launch traced here: 128 us
  blocking collectives  50.7 us (39%)
  waiting for transfers between devices  40.5 us (31%)
  starting transfers between devices  21.6 us (17%)
  Pallas kernels  12.3 us (9%)
    all_to_all x3, blocking collectives, to_slabs(): return lax.all_to_all(values, SLAB, split_axis=0, concat_axis=0, tiled=True)  50.7 us
    ppermute x1, waiting for transfers between devices, local(): before = lax.ppermute(packed[0], 'z', UP)  14.7 us
    pallas_call x10, Pallas kernels, call(): pl.pallas_call(body, out_shape=outs, in_specs=specs or [VM] * len(inputs)...  12.3 us
    all_to_all x1, waiting for transfers between devices, to_slabs(): return lax.all_to_all(values, SLAB, split_axis=0, concat_axis=0, tiled=True)  9.5 us
    all_to_all x1, waiting for transfers between devices, local(): parts = lax.all_to_all(copies, 'z', split_axis=0, concat_axis=0, tiled=True)  9.08 us
    all_to_all x1, starting transfers between devices, local(): parts = lax.all_to_all(copies, 'z', split_axis=0, concat_axis=0, tiled=True)  5.16 us
    all_to_all x1, starting transfers between devices, to_slabs(): return lax.all_to_all(values, SLAB, split_axis=0, concat_axis=0, tiled=True)  4.41 us
    ppermute x1, starting transfers between devices, local(): after = lax.ppermute(packed[1], 'z', DOWN)  4.03 us
  transfers between devices with their start and end apart: 9, of which 5 were waited for; matrix products, arithmetic and copies ran while one was open for 0% of the time, Pallas kernels for 3%

profile of v2, /device:TPU:4, one launch (start us, length us, event | category | flops | bytes accessed | tf_op | source)
XLA Modules:
  0.0 127.7 jit_solution(16374441230433210548)
XLA Ops:
  0.6 0.7 pad.4
  1.4 1.1 pad_maximum_fusion
  2.5 20.1 %all_to_all.25 = f32[16,112,128]{2,1,0:T(8,128)S(1)} all-to-all(f32[16,112,128]{2,1,0:T(8,128)S(1)} %pad_maximum_fusion), channel_id=1, replica_groups=mesh['z'=8,'xl'=2,'y'=4,'core'=2,'xh'=2] {'xl','y','core'}, dimensions={0} | all-to-all | bytes 1835008 | tf_op jit(solution)/shard_map/all_to_all | solution.py:274
  22.6 0.3 shard_map.49
  22.9 2.0 %collective-permute-start = (f32[15,12,8,128]{3,2,1,0:T(8,128)S(1)}, f32[15,12,8,128]{3,2,1,0:T(8,128)S(1)}, u32[]{:S(2)}, u32[]{:S(2)}) collective-permute-start(f32[15,12,8,128]{3,2,1,0:T(8,128)S(1)} %get-tuple-element.20.refs_0_.refs_1_.refs_2_), channel_id=1, source_target_pairs={{0,32},{32,64},{64,96},{96,128},{128,160},{160,192},{192,224},{224... | collective-permute-start | bytes 2211848 | tf_op jit(solution)/shard_map/ppermute | solution.py:298
  24.9 4.0 %collective-permute-start.1 = (f32[15,12,8,128]{3,2,1,0:T(8,128)S(1)}, f32[15,12,8,128]{3,2,1,0:T(8,128)S(1)}, u32[]{:S(2)}, u32[]{:S(2)}) collective-permute-start(f32[15,12,8,128]{3,2,1,0:T(8,128)S(1)} %get-tuple-element.21.refs_1_.refs_2_.refs_3_), channel_id=1, source_target_pairs={{0,224},{32,0},{64,32},{96,64},{128,96},{160,128},{192,160},{224,1... | collective-permute-start | bytes 2211848 | tf_op jit(solution)/shard_map/ppermute | solution.py:299
  28.9 0.1 add_convert_fusion.refs_0_
  29.0 1.1 shard_map.50.refs_5_
  30.1 14.7 %collective-permute-done.refs_3_ = f32[15,12,8,128]{3,2,1,0:T(8,128)S(1)} collective-permute-done((f32[15,12,8,128]{3,2,1,0:T(8,128)S(1)}, f32[15,12,8,128]{3,2,1,0:T(8,128)S(1)}, u32[]{:S(2)}, u32[]{:S(2)}) %collective-permute-start) | collective-permute-done | bytes 737312 | tf_op jit(solution)/shard_map/ppermute | solution.py:298
  44.8 0.0 collective-permute-done.1.refs_4_
  44.8 2.9 %shard_map.51 = (f32[6,12,8,128]{3,2,1,0:T(8,128)S(1)}, f32[6,12,8,128]{3,2,1,0:T(8,128)S(1)}, f32[6,12,8,128]{3,2,1,0:T(8,128)S(1)}, f32[6,12,8,128]{3,2,1,0:T(8,128)S(1)}) custom-call(f32[2]{0:T(128)S(1)} %add_convert_fusion.refs_0_, f32[15,12,8,128]{3,2,1,0:T(8,128)S(1)} %get-tuple-element.20.refs_0_.refs_1_.refs_2_, ...), custom_call_target="tpu_custom_call" | custom-call | flops 1000000 | bytes 2000000 | tf_op jit(solution)/shard_map/pallas_call | solution.py:33
  47.8 3.1 %collective-permute-start.3 = (f32[6,12,8,128]{3,2,1,0:T(8,128)S(1)}, f32[6,12,8,128]{3,2,1,0:T(8,128)S(1)}, u32[]{:S(2)}, u32[]{:S(2)}) collective-permute-start(f32[6,12,8,128]{3,2,1,0:T(8,128)S(1)} %get-tuple-element.22.refs_0_), channel_id=1, source_target_pairs={{0,224},{32,0},{64,32},{96,64},{128,96},{160,128},{192,160},{224,1... | collective-permute-start | bytes 884744 | tf_op jit(solution)/shard_map/ppermute | solution.py:320
  50.9 0.0 collective-permute-start.2
  50.9 1.1 shard_map.52
  52.0 3.7 %collective-permute-done.3.refs_4_ = f32[6,12,8,128]{3,2,1,0:T(8,128)S(1)} collective-permute-done((f32[6,12,8,128]{3,2,1,0:T(8,128)S(1)}, f32[6,12,8,128]{3,2,1,0:T(8,128)S(1)}, u32[]{:S(2)}, u32[]{:S(2)}) %collective-permute-start.3) | collective-permute-done | bytes 294944 | tf_op jit(solution)/shard_map/ppermute | solution.py:320
  55.7 3.4 %collective-permute-done.2.refs_3_ = f32[6,12,8,128]{3,2,1,0:T(8,128)S(1)} collective-permute-done((f32[6,12,8,128]{3,2,1,0:T(8,128)S(1)}, f32[6,12,8,128]{3,2,1,0:T(8,128)S(1)}, u32[]{:S(2)}, u32[]{:S(2)}) %collective-permute-start.2) | collective-permute-done | bytes 294944 | tf_op jit(solution)/shard_map/ppermute | solution.py:319
  59.1 1.6 %shard_map.53 = (f32[6,12,8,128]{3,2,1,0:T(8,128)S(1)}, f32[6,12,8,128]{3,2,1,0:T(8,128)S(1)}, f32[1152,128]{1,0:T(8,128)}) custom-call(f32[2]{0:T(128)S(1)} %add_convert_fusion.refs_0_, f32[6,12,8,128]{3,2,1,0:T(8,128)S(1)} %get-tuple-element.26.refs_1_, f32[6,12,8,128]{3,2,1,0:T(8,128)S(1)} %get-tuple-element.27.refs_2_, ...), custom_call_target="tpu_custom_call" | custom-call | flops 1000000 | bytes 2000000 | tf_op jit(solution)/shard_map/pallas_call | solution.py:33
  60.7 4.4 %all-to-all-start.1 = ((f32[16,72,128]{2,1,0:T(8,128)}), f32[16,72,128]{2,1,0:T(8,128)S(1)}, u32[]{:S(2)}, u32[]{:S(2)}) async-start(f32[16,72,128]{2,1,0:T(8,128)} %bitcast.6), calls=%async_computation.1 | async-start | bytes 1179648 | tf_op jit(solution)/shard_map/all_to_all | solution.py:274
  65.1 0.4 collective-permute-start.6
  65.5 1.7 %collective-permute-start.5 = (f32[6,12,8,128]{3,2,1,0:T(8,128)S(1)}, f32[6,12,8,128]{3,2,1,0:T(8,128)S(1)}, u32[]{:S(2)}, u32[]{:S(2)}) collective-permute-start(f32[6,12,8,128]{3,2,1,0:T(8,128)S(1)} %get-tuple-element.30.refs_1_), channel_id=1, source_target_pairs={{0,32},{32,64},{64,96},{96,128},{128,160},{160,192},{192,224},{224... | collective-permute-start | bytes 884744 | tf_op jit(solution)/shard_map/ppermute | solution.py:319
  67.2 9.5 %all-to-all-done.1 = f32[16,72,128]{2,1,0:T(8,128)S(1)} async-done(((f32[16,72,128]{2,1,0:T(8,128)}), f32[16,72,128]{2,1,0:T(8,128)S(1)}, u32[]{:S(2)}, u32[]{:S(2)}) %all-to-all-start.1) | async-done | bytes 589856 | tf_op jit(solution)/shard_map/all_to_all | solution.py:274
  76.7 0.8 collective-permute-start.4
  77.5 1.1 shard_map.54
  78.6 0.0 collective-permute-done.6.refs_4_
  78.6 0.0 collective-permute-done.5.refs_3_
  78.6 0.7 shard_map.55
  79.4 19.5 %all_to_all.26 = f32[16,72,128]{2,1,0:T(8,128)S(1)} all-to-all(f32[16,72,128]{2,1,0:T(8,128)S(1)} %bitcast.16), channel_id=1, replica_groups=mesh['z'=8,'xl'=2,'y'=4,'core'=2,'xh'=2] {'xl','y','core'}, dimensions={0} | all-to-all | bytes 1179648 | tf_op jit(solution)/shard_map/all_to_all | solution.py:274
  98.9 0.0 collective-permute-done.4.other
  98.9 2.1 %shard_map.56 = (f32[16,32,128]{2,1,0:T(8,128)S(1)}, f32[1152,128]{1,0:T(8,128)}) custom-call(f32[1152,128]{1,0:T(8,128)S(1)} %bitcast.14, f32[1152,128]{1,0:T(8,128)S(1)} %collective-permute-done.4.other, f32[1152,128]{1,0:T(8,128)S(1)} %bitcast.15), custom_call_target="tpu_custom_call" | custom-call | flops 1000000 | bytes 2000000 | tf_op jit(solution)/shard_map/pallas_call | solution.py:33
  101.0 11.0 %all_to_all.27.parts = f32[16,32,128]{2,1,0:T(8,128)S(1)} all-to-all(f32[16,32,128]{2,1,0:T(8,128)S(1)} %get-tuple-element.34), channel_id=1, replica_groups=mesh['z'=8,'xl'=2,'y'=4,'core'=2,'xh'=2] {'xl','y','core'}, dimensions={0} | all-to-all | bytes 524288 | tf_op jit(solution)/shard_map/all_to_all | solution.py:274
  112.0 0.7 shard_map.57
  112.7 5.2 %all-to-all-start.4 = ((f32[8,32,128]{2,1,0:T(8,128)}), f32[8,32,128]{2,1,0:T(8,128)S(1)}, u32[]{:S(2)}, u32[]{:S(2)}) async-start(f32[8,32,128]{2,1,0:T(8,128)} %shard_map.57), calls=%async_computation.4 | async-start | bytes 262144 | tf_op jit(solution)/shard_map/all_to_all | solution.py:348
  117.9 9.1 %all-to-all-done.4.parts = f32[8,32,128]{2,1,0:T(8,128)S(1)} async-done(((f32[8,32,128]{2,1,0:T(8,128)}), f32[8,32,128]{2,1,0:T(8,128)S(1)}, u32[]{:S(2)}, u32[]{:S(2)}) %all-to-all-start.4) | async-done | bytes 131104 | tf_op jit(solution)/shard_map/all_to_all | solution.py:348
  126.9 0.8 shard_map.58
  (1 shorter events, 0.0 us)
Async XLA Ops:
  22.9 21.9 %collective-permute-start = (f32[15,12,8,128]{3,2,1,0:T(8,128)S(1)}, f32[15,12,8,128]{3,2,1,0:T(8,128)S(1)}, u32[]{:S(2)}, u32[]{:S(2)}) collective-permute-start(f32[15,12,8,128]{3,2,1,0:T(8,128)S(1)} %get-tuple-element.20.refs_0_.refs_1_.refs_2_), channel_id=1, source_target_pairs={{0,32},{32,64},{64,96},{96,128},{128,160},{160,192},{192,224},{224... | collective-permute-start | bytes 2211848 | tf_op jit(solution)/shard_map/ppermute | solution.py:298
  24.9 19.9 %collective-permute-start.1 = (f32[15,12,8,128]{3,2,1,0:T(8,128)S(1)}, f32[15,12,8,128]{3,2,1,0:T(8,128)S(1)}, u32[]{:S(2)}, u32[]{:S(2)}) collective-permute-start(f32[15,12,8,128]{3,2,1,0:T(8,128)S(1)} %get-tuple-element.21.refs_1_.refs_2_.refs_3_), channel_id=1, source_target_pairs={{0,224},{32,0},{64,32},{96,64},{128,96},{160,128},{192,160},{224,1... | collective-permute-start | bytes 2211848 | tf_op jit(solution)/shard_map/ppermute | solution.py:299
  47.8 8.0 %collective-permute-start.3 = (f32[6,12,8,128]{3,2,1,0:T(8,128)S(1)}, f32[6,12,8,128]{3,2,1,0:T(8,128)S(1)}, u32[]{:S(2)}, u32[]{:S(2)}) collective-permute-start(f32[6,12,8,128]{3,2,1,0:T(8,128)S(1)} %get-tuple-element.22.refs_0_), channel_id=1, source_target_pairs={{0,224},{32,0},{64,32},{96,64},{128,96},{160,128},{192,160},{224,1... | collective-permute-start | bytes 884744 | tf_op jit(solution)/shard_map/ppermute | solution.py:320
  50.9 8.3 %collective-permute-start.2 = (f32[6,12,8,128]{3,2,1,0:T(8,128)S(1)}, f32[6,12,8,128]{3,2,1,0:T(8,128)S(1)}, u32[]{:S(2)}, u32[]{:S(2)}) collective-permute-start(f32[6,12,8,128]{3,2,1,0:T(8,128)S(1)} %get-tuple-element.23.refs_1_), channel_id=1, source_target_pairs={{0,32},{32,64},{64,96},{96,128},{128,160},{160,192},{192,224},{224... | collective-permute-start | bytes 884744 | tf_op jit(solution)/shard_map/ppermute | solution.py:319
  60.7 16.0 %all-to-all-start.1 = ((f32[16,72,128]{2,1,0:T(8,128)}), f32[16,72,128]{2,1,0:T(8,128)S(1)}, u32[]{:S(2)}, u32[]{:S(2)}) async-start(f32[16,72,128]{2,1,0:T(8,128)} %bitcast.6), calls=%async_computation.1 | async-start | bytes 1179648 | tf_op jit(solution)/shard_map/all_to_all | solution.py:274
  65.1 13.5 %collective-permute-start.6 = (f32[6,12,8,128]{3,2,1,0:T(8,128)S(1)}, f32[6,12,8,128]{3,2,1,0:T(8,128)S(1)}, u32[]{:S(2)}, u32[]{:S(2)}) collective-permute-start(f32[6,12,8,128]{3,2,1,0:T(8,128)S(1)} %get-tuple-element.29.refs_0_), channel_id=1, source_target_pairs={{0,224},{32,0},{64,32},{96,64},{128,96},{160,128},{192,160},{224,1... | collective-permute-start | bytes 884744 | tf_op jit(solution)/shard_map/ppermute | solution.py:320
  65.5 13.1 %collective-permute-start.5 = (f32[6,12,8,128]{3,2,1,0:T(8,128)S(1)}, f32[6,12,8,128]{3,2,1,0:T(8,128)S(1)}, u32[]{:S(2)}, u32[]{:S(2)}) collective-permute-start(f32[6,12,8,128]{3,2,1,0:T(8,128)S(1)} %get-tuple-element.30.refs_1_), channel_id=1, source_target_pairs={{0,32},{32,64},{64,96},{96,128},{128,160},{160,192},{192,224},{224... | collective-permute-start | bytes 884744 | tf_op jit(solution)/shard_map/ppermute | solution.py:319
  76.7 22.2 %collective-permute-start.4 = (f32[1152,128]{1,0:T(8,128)S(1)}, f32[1152,128]{1,0:T(8,128)S(1)}, u32[]{:S(2)}, u32[]{:S(2)}) collective-permute-start(f32[1152,128]{1,0:T(8,128)S(1)} %bitcast.13), channel_id=1, source_target_pairs={{0,1},{1,0},{2,3},{3,2},{4,5},{5,4},{6,7},{7,6},{8,9},{9,8},{10,11... | collective-permute-start | bytes 1769480 | tf_op jit(solution)/shard_map/ppermute | solution.py:336
  112.7 14.2 %all-to-all-start.4 = ((f32[8,32,128]{2,1,0:T(8,128)}), f32[8,32,128]{2,1,0:T(8,128)S(1)}, u32[]{:S(2)}, u32[]{:S(2)}) async-start(f32[8,32,128]{2,1,0:T(8,128)} %shard_map.57), calls=%async_computation.4 | async-start | bytes 262144 | tf_op jit(solution)/shard_map/all_to_all | solution.py:348

commit v3 on v2

--- a/solution.py
+++ b/solution.py
@@ -26,7 +26,7 @@
 
 HALF = jax.ShapeDtypeStruct((6, 12, 8, 128), F32)
 RAW = jax.ShapeDtypeStruct((1152, 128), F32)
-WIDE = jax.ShapeDtypeStruct((15, 12, 8, 128), F32)
+SLABF = jax.ShapeDtypeStruct((12, 12, 8, 128), F32)
 
 
 def call(body, outs, inputs, specs=None, out_specs=None, scratch=(), flops=1_000_000):
@@ -41,16 +41,22 @@
     )(*inputs)
 
 
-def unpack_body(raw, to_up, to_down):
+def unpack_body(raw, planes):
     for half in range(2):
         for xi in range(6):
-            for yi in range(6):
-                for o in range(2):
-                    rows = raw[pl.ds(half * 896 + o * 36 + xi * 6 + yi, 8, stride=112), :]
-                    to_up[half * 6 + xi, o * 6 + yi] = rows
-                    to_down[half * 6 + xi, o * 6 + yi] = rows
-                rows = raw[pl.ds(half * 896 + 72 + xi * 6 + yi, 8, stride=112), :]
-                (to_down, to_up)[half][12 + xi // 2, (xi % 2) * 6 + yi] = rows
+            for n in range(12):
+                planes[half * 6 + xi, n] = raw[brick_rows(half, xi, n), :]
+
+
+def brick_rows(half, x, n):
+    return pl.ds(half * 576 + (n // 6) * 36 + x * 6 + n % 6, 8, stride=72)
+
+
+def field_rows(field, x, yi):
+    if 0 <= x < 12:
+        return field[pl.ds((x // 6) * 576 + (x % 6) * 6 + yi, 8, stride=72), :]
+    half = 0 if x < 0 else 1
+    return field[pl.ds(half * 576 + 36 + (x % 6) * 6 + yi, 8, stride=72), :]
 
 
 class Step:
@@ -89,17 +95,8 @@
                 emit(n, total)
 
 
-def field_of(to_up, to_down):
-    def rows(x, yi):
-        source = to_down if x < 6 else to_up
-        return source[12 + (x % 6) // 2, (x % 2) * 6 + yi]
-
-    return rows
-
-
-def first_body(alpha, shift, to_up, to_down, acc):
+def first_body(alpha, shift, planes, field, acc):
     step = Step(alpha, shift)
-    field = field_of(to_up, to_down)
     for x in range(12):
 
         def emit(n, value, x=x):
@@ -107,15 +104,14 @@
 
         step.plane(
             x,
-            lambda i: (to_up, i) if 0 <= i < 12 else None,
-            lambda yi, x=x: field(x, yi),
+            lambda i: (planes, i) if 0 <= i < 12 else None,
+            lambda yi, x=x: field_rows(field, x, yi),
             emit,
         )
 
 
-def two_steps_body(first, second, inside, to_up, to_down, before, after, acc, y1_low, y1_high, y2_low, y2_high, wide):
+def two_steps_body(first, second, inside, planes, field, before, after, acc, y1_low, y1_high, y2_low, y2_high, wide):
     step = Step(first[0], first[1])
-    field = field_of(to_up, to_down)
     mask = (inside[0], inside[1])
     terms_before = [mask[0] * F32(s) for s in step.scaled]
     terms_after = [mask[1] * F32(s) for s in step.scaled]
@@ -137,10 +133,10 @@
     def layer(i):
         if i < 0:
             return before, 12 + i
-        return (to_up, i) if i < 12 else (after, i - 12)
+        return (planes, i) if i < 12 else (after, i - 12)
 
     for j in range(6):
-        for x, source, side in ((j - 6, before, 0), (12 + j, after, 1)):
+        for x, side in ((j - 6, 0), (12 + j, 1)):
 
             def emit(n, value, x=x, side=side):
                 wide[6 + x, n] = value * mask[side]
@@ -148,7 +144,7 @@
             step.plane(
                 x,
                 layer,
-                lambda yi, j=j, source=source: source[12 + j // 2, (j % 2) * 6 + yi],
+                lambda yi, x=x: field_rows(field, x, yi),
                 emit,
             )
     step = Step(second[0], second[1])
@@ -156,18 +152,17 @@
     for x in range(12):
 
         def emit(n, value, x=x):
-            (y2_low, y2_high)[x // 6][x % 6, n] = value - F32(beta) * to_up[x, n]
-
-        step.plane(x, lambda i: (wide, 6 + i), lambda yi, x=x: field(x, yi), emit)
-
-
-def interior_body(alpha, shift, beta, low, high, to_up, to_down, *refs):
+            (y2_low, y2_high)[x // 6][x % 6, n] = value - F32(beta) * planes[x, n]
+
+        step.plane(x, lambda i: (wide, 6 + i), lambda yi, x=x: field_rows(field, x, yi), emit)
+
+
+def interior_body(alpha, shift, beta, low, high, field, *refs):
     if len(refs) == 2:
         acc_low, acc_high = refs
     else:
         previous_low, previous_high, acc_low, acc_high = refs
     step = Step(alpha, shift)
-    field = field_of(to_up, to_down)
     for x in range(12):
 
         def emit(n, value, x=x):
@@ -178,7 +173,7 @@
         step.plane(
             x,
             lambda i: ((low, high)[i // 6], i % 6) if 0 <= i < 12 else None,
-            lambda yi, x=x: field(x, yi),
+            lambda yi, x=x: field_rows(field, x, yi),
             emit,
         )
 
@@ -199,10 +194,6 @@
             for k in range(x + 1, 7):
                 total = total + terms_after[k] * highs[k - x - 1]
             emit(1, 5 - x, n, total)
-
-
-def brick_rows(half, x, n):
-    return pl.ds(half * 576 + (n // 6) * 36 + x * 6 + n % 6, 8, stride=72)
 
 
 def edge_both_body(alpha, inside, acc_low, acc_high, before, after, out_low, out_high, raw):
@@ -289,19 +280,21 @@
     second = (2.0 * sigma_second / half_width, centre, sigma_first * sigma_second)
     third = (2.0 * sigma_third / half_width, centre, sigma_second * sigma_third)
 
-    field = jnp.pad(potential.reshape(1, 36, 128), ((0, 0), (0, 4), (0, 0)))
-    field = jnp.broadcast_to(field, (16, 40, 128))
-    joined = jnp.concatenate([orbitals.reshape(16, 72, 128), field], axis=1)
-    raw = to_slabs(joined).reshape(1792, 128)
-    packed = call(unpack_body, [WIDE, WIDE], [raw])
-
-    before = lax.ppermute(packed[0], "z", UP)
-    after = lax.ppermute(packed[1], "z", DOWN)
+    own_field = potential.reshape(36, 128)
+    across = [(2 * i + 1, (2 * i + 2) % 16) for i in range(8)] + [(2 * i, (2 * i + 15) % 16) for i in range(8)]
+    next_field = lax.ppermute(own_field, ("z", "xl"), across)
+    raw = to_slabs(orbitals.reshape(16, 72, 128)).reshape(1152, 128)
+    planes = call(unpack_body, SLABF, [raw])
+    before = lax.ppermute(planes, "z", UP)
+    after = lax.ppermute(planes, "z", DOWN)
+    field = jnp.broadcast_to(jnp.concatenate([own_field, next_field])[None], (16, 72, 128))
+    field, planes = lax.optimization_barrier((field, planes))
+    field = to_slabs(field).reshape(1152, 128)
 
     def first_part(*refs):
         first_body(first[0], first[1], *refs)
 
-    acc = call(first_part, jax.ShapeDtypeStruct((12, 12, 8, 128), F32), packed, flops=400_000_000)
+    acc = call(first_part, SLABF, [planes, field], flops=400_000_000)
 
     def two_steps(*refs):
         two_steps_body(first, second, *refs)
@@ -309,32 +302,35 @@
     y1_low, y1_high, y2_low, y2_high = call(
         two_steps,
         [HALF] * 4,
-        [inside, *packed, before, after, acc],
+        [inside, planes, field, before, after, acc],
         [SM] + [VM] * 5,
         scratch=[pltpu.VMEM((24, 12, 8, 128), F32)],
     )
 
-    def one_step(numbers, values, previous, body, outs):
-        alpha, shift, beta = numbers
-        before = lax.ppermute(values[1], "z", UP)
-        after = lax.ppermute(values[0], "z", DOWN)
-
+    def exchange(values):
+        return lax.ppermute(values[1], "z", UP), lax.ppermute(values[0], "z", DOWN)
+
+    def interior_of(numbers, values, previous):
         def interior(*refs):
-            interior_body(alpha, shift, beta, *refs)
-
-        accs = call(interior, [HALF, HALF], [*values, *packed, *previous], flops=400_000_000)
-
+            interior_body(*numbers, *refs)
+
+        return call(interior, [HALF, HALF], [*values, field, *previous], flops=400_000_000)
+
+    def finish(numbers, accs, halos, body, outs):
         def edge(*refs):
-            body(alpha, *refs)
-
-        return call(edge, outs, [inside, *accs, before, after], [SM] + [VM] * 4)
-
-    low, high, filtered_raw = one_step(
-        third, (y2_low, y2_high), (y1_low, y1_high), edge_both_body, [HALF, HALF, RAW]
-    )
+            body(numbers[0], *refs)
+
+        return call(edge, outs, [inside, *accs, *halos], [SM] + [VM] * 4)
+
+    halos = exchange((y2_low, y2_high))
+    accs = interior_of(third, (y2_low, y2_high), (y1_low, y1_high))
+    low, high, filtered_raw = finish(third, accs, halos, edge_both_body, [HALF, HALF, RAW])
     filtered = to_slabs(filtered_raw.reshape(16, 72, 128)).reshape(1152, 128)
+    halos = exchange((low, high))
+    accs = interior_of((1.0, 0.0, 0.0), (low, high), ())
+    filtered, accs = lax.optimization_barrier((filtered, accs))
     other = lax.ppermute(filtered, "xh", [(0, 1), (1, 0)])
-    applied_raw = one_step((1.0, 0.0, 0.0), (low, high), (), edge_raw_body, RAW)
+    applied_raw = finish((1.0, 0.0, 0.0), accs, halos, edge_raw_body, RAW)
     applied = to_slabs(applied_raw.reshape(16, 72, 128)).reshape(1152, 128)
     copies, result = call(
         gram_body,

time: 130 us -> 128 us (0.985)
  blocking collectives: 50.7 us -> 31.7 us
  starting transfers between devices: 21.6 us -> 35.9 us
  waiting for transfers between devices: 40.5 us -> 43.4 us
    all_to_all x3 -> x2, blocking collectives: 50.7 us -> 31.7 us  [to_slabs(): return lax.all_to_all(values, SLAB, split_axis=0, concat_axis=0, tiled=True)]
    all_to_all x1 -> x3, starting transfers between devices: 4.41 us -> 14.3 us  [to_slabs(): return lax.all_to_all(values, SLAB, split_axis=0, concat_axis=0, tiled=True)]
    all_to_all x1 -> x3, waiting for transfers between devices: 9.5 us -> 16.8 us  [to_slabs(): return lax.all_to_all(values, SLAB, split_axis=0, concat_axis=0, tiled=True)]
    ppermute x6 -> x7, starting transfers between devices: 11.2 us -> 17.4 us  [the longest x1 7.3 us: local(): next_field = lax.ppermute(own_field, ('z', 'xl'), across)]
    ppermute x6 -> x7, waiting for transfers between devices: 21.9 us -> 17.7 us  [the longest x1 6.15 us: local(): after = lax.ppermute(planes, 'z', DOWN)]
    all_to_all x1, starting transfers between devices: 5.16 us -> 3.37 us  [local(): parts = lax.all_to_all(copies, 'z', split_axis=0, concat_axis=0, tiled=True)]
  transfers between devices with their start and end apart: 9 -> 12, of which waited for: 5 -> 9; matrix products, arithmetic and copies ran while one was open for 0% -> 0% of each run, Pallas kernels for 3% -> 3%
where the time goes in v3:
time: 128 us; the launch traced here: 125 us
  waiting for transfers between devices  43.4 us (34%)
  starting transfers between devices  35.9 us (28%)
  blocking collectives  31.7 us (25%)
  Pallas kernels  12.6 us (10%)
    all_to_all x2, blocking collectives, to_slabs(): return lax.all_to_all(values, SLAB, split_axis=0, concat_axis=0, tiled=True)  31.7 us
    all_to_all x3, waiting for transfers between devices, to_slabs(): return lax.all_to_all(values, SLAB, split_axis=0, concat_axis=0, tiled=True)  16.8 us
    all_to_all x3, starting transfers between devices, to_slabs(): return lax.all_to_all(values, SLAB, split_axis=0, concat_axis=0, tiled=True)  14.3 us
    pallas_call x10, Pallas kernels, call(): pl.pallas_call(body, out_shape=outs, in_specs=specs or [VM] * len(inputs)...  12.6 us
    all_to_all x1, waiting for transfers between devices, local(): parts = lax.all_to_all(copies, 'z', split_axis=0, concat_axis=0, tiled=True)  8.99 us
    ppermute x1, starting transfers between devices, local(): next_field = lax.ppermute(own_field, ('z', 'xl'), across)  7.3 us
    ppermute x1, waiting for transfers between devices, local(): after = lax.ppermute(planes, 'z', DOWN)  6.15 us
    ppermute x1, starting transfers between devices, local(): after = lax.ppermute(planes, 'z', DOWN)  5.93 us
  transfers between devices with their start and end apart: 12, of which 9 were waited for; matrix products, arithmetic and copies ran while one was open for 0% of the time, Pallas kernels for 3%

profile of v3, /device:TPU:4, one launch (start us, length us, event | category | flops | bytes accessed | tf_op | source)
XLA Modules:
  0.0 125.4 jit_solution(15422374320521351026)
XLA Ops:
  0.6 0.0 copy-start
  0.6 5.2 %all-to-all-start = ((f32[16,72,128]{2,1,0:T(8,128)}), f32[16,72,128]{2,1,0:T(8,128)S(1)}, u32[]{:S(2)}, u32[]{:S(2)}) async-start(f32[16,72,128]{2,1,0:T(8,128)} %bitcast.20), calls=%async_computation | async-start | bytes 1179648 | tf_op jit(solution)/shard_map/all_to_all | solution.py:265
  5.9 0.0 copy-done
  5.9 7.3 %collective-permute-start = (f32[36,128]{1,0:T(8,128)S(1)}, f32[36,128]{1,0:T(8,128)S(1)}, u32[]{:S(2)}, u32[]{:S(2)}) collective-permute-start(f32[36,128]{1,0:T(8,128)S(1)} %reshape.37), channel_id=1, source_target_pairs={{16,32},{48,64},{80,96},{112,128},{144,160},{176,192},{208,224},{2... | collective-permute-start | bytes 55304 | tf_op jit(solution)/shard_map/ppermute | solution.py:285
  13.2 1.8 %collective-permute-done = f32[36,128]{1,0:T(8,128)S(1)} collective-permute-done((f32[36,128]{1,0:T(8,128)S(1)}, f32[36,128]{1,0:T(8,128)S(1)}, u32[]{:S(2)}, u32[]{:S(2)}) %collective-permute-start) | collective-permute-done | bytes 18464 | tf_op jit(solution)/shard_map/ppermute | solution.py:285
  15.0 2.9 %all-to-all-done = f32[16,72,128]{2,1,0:T(8,128)S(1)} async-done(((f32[16,72,128]{2,1,0:T(8,128)}), f32[16,72,128]{2,1,0:T(8,128)S(1)}, u32[]{:S(2)}, u32[]{:S(2)}) %all-to-all-start) | async-done | bytes 589856 | tf_op jit(solution)/shard_map/all_to_all | solution.py:265
  17.9 0.1 shard_map.49.refs_0_.refs_1_
  18.0 0.9 broadcast_in_dim.2
  18.9 3.6 %all-to-all-start.1 = ((f32[16,72,128]{2,1,0:T(8,128)}), f32[16,72,128]{2,1,0:T(8,128)S(1)}, u32[]{:S(2)}, u32[]{:S(2)}) async-start(f32[16,72,128]{2,1,0:T(8,128)} %broadcast_in_dim.2), calls=%async_computation.1 | async-start | bytes 1179648 | tf_op jit(solution)/shard_map/all_to_all | solution.py:265
  22.5 5.9 %collective-permute-start.2 = (f32[12,12,8,128]{3,2,1,0:T(8,128)S(1)}, f32[12,12,8,128]{3,2,1,0:T(8,128)S(1)}, u32[]{:S(2)}, u32[]{:S(2)}) collective-permute-start(f32[12,12,8,128]{3,2,1,0:T(8,128)S(1)} %shard_map.49.refs_0_.refs_1_), channel_id=1, source_target_pairs={{0,224},{32,0},{64,32},{96,64},{128,96},{160,128},{192,160},{224,1... | collective-permute-start | bytes 1769480 | tf_op jit(solution)/shard_map/ppermute | solution.py:289
  28.4 0.0 collective-permute-start.1
  28.4 0.1 add_convert_fusion.refs_0_
  28.5 5.6 %all-to-all-done.1 = f32[16,72,128]{2,1,0:T(8,128)S(1)} async-done(((f32[16,72,128]{2,1,0:T(8,128)}), f32[16,72,128]{2,1,0:T(8,128)S(1)}, u32[]{:S(2)}, u32[]{:S(2)}) %all-to-all-start.1) | async-done | bytes 589856 | tf_op jit(solution)/shard_map/all_to_all | solution.py:265
  34.1 1.2 shard_map.50.refs_5_
  35.2 6.1 %collective-permute-done.2.refs_4_ = f32[12,12,8,128]{3,2,1,0:T(8,128)S(1)} collective-permute-done((f32[12,12,8,128]{3,2,1,0:T(8,128)S(1)}, f32[12,12,8,128]{3,2,1,0:T(8,128)S(1)}, u32[]{:S(2)}, u32[]{:S(2)}) %collective-permute-start.2) | collective-permute-done | bytes 589856 | tf_op jit(solution)/shard_map/ppermute | solution.py:289
  41.4 3.4 %collective-permute-done.1.refs_3_ = f32[12,12,8,128]{3,2,1,0:T(8,128)S(1)} collective-permute-done((f32[12,12,8,128]{3,2,1,0:T(8,128)S(1)}, f32[12,12,8,128]{3,2,1,0:T(8,128)S(1)}, u32[]{:S(2)}, u32[]{:S(2)}) %collective-permute-start.1) | collective-permute-done | bytes 589856 | tf_op jit(solution)/shard_map/ppermute | solution.py:288
  44.8 3.2 %shard_map.51 = (f32[6,12,8,128]{3,2,1,0:T(8,128)S(1)}, f32[6,12,8,128]{3,2,1,0:T(8,128)S(1)}, f32[6,12,8,128]{3,2,1,0:T(8,128)S(1)}, f32[6,12,8,128]{3,2,1,0:T(8,128)S(1)}) custom-call(f32[2]{0:T(128)S(1)} %add_convert_fusion.refs_0_, f32[12,12,8,128]{3,2,1,0:T(8,128)S(1)} %shard_map.49.refs_0_.refs_1_, f32[1152,128]{1,0:T(8,128)S(1)} %bitcast.12, ...), custom_call_target="tpu_custom_call" | custom-call | flops 1000000 | bytes 2000000 | tf_op jit(solution)/shard_map/pallas_call | solution.py:33
  48.0 0.4 collective-permute-start.4
  48.4 1.7 %collective-permute-start.3 = (f32[6,12,8,128]{3,2,1,0:T(8,128)S(1)}, f32[6,12,8,128]{3,2,1,0:T(8,128)S(1)}, u32[]{:S(2)}, u32[]{:S(2)}) collective-permute-start(f32[6,12,8,128]{3,2,1,0:T(8,128)S(1)} %get-tuple-element.26.refs_1_), channel_id=1, source_target_pairs={{0,32},{32,64},{64,96},{96,128},{128,160},{160,192},{192,224},{224... | collective-permute-start | bytes 884744 | tf_op jit(solution)/shard_map/ppermute | solution.py:311
  50.1 1.2 shard_map.52
  51.3 4.8 %collective-permute-done.4.refs_4_ = f32[6,12,8,128]{3,2,1,0:T(8,128)S(1)} collective-permute-done((f32[6,12,8,128]{3,2,1,0:T(8,128)S(1)}, f32[6,12,8,128]{3,2,1,0:T(8,128)S(1)}, u32[]{:S(2)}, u32[]{:S(2)}) %collective-permute-start.4) | collective-permute-done | bytes 294944 | tf_op jit(solution)/shard_map/ppermute | solution.py:311
  56.1 1.5 %collective-permute-done.3.refs_3_ = f32[6,12,8,128]{3,2,1,0:T(8,128)S(1)} collective-permute-done((f32[6,12,8,128]{3,2,1,0:T(8,128)S(1)}, f32[6,12,8,128]{3,2,1,0:T(8,128)S(1)}, u32[]{:S(2)}, u32[]{:S(2)}) %collective-permute-start.3) | collective-permute-done | bytes 294944 | tf_op jit(solution)/shard_map/ppermute | solution.py:311
  57.6 1.6 %shard_map.53 = (f32[6,12,8,128]{3,2,1,0:T(8,128)S(1)}, f32[6,12,8,128]{3,2,1,0:T(8,128)S(1)}, f32[1152,128]{1,0:T(8,128)}) custom-call(f32[2]{0:T(128)S(1)} %add_convert_fusion.refs_0_, f32[6,12,8,128]{3,2,1,0:T(8,128)S(1)} %get-tuple-element.29.refs_1_, f32[6,12,8,128]{3,2,1,0:T(8,128)S(1)} %get-tuple-element.30.refs_2_, ...), custom_call_target="tpu_custom_call" | custom-call | flops 1000000 | bytes 2000000 | tf_op jit(solution)/shard_map/pallas_call | solution.py:33
  59.2 5.4 %all-to-all-start.2 = ((f32[16,72,128]{2,1,0:T(8,128)}), f32[16,72,128]{2,1,0:T(8,128)S(1)}, u32[]{:S(2)}, u32[]{:S(2)}) async-start(f32[16,72,128]{2,1,0:T(8,128)} %bitcast.5), calls=%async_computation.2 | async-start | bytes 1179648 | tf_op jit(solution)/shard_map/all_to_all | solution.py:265
  64.7 0.4 collective-permute-start.7
  65.0 1.7 %collective-permute-start.6 = (f32[6,12,8,128]{3,2,1,0:T(8,128)S(1)}, f32[6,12,8,128]{3,2,1,0:T(8,128)S(1)}, u32[]{:S(2)}, u32[]{:S(2)}) collective-permute-start(f32[6,12,8,128]{3,2,1,0:T(8,128)S(1)} %get-tuple-element.33.refs_1_), channel_id=1, source_target_pairs={{0,32},{32,64},{64,96},{96,128},{128,160},{160,192},{192,224},{224... | collective-permute-start | bytes 884744 | tf_op jit(solution)/shard_map/ppermute | solution.py:311
  66.8 1.2 shard_map.54
  67.9 8.3 %all-to-all-done.2 = f32[16,72,128]{2,1,0:T(8,128)S(1)} async-done(((f32[16,72,128]{2,1,0:T(8,128)}), f32[16,72,128]{2,1,0:T(8,128)S(1)}, u32[]{:S(2)}, u32[]{:S(2)}) %all-to-all-start.2) | async-done | bytes 589856 | tf_op jit(solution)/shard_map/all_to_all | solution.py:265
  76.3 0.8 collective-permute-start.5
  77.1 0.0 collective-permute-done.7.refs_4_
  77.1 0.0 collective-permute-done.6.refs_3_
  77.1 0.7 shard_map.55
  77.8 20.7 %all_to_all.30 = f32[16,72,128]{2,1,0:T(8,128)S(1)} all-to-all(f32[16,72,128]{2,1,0:T(8,128)S(1)} %bitcast.19), channel_id=1, replica_groups=mesh['z'=8,'xl'=2,'y'=4,'core'=2,'xh'=2] {'xl','y','core'}, dimensions={0} | all-to-all | bytes 1179648 | tf_op jit(solution)/shard_map/all_to_all | solution.py:265
  98.5 0.0 collective-permute-done.5.other
  98.5 2.1 %shard_map.56 = (f32[16,32,128]{2,1,0:T(8,128)S(1)}, f32[1152,128]{1,0:T(8,128)}) custom-call(f32[1152,128]{1,0:T(8,128)S(1)} %bitcast.16, f32[1152,128]{1,0:T(8,128)S(1)} %collective-permute-done.5.other, f32[1152,128]{1,0:T(8,128)S(1)} %bitcast.17), custom_call_target="tpu_custom_call" | custom-call | flops 1000000 | bytes 2000000 | tf_op jit(solution)/shard_map/pallas_call | solution.py:33
  100.5 11.0 %all_to_all.31.parts = f32[16,32,128]{2,1,0:T(8,128)S(1)} all-to-all(f32[16,32,128]{2,1,0:T(8,128)S(1)} %get-tuple-element.40), channel_id=1, replica_groups=mesh['z'=8,'xl'=2,'y'=4,'core'=2,'xh'=2] {'xl','y','core'}, dimensions={0} | all-to-all | bytes 524288 | tf_op jit(solution)/shard_map/all_to_all | solution.py:265
  111.5 0.7 shard_map.57
  112.2 3.4 %all-to-all-start.5 = ((f32[8,32,128]{2,1,0:T(8,128)}), f32[8,32,128]{2,1,0:T(8,128)S(1)}, u32[]{:S(2)}, u32[]{:S(2)}) async-start(f32[8,32,128]{2,1,0:T(8,128)} %shard_map.57), calls=%async_computation.5 | async-start | bytes 262144 | tf_op jit(solution)/shard_map/all_to_all | solution.py:344
  115.6 9.0 %all-to-all-done.5.parts = f32[8,32,128]{2,1,0:T(8,128)S(1)} async-done(((f32[8,32,128]{2,1,0:T(8,128)}), f32[8,32,128]{2,1,0:T(8,128)S(1)}, u32[]{:S(2)}, u32[]{:S(2)}) %all-to-all-start.5) | async-done | bytes 131104 | tf_op jit(solution)/shard_map/all_to_all | solution.py:344
  124.6 0.8 shard_map.58
  (3 shorter events, 0.1 us)
Async XLA Ops:
  0.6 5.2 %copy-start = (f32[1,6,6,128]{3,0,2,1:T(1,128)S(1)}, f32[1,6,6,128]{3,0,2,1:T(1,128)}, u32[]{:S(2)}) copy-start(f32[1,6,6,128]{3,0,2,1:T(1,128)} %param.3) | copy-start | bytes 55300
  0.6 17.3 %all-to-all-start = ((f32[16,72,128]{2,1,0:T(8,128)}), f32[16,72,128]{2,1,0:T(8,128)S(1)}, u32[]{:S(2)}, u32[]{:S(2)}) async-start(f32[16,72,128]{2,1,0:T(8,128)} %bitcast.20), calls=%async_computation | async-start | bytes 1179648 | tf_op jit(solution)/shard_map/all_to_all | solution.py:265
  5.9 9.1 %collective-permute-start = (f32[36,128]{1,0:T(8,128)S(1)}, f32[36,128]{1,0:T(8,128)S(1)}, u32[]{:S(2)}, u32[]{:S(2)}) collective-permute-start(f32[36,128]{1,0:T(8,128)S(1)} %reshape.37), channel_id=1, source_target_pairs={{16,32},{48,64},{80,96},{112,128},{144,160},{176,192},{208,224},{2... | collective-permute-start | bytes 55304 | tf_op jit(solution)/shard_map/ppermute | solution.py:285
  18.9 15.2 %all-to-all-start.1 = ((f32[16,72,128]{2,1,0:T(8,128)}), f32[16,72,128]{2,1,0:T(8,128)S(1)}, u32[]{:S(2)}, u32[]{:S(2)}) async-start(f32[16,72,128]{2,1,0:T(8,128)} %broadcast_in_dim.2), calls=%async_computation.1 | async-start | bytes 1179648 | tf_op jit(solution)/shard_map/all_to_all | solution.py:265
  22.5 18.9 %collective-permute-start.2 = (f32[12,12,8,128]{3,2,1,0:T(8,128)S(1)}, f32[12,12,8,128]{3,2,1,0:T(8,128)S(1)}, u32[]{:S(2)}, u32[]{:S(2)}) collective-permute-start(f32[12,12,8,128]{3,2,1,0:T(8,128)S(1)} %shard_map.49.refs_0_.refs_1_), channel_id=1, source_target_pairs={{0,224},{32,0},{64,32},{96,64},{128,96},{160,128},{192,160},{224,1... | collective-permute-start | bytes 1769480 | tf_op jit(solution)/shard_map/ppermute | solution.py:289
  28.4 16.4 %collective-permute-start.1 = (f32[12,12,8,128]{3,2,1,0:T(8,128)S(1)}, f32[12,12,8,128]{3,2,1,0:T(8,128)S(1)}, u32[]{:S(2)}, u32[]{:S(2)}) collective-permute-start(f32[12,12,8,128]{3,2,1,0:T(8,128)S(1)} %shard_map.49.refs_0_.refs_1_), channel_id=1, source_target_pairs={{0,32},{32,64},{64,96},{96,128},{128,160},{160,192},{192,224},{224... | collective-permute-start | bytes 1769480 | tf_op jit(solution)/shard_map/ppermute | solution.py:288
  48.0 8.1 %collective-permute-start.4 = (f32[6,12,8,128]{3,2,1,0:T(8,128)S(1)}, f32[6,12,8,128]{3,2,1,0:T(8,128)S(1)}, u32[]{:S(2)}, u32[]{:S(2)}) collective-permute-start(f32[6,12,8,128]{3,2,1,0:T(8,128)S(1)} %get-tuple-element.25.refs_0_), channel_id=1, source_target_pairs={{0,224},{32,0},{64,32},{96,64},{128,96},{160,128},{192,160},{224,1... | collective-permute-start | bytes 884744 | tf_op jit(solution)/shard_map/ppermute | solution.py:311
  48.4 9.2 %collective-permute-start.3 = (f32[6,12,8,128]{3,2,1,0:T(8,128)S(1)}, f32[6,12,8,128]{3,2,1,0:T(8,128)S(1)}, u32[]{:S(2)}, u32[]{:S(2)}) collective-permute-start(f32[6,12,8,128]{3,2,1,0:T(8,128)S(1)} %get-tuple-element.26.refs_1_), channel_id=1, source_target_pairs={{0,32},{32,64},{64,96},{96,128},{128,160},{160,192},{192,224},{224... | collective-permute-start | bytes 884744 | tf_op jit(solution)/shard_map/ppermute | solution.py:311
  59.2 17.1 %all-to-all-start.2 = ((f32[16,72,128]{2,1,0:T(8,128)}), f32[16,72,128]{2,1,0:T(8,128)S(1)}, u32[]{:S(2)}, u32[]{:S(2)}) async-start(f32[16,72,128]{2,1,0:T(8,128)} %bitcast.5), calls=%async_computation.2 | async-start | bytes 1179648 | tf_op jit(solution)/shard_map/all_to_all | solution.py:265
  64.7 12.4 %collective-permute-start.7 = (f32[6,12,8,128]{3,2,1,0:T(8,128)S(1)}, f32[6,12,8,128]{3,2,1,0:T(8,128)S(1)}, u32[]{:S(2)}, u32[]{:S(2)}) collective-permute-start(f32[6,12,8,128]{3,2,1,0:T(8,128)S(1)} %get-tuple-element.32.refs_0_), channel_id=1, source_target_pairs={{0,224},{32,0},{64,32},{96,64},{128,96},{160,128},{192,160},{224,1... | collective-permute-start | bytes 884744 | tf_op jit(solution)/shard_map/ppermute | solution.py:311
  65.0 12.1 %collective-permute-start.6 = (f32[6,12,8,128]{3,2,1,0:T(8,128)S(1)}, f32[6,12,8,128]{3,2,1,0:T(8,128)S(1)}, u32[]{:S(2)}, u32[]{:S(2)}) collective-permute-start(f32[6,12,8,128]{3,2,1,0:T(8,128)S(1)} %get-tuple-element.33.refs_1_), channel_id=1, source_target_pairs={{0,32},{32,64},{64,96},{96,128},{128,160},{160,192},{192,224},{224... | collective-permute-start | bytes 884744 | tf_op jit(solution)/shard_map/ppermute | solution.py:311
  76.3 22.2 %collective-permute-start.5 = (f32[1152,128]{1,0:T(8,128)S(1)}, f32[1152,128]{1,0:T(8,128)S(1)}, u32[]{:S(2)}, u32[]{:S(2)}) collective-permute-start(f32[1152,128]{1,0:T(8,128)S(1)} %bitcast.15), channel_id=1, source_target_pairs={{0,1},{1,0},{2,3},{3,2},{4,5},{5,4},{6,7},{7,6},{8,9},{9,8},{10,11... | collective-permute-start | bytes 1769480 | tf_op jit(solution)/shard_map/ppermute | solution.py:332
  112.2 12.4 %all-to-all-start.5 = ((f32[8,32,128]{2,1,0:T(8,128)}), f32[8,32,128]{2,1,0:T(8,128)S(1)}, u32[]{:S(2)}, u32[]{:S(2)}) async-start(f32[8,32,128]{2,1,0:T(8,128)} %shard_map.57), calls=%async_computation.5 | async-start | bytes 262144 | tf_op jit(solution)/shard_map/all_to_all | solution.py:344

commit v4 on v0

v4 whole, which is shorter than its diff:
```python
import jax
import jax.numpy as jnp
from jax import lax
from jax.experimental import pallas as pl
from jax.experimental.pallas import tpu as pltpu
from jax.sharding import Mesh, PartitionSpec as P

weights = (
    -5369.0 / 1800.0,
    12.0 / 7.0,
    -15.0 / 56.0,
    10.0 / 189.0,
    -1.0 / 112.0,
    2.0 / 825.0,
    -1.0 / 4752.0,
)
lower_edge = 0.0
cut_edge = 3.0
upper_edge = 13.0
CELLS = 96 * 48 * 128

VM = pl.BlockSpec(memory_space=pltpu.VMEM)
SM = pl.BlockSpec(memory_space=pltpu.SMEM)
PARAMS = pltpu.CompilerParams(vmem_limit_bytes=32 * 1024 * 1024)
F32 = jnp.float32

HALF = jax.ShapeDtypeStruct((6, 12, 8, 128), F32)
FULL = jax.ShapeDtypeStruct((12, 12, 8, 128), F32)


def call(body, outs, inputs, specs=None, out_specs=None, scratch=(), flops=1_000_000):
    return pl.pallas_call(
        body,
        out_shape=outs,
        in_specs=specs or [VM] * len(inputs),
        out_specs=out_specs or jax.tree.map(lambda _: VM, outs),
        scratch_shapes=scratch,
        compiler_params=PARAMS,
        cost_estimate=pl.CostEstimate(flops=flops, bytes_accessed=2_000_000, transcendentals=0),
    )(*inputs)


def assemble_body(place, keep, received, own_field, other_field, full, low, high, field):
    first = place[0] == 0
    for xi in range(6):
        for yi in range(6):
            r = xi * 6 + yi
            for g in range(2):
                rows = pl.ds(g * 288 + r, 8, stride=36)
                a = keep[rows, :]
                b = received[rows, :]
                n = yi * 2 + g
                left = jnp.where(first, a, b)
                right = jnp.where(first, b, a)
                full[xi, n] = left
                low[xi, n] = left
                full[6 + xi, n] = right
                high[xi, n] = right
            a = jnp.broadcast_to(own_field[pl.ds(r, 1), :], (8, 128))
            b = jnp.broadcast_to(other_field[pl.ds(r, 1), :], (8, 128))
            field[xi, yi] = jnp.where(first, a, b)
            field[6 + xi, yi] = jnp.where(first, b, a)


def interior_body(alpha, shift, beta, full, field, *refs):
    acc = refs[-1]
    scaled = [-0.5 * alpha * w for w in weights]
    row = lax.broadcasted_iota(jnp.int32, (128, 128), 0)
    column = lax.broadcasted_iota(jnp.int32, (128, 128), 1)
    distance = jnp.abs(row - column)
    band = jnp.zeros((128, 128), F32)
    for k in range(1, 7):
        band = jnp.where(distance == k, F32(scaled[k]), band)
    band = jnp.where(distance == 0, F32(3.0 * scaled[0] - alpha * shift), band)
    for x in range(12):
        along = jnp.dot(
            full[x].reshape(96, 128), band, precision=lax.Precision.HIGHEST, preferred_element_type=F32
        ).reshape(12, 8, 128)
        for g in range(2):
            line = [full[x, yi * 2 + g] for yi in range(6)]
            for yi in range(6):
                n = yi * 2 + g
                total = along[n] + field[x, yi] * F32(alpha) * line[yi]
                for k in range(1, 7):
                    near = [line[yi + s] for s in (k, -k) if 0 <= yi + s < 6]
                    near += [full[x + s, n] for s in (k, -k) if 0 <= x + s < 12]
                    if near:
                        pair = near[0]
                        for v in near[1:]:
                            pair = pair + v
                        total = total + F32(scaled[k]) * pair
                if len(refs) == 2:
                    total = total - F32(beta) * refs[0][x, n]
                acc[x, n] = total


def edge_body(alpha, inside, acc, before_x, after_x, before_y, after_y, full, *halves):
    scaled = [-0.5 * alpha * w for w in weights]
    from_x = [[inside[i] * F32(s) for s in scaled] for i in range(2)]
    from_y = [[inside[2 + i] * F32(s) for s in scaled] for i in range(2)]
    for x in range(12):
        for g in range(2):
            lows = [before_y[x, j * 2 + g] for j in range(6)]
            highs = [after_y[x, j * 2 + g] for j in range(6)]
            for yi in range(6):
                n = yi * 2 + g
                total = acc[x, n]
                for k in range(yi + 1, 7):
                    total = total + from_y[0][k] * lows[6 + yi - k]
                for k in range(6 - yi, 7):
                    total = total + from_y[1][k] * highs[yi + k - 6]
                if x < 6:
                    for k in range(x + 1, 7):
                        total = total + from_x[0][k] * before_x[6 + x - k, n]
                else:
                    for k in range(12 - x, 7):
                        total = total + from_x[1][k] * after_x[x + k - 12, n]
                full[x, n] = total
                if halves:
                    halves[x // 6][x % 6, n] = total


def bricks_body(place, low, high, next_low, last_high, out, rows, sem):
    first = place[0] == 0
    for xi in range(6):
        for yi in range(6):
            for g in range(2):
                n = yi * 2 + g
                start = g * 288 + xi * 6 + yi
                rows[pl.ds(start, 8, stride=36), :] = jnp.where(first, low[xi, n], last_high[xi, n])
                rows[pl.ds(576 + start, 8, stride=36), :] = jnp.where(first, next_low[xi, n], high[xi, n])
    write = pltpu.make_async_copy(rows, out, sem)
    write.start()
    write.wait()


def stack(parts, half, xi, yi):
    left = [p[half][xi, yi * 2 + g] for p in parts for g in range(2)]
    right = [p[half][xi, yi * 2 + 2 + g] for p in parts for g in range(2)]
    return jnp.concatenate([jnp.concatenate(left, axis=0), jnp.concatenate(right, axis=0)], axis=1)


def products(left, right):
    total = None
    for half in range(2):
        for xi in range(6):
            for yi in range(0, 6, 2):
                term = lax.dot_general(
                    stack(left, half, xi, yi),
                    stack(right, half, xi, yi),
                    (((1,), (1,)), ((), ())),
                    precision=lax.Precision.HIGHEST,
                    preferred_element_type=F32,
                )
                total = term if total is None else total + term
    return total


def halves_of(full):
    return full.at[pl.ds(0, 6)], full.at[pl.ds(6, 6)]


def near_gram_body(low, high, applied, next_low, next_high, last_low, last_high, out):
    mine = (low, high)
    total = products([mine, halves_of(applied)], [mine, (next_low, next_high), (last_low, last_high)])
    out[...] = jnp.concatenate([total, jnp.zeros((32, 80), F32)], axis=1)


def far_gram_body(place, low, high, applied, far_low, far_high, near, copies):
    far = products([(low, high), halves_of(applied)], [(far_low, far_high)])
    blocks = [near[:, 0:16], near[:, 16:32], far, near[:, 32:48]]
    total = None
    for p in range(4):
        turned = jnp.concatenate([blocks[(b - p) % 4] for b in range(4)], axis=1)
        total = turned if total is None else jnp.where(place[1] == p, turned, total)
    packed = jnp.concatenate([total[:16], total[16:]], axis=1)
    for n in range(16):
        copies[n] = packed


def sum_body(parts, copies):
    for half in range(2):
        total = parts[half * 8]
        for n in range(1, 8):
            total = total + parts[half * 8 + n]
        for n in range(8):
            copies[n, half * 16 : half * 16 + 16] = total


def finish_body(parts, energy, margin):
    total = parts[0]
    for n in range(1, 8):
        total = total + parts[n]
    total = total * F32(1.0 / CELLS)
    margin[...] = total[:, :64]
    energy[...] = total[:, 64:]


UP = [(i, (i + 1) % 8) for i in range(8)]
DOWN = [(i, (i + 7) % 8) for i in range(8)]
SWAP = [(0, 1), (1, 0)]
RING = ("xl", "xh")
SPOT = (0, 2, 1, 3)
NEXT = [(SPOT[i], SPOT[(i + 1) % 4]) for i in range(4)]
LAST = [(SPOT[i], SPOT[(i + 3) % 4]) for i in range(4)]
ROWS = ("y", "core")


def local(orbitals, potential):
    position_x = lax.axis_index("z")
    position_y = lax.axis_index(ROWS)
    side = lax.axis_index("xl")
    inside = jnp.stack([position_x > 0, position_x < 7, position_y > 0, position_y < 7]).astype(F32)
    place = jnp.stack([side, 2 * lax.axis_index("xh") + side]).astype(jnp.int32)

    half_width = (upper_edge - cut_edge) / 2.0
    centre = (upper_edge + cut_edge) / 2.0
    sigma_first = half_width / (lower_edge - centre)
    tau_value = 2.0 / sigma_first
    sigma_second = 1.0 / (tau_value - sigma_first)
    sigma_third = 1.0 / (tau_value - sigma_second)
    first = (sigma_first / half_width, centre, 0.0)
    second = (2.0 * sigma_second / half_width, centre, sigma_first * sigma_second)
    third = (2.0 * sigma_third / half_width, centre, sigma_second * sigma_third)
    plain = (1.0, 0.0, 0.0)

    mine = orbitals.reshape(1152, 128)
    own_field = potential.reshape(36, 128)
    received = lax.ppermute(lax.dynamic_slice_in_dim(mine, (1 - side) * 576, 576), "xl", SWAP)
    other_field = lax.ppermute(own_field, "xl", SWAP)
    keep = lax.dynamic_slice_in_dim(mine, side * 576, 576)
    full, low, high, field = call(
        assemble_body,
        [FULL, HALF, HALF, jax.ShapeDtypeStruct((12, 6, 8, 128), F32)],
        [place, keep, received, own_field, other_field],
        [SM] + [VM] * 4,
    )

    def step(numbers, planes, previous, outs):
        full, low, high = planes
        halos = (
            lax.ppermute(full, ROWS, UP),
            lax.ppermute(full, ROWS, DOWN),
            lax.ppermute(high, "z", UP),
            lax.ppermute(low, "z", DOWN),
        )

        def interior(*refs):
            interior_body(*numbers, *refs)

        acc = call(interior, FULL, [full, field, *previous], flops=400_000_000)

        def edge(*refs):
            edge_body(numbers[0], *refs)

        return call(edge, outs, [inside, acc, *halos[2:], *halos[:2]], [SM] + [VM] * 5)

    y0 = (full, low, high)
    y1 = step(first, y0, (), [FULL, HALF, HALF])
    y2 = step(second, y1, (y0[0],), [FULL, HALF, HALF])
    y3 = step(third, y2, (y1[0],), [FULL, HALF, HALF])
    applied = step(plain, y3, (), [FULL])[0]
    full, low, high = y3
    next_low = lax.ppermute(low, RING, LAST)
    last_high = lax.ppermute(high, RING, NEXT)
    next_high = lax.ppermute(high, RING, LAST)
    last_low = lax.ppermute(low, RING, NEXT)
    far_low = lax.ppermute(next_low, RING, LAST)
    far_high = lax.ppermute(last_high, RING, NEXT)
    filtered = call(
        bricks_body,
        jax.ShapeDtypeStruct((1152, 128), F32),
        [place, low, high, next_low, last_high],
        [SM] + [VM] * 4,
        out_specs=pl.BlockSpec(memory_space=pl.ANY),
        scratch=[pltpu.VMEM((1152, 128), F32), pltpu.SemaphoreType.DMA],
        flops=400_000_000,
    )
    near = call(
        near_gram_body,
        jax.ShapeDtypeStruct((32, 128), F32),
        [low, high, applied, next_low, next_high, last_low, last_high],
        flops=400_000_000,
    )
    copies = call(
        far_gram_body,
        jax.ShapeDtypeStruct((16, 16, 128), F32),
        [place, low, high, applied, far_low, far_high, near],
        [SM] + [VM] * 6,
    )
    parts = lax.all_to_all(copies, ("xl",) + ROWS, split_axis=0, concat_axis=0, tiled=True)
    copies = call(sum_body, jax.ShapeDtypeStruct((8, 32, 128), F32), [parts])
    parts = lax.all_to_all(copies, "z", split_axis=0, concat_axis=0, tiled=True)
    energy, margin = call(finish_body, [jax.ShapeDtypeStruct((32, 64), F32)] * 2, [parts])
    return filtered.reshape(32, 1, 6, 6, 128), energy, margin


def solution(mesh):
    fine = Mesh(mesh.devices.reshape(8, 2, 4, 2, 2), ("z", "xl", "y", "core", "xh"))
    brick = ("z", "xl", "y", "core")
    return jax.shard_map(
        local,
        mesh=fine,
        in_specs=(P("xh", brick, None, None, None), P(brick, None, None, None)),
        out_specs=(P("xh", brick, None, None, None), P("xh", None), P("xh", None)),
        check_vma=False,
    )
```

time: 876 us -> 113 us (0.13)
  blocking collectives: 555 us -> 12.3 us
  waiting for transfers between devices: 149 us -> 40.4 us
  starting transfers between devices: 115 us -> 43 us
  other arithmetic: 31.7 us -> 0.2 us
  Pallas kernels: 0 us -> 14.9 us
  between operations: 14.4 us -> 0.8 us
    psum x1 -> x0, blocking collectives: 555 us -> none  [local(): lax.psum((margin_rows / cell_count, energy_rows / cell_count), 'brick')]
    ppermute x16 -> x24, starting transfers between devices: 114 us -> 36.4 us  [the longest x4 11.8 us: step(): lax.ppermute(full, ROWS, DOWN)]
    all_gather x2 -> x0, waiting for transfers between devices: 62.9 us -> none  [the longest x1 34.7 us: local(): lax.all_gather(mine_applied, 'orb', axis=0, tiled=True)]
    ppermute x16 -> x24, waiting for transfers between devices: 85.6 us -> 32.7 us  [the longest x4 15.4 us: step(): lax.ppermute(high, 'z', UP)]
    pallas_call x0 -> x14, Pallas kernels: none -> 14.9 us  [call(): pl.pallas_call(body, out_shape=outs, in_specs=specs or [VM] * len(inputs)...]
    mul x10 -> x0, other arithmetic: 13.2 us -> none  [the longest x1 5.56 us: local(): sigma_first / half_width * (hamiltonian_of(values) - centre * values)]
    all_to_all x0 -> x1, blocking collectives: none -> 12.3 us  [local(): lax.all_to_all(copies, ('xl',) + ROWS, split_axis=0, concat_axis=0, tiled...]
    sub x2 -> x0, other arithmetic: 11.2 us -> none  [local(): 2.0 * sigma_next / half_width * (hamiltonian_of(current) - centre * current)]
  transfers between devices with their start and end apart: 18 -> 25, of which waited for: 14 -> 12; matrix products, arithmetic and copies ran while one was open for 2% -> 0% of each run, Pallas kernels for 0% -> 7%
where the time goes in v4:
time: 113 us
  starting transfers between devices  43 us (38%)
  waiting for transfers between devices  40.4 us (36%)
  Pallas kernels  14.9 us (13%)
  blocking collectives  12.3 us (11%)
    ppermute x4, waiting for transfers between devices, step(): lax.ppermute(high, 'z', UP)  15.4 us
    pallas_call x14, Pallas kernels, call(): pl.pallas_call(body, out_shape=outs, in_specs=specs or [VM] * len(inputs)...  14.9 us
    all_to_all x1, blocking collectives, local(): lax.all_to_all(copies, ('xl',) + ROWS, split_axis=0, concat_axis=0, tiled...  12.3 us
    ppermute x4, starting transfers between devices, step(): lax.ppermute(full, ROWS, DOWN)  11.8 us
    ppermute x4, starting transfers between devices, step(): lax.ppermute(low, 'z', DOWN)  9.46 us
    all_to_all x1, waiting for transfers between devices, local(): parts = lax.all_to_all(copies, 'z', split_axis=0, concat_axis=0, tiled=True)  7.69 us
    ppermute x1, waiting for transfers between devices, local(): other_field = lax.ppermute(own_field, 'xl', SWAP)  6.93 us
    all_to_all x1, starting transfers between devices, local(): parts = lax.all_to_all(copies, 'z', split_axis=0, concat_axis=0, tiled=True)  6.62 us
  transfers between devices with their start and end apart: 25, of which 12 were waited for; matrix products, arithmetic and copies ran while one was open for 0% of the time, Pallas kernels for 7%

profile of v4, /device:TPU:4, one launch (start us, length us, event | category | flops | bytes accessed | tf_op | source)
XLA Modules:
  0.0 112.7 jit_solution(14877620197276254945)
XLA Ops:
  0.6 1.1 constant_dynamic-slice_fusion
  1.7 1.3 %collective-permute-start = (f32[576,128]{1,0:T(8,128)S(1)}, f32[576,128]{1,0:T(8,128)S(1)}, u32[]{:S(2)}, u32[]{:S(2)}) collective-permute-start(f32[576,128]{1,0:T(8,128)S(1)} %get-tuple-element.39), channel_id=1, source_target_pairs={{0,16},{16,0},{1,17},{17,1},{2,18},{18,2},{3,19},{19,3},{4,20},{20... | collective-permute-start | bytes 884744 | tf_op jit(solution)/shard_map/ppermute | solution.py:229
  3.1 0.9 collective-permute-start.1
  4.0 0.1 pad_add_fusion.place
  4.1 6.9 %collective-permute-done.1.other_field = f32[36,128]{1,0:T(8,128)S(1)} collective-permute-done((f32[36,128]{1,0:T(8,128)S(1)}, f32[36,128]{1,0:T(8,128)S(1)}, u32[]{:S(2)}, u32[]{:S(2)}) %collective-permute-start.1) | collective-permute-done | bytes 18464 | tf_op jit(solution)/shard_map/ppermute | solution.py:230
  11.0 0.0 collective-permute-done.received
  11.0 0.6 shard_map.49
  11.7 0.0 collective-permute-start.4
  11.7 2.9 %collective-permute-start.5 = (f32[12,12,8,128]{3,2,1,0:T(8,128)S(1)}, f32[12,12,8,128]{3,2,1,0:T(8,128)S(1)}, u32[]{:S(2)}, u32[]{:S(2)}) collective-permute-start(f32[12,12,8,128]{3,2,1,0:T(8,128)S(1)} %get-tuple-element.18.refs_0_.refs_2_), channel_id=1, source_target_pairs={{0,14},{2,0},{4,2},{6,4},{8,6},{10,8},{12,10},{14,12},{1,15},{3,1}... | collective-permute-start | bytes 1769480 | tf_op jit(solution)/shard_map/ppermute | solution.py:243
  14.6 1.9 %collective-permute-start.2 = (f32[6,12,8,128]{3,2,1,0:T(8,128)S(1)}, f32[6,12,8,128]{3,2,1,0:T(8,128)S(1)}, u32[]{:S(2)}, u32[]{:S(2)}) collective-permute-start(f32[6,12,8,128]{3,2,1,0:T(8,128)S(1)} %get-tuple-element.20), channel_id=1, source_target_pairs={{0,32},{32,64},{64,96},{96,128},{128,160},{160,192},{192,224},{224... | collective-permute-start | bytes 884744 | tf_op jit(solution)/shard_map/ppermute | solution.py:244
  16.6 3.9 %collective-permute-start.3 = (f32[6,12,8,128]{3,2,1,0:T(8,128)S(1)}, f32[6,12,8,128]{3,2,1,0:T(8,128)S(1)}, u32[]{:S(2)}, u32[]{:S(2)}) collective-permute-start(f32[6,12,8,128]{3,2,1,0:T(8,128)S(1)} %get-tuple-element.21), channel_id=1, source_target_pairs={{0,224},{32,0},{64,32},{96,64},{128,96},{160,128},{192,160},{224,1... | collective-permute-start | bytes 884744 | tf_op jit(solution)/shard_map/ppermute | solution.py:245
  20.5 0.1 add_convert_fusion.refs_0_
  20.6 1.0 shard_map.50.refs_1_
  21.6 4.8 %collective-permute-done.2.refs_2_ = f32[6,12,8,128]{3,2,1,0:T(8,128)S(1)} collective-permute-done((f32[6,12,8,128]{3,2,1,0:T(8,128)S(1)}, f32[6,12,8,128]{3,2,1,0:T(8,128)S(1)}, u32[]{:S(2)}, u32[]{:S(2)}) %collective-permute-start.2) | collective-permute-done | bytes 294944 | tf_op jit(solution)/shard_map/ppermute | solution.py:244
  26.4 0.0 collective-permute-done.3.refs_3_
  26.4 0.0 collective-permute-done.4.refs_4_
  26.4 0.0 collective-permute-done.5.refs_5_
  26.4 1.0 shard_map.51
  27.4 0.0 collective-permute-start.8
  27.4 2.9 %collective-permute-start.9 = (f32[12,12,8,128]{3,2,1,0:T(8,128)S(1)}, f32[12,12,8,128]{3,2,1,0:T(8,128)S(1)}, u32[]{:S(2)}, u32[]{:S(2)}) collective-permute-start(f32[12,12,8,128]{3,2,1,0:T(8,128)S(1)} %get-tuple-element.22.refs_0_.refs_2_), channel_id=1, source_target_pairs={{0,14},{2,0},{4,2},{6,4},{8,6},{10,8},{12,10},{14,12},{1,15},{3,1}... | collective-permute-start | bytes 1769480 | tf_op jit(solution)/shard_map/ppermute | solution.py:243
  30.4 0.0 collective-permute-start.6
  30.4 3.2 %collective-permute-start.7 = (f32[6,12,8,128]{3,2,1,0:T(8,128)S(1)}, f32[6,12,8,128]{3,2,1,0:T(8,128)S(1)}, u32[]{:S(2)}, u32[]{:S(2)}) collective-permute-start(f32[6,12,8,128]{3,2,1,0:T(8,128)S(1)} %get-tuple-element.24), channel_id=1, source_target_pairs={{0,224},{32,0},{64,32},{96,64},{128,96},{160,128},{192,160},{224,1... | collective-permute-start | bytes 884744 | tf_op jit(solution)/shard_map/ppermute | solution.py:245
  33.6 1.1 %shard_map.52.refs_1_ = f32[12,12,8,128]{3,2,1,0:T(8,128)S(1)} custom-call(f32[12,12,8,128]{3,2,1,0:T(8,128)S(1)} %get-tuple-element.22.refs_0_.refs_2_, f32[12,6,8,128]{3,2,1,0:T(8,128)S(1)} %get-tuple-element.19.refs_1_, f32[12,12,8,128]{3,2,1,0:T(8,128)S(1)} %get-tuple-element.18.refs_0_.refs_2_), custom_call_target="tpu_custom_call" | custom-call | flops 400000000 | bytes 2000000 | tf_op jit(solution)/shard_map/pallas_call | solution.py:32
  34.8 4.5 %collective-permute-done.6.refs_2_ = f32[6,12,8,128]{3,2,1,0:T(8,128)S(1)} collective-permute-done((f32[6,12,8,128]{3,2,1,0:T(8,128)S(1)}, f32[6,12,8,128]{3,2,1,0:T(8,128)S(1)}, u32[]{:S(2)}, u32[]{:S(2)}) %collective-permute-start.6) | collective-permute-done | bytes 294944 | tf_op jit(solution)/shard_map/ppermute | solution.py:244
  39.2 0.0 collective-permute-done.7.refs_3_
  39.2 0.0 collective-permute-done.8.refs_4_
  39.2 1.0 shard_map.53
  40.2 0.0 collective-permute-start.12
  40.3 2.9 %collective-permute-start.13 = (f32[12,12,8,128]{3,2,1,0:T(8,128)S(1)}, f32[12,12,8,128]{3,2,1,0:T(8,128)S(1)}, u32[]{:S(2)}, u32[]{:S(2)}) collective-permute-start(f32[12,12,8,128]{3,2,1,0:T(8,128)S(1)} %get-tuple-element.25.refs_0_), channel_id=1, source_target_pairs={{0,14},{2,0},{4,2},{6,4},{8,6},{10,8},{12,10},{14,12},{1,15},{3,1}... | collective-permute-start | bytes 1769480 | tf_op jit(solution)/shard_map/ppermute | solution.py:243
  43.2 2.5 %collective-permute-start.10 = (f32[6,12,8,128]{3,2,1,0:T(8,128)S(1)}, f32[6,12,8,128]{3,2,1,0:T(8,128)S(1)}, u32[]{:S(2)}, u32[]{:S(2)}) collective-permute-start(f32[6,12,8,128]{3,2,1,0:T(8,128)S(1)} %get-tuple-element.26), channel_id=1, source_target_pairs={{0,32},{32,64},{64,96},{96,128},{128,160},{160,192},{192,224},{224... | collective-permute-start | bytes 884744 | tf_op jit(solution)/shard_map/ppermute | solution.py:244
  45.6 0.8 collective-permute-start.11
  46.4 1.1 %shard_map.54.refs_1_ = f32[12,12,8,128]{3,2,1,0:T(8,128)S(1)} custom-call(f32[12,12,8,128]{3,2,1,0:T(8,128)S(1)} %get-tuple-element.25.refs_0_, f32[12,6,8,128]{3,2,1,0:T(8,128)S(1)} %get-tuple-element.19.refs_1_, f32[12,12,8,128]{3,2,1,0:T(8,128)S(1)} %get-tuple-element.22.refs_0_.refs_2_), custom_call_target="tpu_custom_call" | custom-call | flops 400000000 | bytes 2000000 | tf_op jit(solution)/shard_map/pallas_call | solution.py:32
  47.6 4.2 %collective-permute-done.10.refs_2_ = f32[6,12,8,128]{3,2,1,0:T(8,128)S(1)} collective-permute-done((f32[6,12,8,128]{3,2,1,0:T(8,128)S(1)}, f32[6,12,8,128]{3,2,1,0:T(8,128)S(1)}, u32[]{:S(2)}, u32[]{:S(2)}) %collective-permute-start.10) | collective-permute-done | bytes 294944 | tf_op jit(solution)/shard_map/ppermute | solution.py:244
  51.8 1.0 collective-permute-done.11.refs_3_
  52.7 0.0 collective-permute-done.12.refs_4_
  52.7 1.0 shard_map.55
  53.7 1.8 %collective-permute-start.16 = (f32[6,12,8,128]{3,2,1,0:T(8,128)S(1)}, f32[6,12,8,128]{3,2,1,0:T(8,128)S(1)}, u32[]{:S(2)}, u32[]{:S(2)}) collective-permute-start(f32[6,12,8,128]{3,2,1,0:T(8,128)S(1)} %get-tuple-element.29.high), channel_id=1, source_target_pairs={{0,32},{32,64},{64,96},{96,128},{128,160},{160,192},{192,224},{224... | collective-permute-start | bytes 884744 | tf_op jit(solution)/shard_map/ppermute | solution.py:244
  55.5 0.0 collective-permute-start.18
  55.5 3.0 %collective-permute-start.19 = (f32[12,12,8,128]{3,2,1,0:T(8,128)S(1)}, f32[12,12,8,128]{3,2,1,0:T(8,128)S(1)}, u32[]{:S(2)}, u32[]{:S(2)}) collective-permute-start(f32[12,12,8,128]{3,2,1,0:T(8,128)S(1)} %get-tuple-element.30.refs_0_), channel_id=1, source_target_pairs={{0,14},{2,0},{4,2},{6,4},{8,6},{10,8},{12,10},{14,12},{1,15},{3,1}... | collective-permute-start | bytes 1769480 | tf_op jit(solution)/shard_map/ppermute | solution.py:243
  58.5 1.5 %collective-permute-start.17 = (f32[6,12,8,128]{3,2,1,0:T(8,128)S(1)}, f32[6,12,8,128]{3,2,1,0:T(8,128)S(1)}, u32[]{:S(2)}, u32[]{:S(2)}) collective-permute-start(f32[6,12,8,128]{3,2,1,0:T(8,128)S(1)} %get-tuple-element.28.low), channel_id=1, source_target_pairs={{0,224},{32,0},{64,32},{96,64},{128,96},{160,128},{192,160},{224,1... | collective-permute-start | bytes 884744 | tf_op jit(solution)/shard_map/ppermute | solution.py:245
  60.0 0.5 collective-permute-start.14
  60.5 1.9 %collective-permute-done.16.refs_2_ = f32[6,12,8,128]{3,2,1,0:T(8,128)S(1)} collective-permute-done((f32[6,12,8,128]{3,2,1,0:T(8,128)S(1)}, f32[6,12,8,128]{3,2,1,0:T(8,128)S(1)}, u32[]{:S(2)}, u32[]{:S(2)}) %collective-permute-start.16) | collective-permute-done | bytes 294944 | tf_op jit(solution)/shard_map/ppermute | solution.py:244
  62.4 1.2 %collective-permute-start.15 = (f32[6,12,8,128]{3,2,1,0:T(8,128)S(1)}, f32[6,12,8,128]{3,2,1,0:T(8,128)S(1)}, u32[]{:S(2)}, u32[]{:S(2)}) collective-permute-start(f32[6,12,8,128]{3,2,1,0:T(8,128)S(1)} %get-tuple-element.29.high), channel_id=1, source_target_pairs={{0,16},{16,1},{1,17},{17,0},{2,18},{18,3},{3,19},{19,2},{4,20},{20... | collective-permute-start | bytes 884744 | tf_op jit(solution)/shard_map/ppermute | solution.py:265
  63.6 1.6 %collective-permute-done.17.refs_3_ = f32[6,12,8,128]{3,2,1,0:T(8,128)S(1)} collective-permute-done((f32[6,12,8,128]{3,2,1,0:T(8,128)S(1)}, f32[6,12,8,128]{3,2,1,0:T(8,128)S(1)}, u32[]{:S(2)}, u32[]{:S(2)}) %collective-permute-start.17) | collective-permute-done | bytes 294944 | tf_op jit(solution)/shard_map/ppermute | solution.py:245
  65.2 0.5 collective-permute-start.22
  65.8 3.1 %collective-permute-done.14.next_low = f32[6,12,8,128]{3,2,1,0:T(8,128)S(1)} collective-permute-done((f32[6,12,8,128]{3,2,1,0:T(8,128)S(1)}, f32[6,12,8,128]{3,2,1,0:T(8,128)S(1)}, u32[]{:S(2)}, u32[]{:S(2)}) %collective-permute-start.14) | collective-permute-done | bytes 294944 | tf_op jit(solution)/shard_map/ppermute | solution.py:264
  68.9 2.4 %collective-permute-start.23 = (f32[6,12,8,128]{3,2,1,0:T(8,128)S(1)}, f32[6,12,8,128]{3,2,1,0:T(8,128)S(1)}, u32[]{:S(2)}, u32[]{:S(2)}) collective-permute-start(f32[6,12,8,128]{3,2,1,0:T(8,128)S(1)} %get-tuple-element.28.low), channel_id=1, source_target_pairs={{0,16},{16,1},{1,17},{17,0},{2,18},{18,3},{3,19},{19,2},{4,20},{20... | collective-permute-start | bytes 884744 | tf_op jit(solution)/shard_map/ppermute | solution.py:267
  71.3 1.1 collective-permute-done.15.last_high
  72.4 0.5 collective-permute-start.20
  72.8 0.0 collective-permute-done.18.refs_4_
  72.8 1.6 %collective-permute-start.21 = (f32[6,12,8,128]{3,2,1,0:T(8,128)S(1)}, f32[6,12,8,128]{3,2,1,0:T(8,128)S(1)}, u32[]{:S(2)}, u32[]{:S(2)}) collective-permute-start(f32[6,12,8,128]{3,2,1,0:T(8,128)S(1)} %collective-permute-done.15.last_high), channel_id=1, source_target_pairs={{0,16},{16,1},{1,17},{17,0},{2,18},{18,3},{3,19},{19,2},{4,20},{20... | collective-permute-start | bytes 884744 | tf_op jit(solution)/shard_map/ppermute | solution.py:269
  74.4 1.1 shard_map.57.refs_1_
  75.5 1.0 shard_map.58.applied
  76.5 1.9 %collective-permute-done.23.last_low = f32[6,12,8,128]{3,2,1,0:T(8,128)S(1)} collective-permute-done((f32[6,12,8,128]{3,2,1,0:T(8,128)S(1)}, f32[6,12,8,128]{3,2,1,0:T(8,128)S(1)}, u32[]{:S(2)}, u32[]{:S(2)}) %collective-permute-start.23) | collective-permute-done | bytes 294944 | tf_op jit(solution)/shard_map/ppermute | solution.py:267
  78.4 1.5 %shard_map.59.near = f32[32,128]{1,0:T(8,128)S(1)} custom-call(f32[6,12,8,128]{3,2,1,0:T(8,128)S(1)} %get-tuple-element.28.low, f32[6,12,8,128]{3,2,1,0:T(8,128)S(1)} %get-tuple-element.29.high, f32[12,12,8,128]{3,2,1,0:T(8,128)S(1)} %shard_map.58.applied, f32[6,12,8,128]{3,2,1,0:T(8,128)S(1)} %collective-permute-done.14.next_low, ...), custom_call_target="tpu_custom_call" | custom-call | flops 400000000 | bytes 2000000 | tf_op jit(solution)/shard_map/pallas_call | solution.py:32
  79.9 0.0 collective-permute-done.20.far_low
  79.9 1.7 %collective-permute-done.21.far_high = f32[6,12,8,128]{3,2,1,0:T(8,128)S(1)} collective-permute-done((f32[6,12,8,128]{3,2,1,0:T(8,128)S(1)}, f32[6,12,8,128]{3,2,1,0:T(8,128)S(1)}, u32[]{:S(2)}, u32[]{:S(2)}) %collective-permute-start.21) | collective-permute-done | bytes 294944 | tf_op jit(solution)/shard_map/ppermute | solution.py:269
  81.6 1.7 %shard_map.60 = f32[16,16,128]{2,1,0:T(8,128)S(1)} custom-call(s32[2]{0:T(128)S(1)} %pad_add_fusion.place, f32[6,12,8,128]{3,2,1,0:T(8,128)S(1)} %get-tuple-element.28.low, f32[6,12,8,128]{3,2,1,0:T(8,128)S(1)} %get-tuple-element.29.high, f32[12,12,8,128]{3,2,1,0:T(8,128)S(1)} %shard_map.58.applied, f32[6,12,8,128]{3,2,1,0:T(8,128)S(1)} %collective-permute-done.20.far_low, ...), custom_call_target="tpu_custom_call" | custom-call | flops 1000000 | bytes 2000000 | tf_op jit(solution)/shard_map/pallas_call | solution.py:32
  83.3 12.3 %all_to_all.10.parts = f32[16,16,128]{2,1,0:T(8,128)S(1)} all-to-all(f32[16,16,128]{2,1,0:T(8,128)S(1)} %shard_map.60), channel_id=1, replica_groups=mesh['z'=8,'xl'=2,'y'=4,'core'=2,'xh'=2] {'xl','y','core'}, dimensions={0} | all-to-all | bytes 262144 | tf_op jit(solution)/shard_map/all_to_all | solution.py:291
  95.6 0.7 shard_map.61
  96.3 6.6 %all-to-all-start.1 = ((f32[8,32,128]{2,1,0:T(8,128)}), f32[8,32,128]{2,1,0:T(8,128)S(1)}, u32[]{:S(2)}, u32[]{:S(2)}) async-start(f32[8,32,128]{2,1,0:T(8,128)} %shard_map.61), calls=%async_computation.1 | async-start | bytes 262144 | tf_op jit(solution)/shard_map/all_to_all | solution.py:293
  102.9 1.4 %shard_map.56 = f32[1152,128]{1,0:T(8,128)} custom-call(s32[2]{0:T(128)S(1)} %pad_add_fusion.place, f32[6,12,8,128]{3,2,1,0:T(8,128)S(1)} %get-tuple-element.28.low, f32[6,12,8,128]{3,2,1,0:T(8,128)S(1)} %get-tuple-element.29.high, f32[6,12,8,128]{3,2,1,0:T(8,128)S(1)} %collective-permute-done.14.next_low, ...), custom_call_target="tpu_custom_call" | custom-call | flops 400000000 | bytes 2000000 | tf_op jit(solution)/shard_map/pallas_call | solution.py:32
  104.3 7.7 %all-to-all-done.1.parts = f32[8,32,128]{2,1,0:T(8,128)S(1)} async-done(((f32[8,32,128]{2,1,0:T(8,128)}), f32[8,32,128]{2,1,0:T(8,128)S(1)}, u32[]{:S(2)}, u32[]{:S(2)}) %all-to-all-start.1) | async-done | bytes 131104 | tf_op jit(solution)/shard_map/all_to_all | solution.py:293
  112.0 0.7 shard_map.62
  (8 shorter events, 0.1 us)
Async XLA Ops:
  0.6 2.4 %copy-start = (f32[1,6,6,128]{3,0,2,1:T(1,128)S(1)}, f32[1,6,6,128]{3,0,2,1:T(1,128)}, u32[]{:S(2)}) copy-start(f32[1,6,6,128]{3,0,2,1:T(1,128)} %param.3) | copy-start | bytes 55300
  1.7 9.3 %collective-permute-start = (f32[576,128]{1,0:T(8,128)S(1)}, f32[576,128]{1,0:T(8,128)S(1)}, u32[]{:S(2)}, u32[]{:S(2)}) collective-permute-start(f32[576,128]{1,0:T(8,128)S(1)} %get-tuple-element.39), channel_id=1, source_target_pairs={{0,16},{16,0},{1,17},{17,1},{2,18},{18,2},{3,19},{19,3},{4,20},{20... | collective-permute-start | bytes 884744 | tf_op jit(solution)/shard_map/ppermute | solution.py:229
  3.1 7.9 %collective-permute-start.1 = (f32[36,128]{1,0:T(8,128)S(1)}, f32[36,128]{1,0:T(8,128)S(1)}, u32[]{:S(2)}, u32[]{:S(2)}) collective-permute-start(f32[36,128]{1,0:T(8,128)S(1)} %reshape.16.own_field), channel_id=1, source_target_pairs={{0,16},{16,0},{1,17},{17,1},{2,18},{18,2},{3,19},{19,3},{4,20},{20... | collective-permute-start | bytes 55304 | tf_op jit(solution)/shard_map/ppermute | solution.py:230
  11.7 14.7 %collective-permute-start.4 = (f32[12,12,8,128]{3,2,1,0:T(8,128)S(1)}, f32[12,12,8,128]{3,2,1,0:T(8,128)S(1)}, u32[]{:S(2)}, u32[]{:S(2)}) collective-permute-start(f32[12,12,8,128]{3,2,1,0:T(8,128)S(1)} %get-tuple-element.18.refs_0_.refs_2_), channel_id=1, source_target_pairs={{0,2},{2,4},{4,6},{6,8},{8,10},{10,12},{12,14},{14,0},{1,3},{3,5},... | collective-permute-start | bytes 1769480 | tf_op jit(solution)/shard_map/ppermute | solution.py:242
  11.7 14.7 %collective-permute-start.5 = (f32[12,12,8,128]{3,2,1,0:T(8,128)S(1)}, f32[12,12,8,128]{3,2,1,0:T(8,128)S(1)}, u32[]{:S(2)}, u32[]{:S(2)}) collective-permute-start(f32[12,12,8,128]{3,2,1,0:T(8,128)S(1)} %get-tuple-element.18.refs_0_.refs_2_), channel_id=1, source_target_pairs={{0,14},{2,0},{4,2},{6,4},{8,6},{10,8},{12,10},{14,12},{1,15},{3,1}... | collective-permute-start | bytes 1769480 | tf_op jit(solution)/shard_map/ppermute | solution.py:243
  14.6 11.8 %collective-permute-start.2 = (f32[6,12,8,128]{3,2,1,0:T(8,128)S(1)}, f32[6,12,8,128]{3,2,1,0:T(8,128)S(1)}, u32[]{:S(2)}, u32[]{:S(2)}) collective-permute-start(f32[6,12,8,128]{3,2,1,0:T(8,128)S(1)} %get-tuple-element.20), channel_id=1, source_target_pairs={{0,32},{32,64},{64,96},{96,128},{128,160},{160,192},{192,224},{224... | collective-permute-start | bytes 884744 | tf_op jit(solution)/shard_map/ppermute | solution.py:244
  16.6 9.8 %collective-permute-start.3 = (f32[6,12,8,128]{3,2,1,0:T(8,128)S(1)}, f32[6,12,8,128]{3,2,1,0:T(8,128)S(1)}, u32[]{:S(2)}, u32[]{:S(2)}) collective-permute-start(f32[6,12,8,128]{3,2,1,0:T(8,128)S(1)} %get-tuple-element.21), channel_id=1, source_target_pairs={{0,224},{32,0},{64,32},{96,64},{128,96},{160,128},{192,160},{224,1... | collective-permute-start | bytes 884744 | tf_op jit(solution)/shard_map/ppermute | solution.py:245
  27.4 11.8 %collective-permute-start.8 = (f32[12,12,8,128]{3,2,1,0:T(8,128)S(1)}, f32[12,12,8,128]{3,2,1,0:T(8,128)S(1)}, u32[]{:S(2)}, u32[]{:S(2)}) collective-permute-start(f32[12,12,8,128]{3,2,1,0:T(8,128)S(1)} %get-tuple-element.22.refs_0_.refs_2_), channel_id=1, source_target_pairs={{0,2},{2,4},{4,6},{6,8},{8,10},{10,12},{12,14},{14,0},{1,3},{3,5},... | collective-permute-start | bytes 1769480 | tf_op jit(solution)/shard_map/ppermute | solution.py:242
  27.4 11.8 %collective-permute-start.9 = (f32[12,12,8,128]{3,2,1,0:T(8,128)S(1)}, f32[12,12,8,128]{3,2,1,0:T(8,128)S(1)}, u32[]{:S(2)}, u32[]{:S(2)}) collective-permute-start(f32[12,12,8,128]{3,2,1,0:T(8,128)S(1)} %get-tuple-element.22.refs_0_.refs_2_), channel_id=1, source_target_pairs={{0,14},{2,0},{4,2},{6,4},{8,6},{10,8},{12,10},{14,12},{1,15},{3,1}... | collective-permute-start | bytes 1769480 | tf_op jit(solution)/shard_map/ppermute | solution.py:243
  30.4 8.9 %collective-permute-start.6 = (f32[6,12,8,128]{3,2,1,0:T(8,128)S(1)}, f32[6,12,8,128]{3,2,1,0:T(8,128)S(1)}, u32[]{:S(2)}, u32[]{:S(2)}) collective-permute-start(f32[6,12,8,128]{3,2,1,0:T(8,128)S(1)} %get-tuple-element.23), channel_id=1, source_target_pairs={{0,32},{32,64},{64,96},{96,128},{128,160},{160,192},{192,224},{224... | collective-permute-start | bytes 884744 | tf_op jit(solution)/shard_map/ppermute | solution.py:244
  30.4 8.9 %collective-permute-start.7 = (f32[6,12,8,128]{3,2,1,0:T(8,128)S(1)}, f32[6,12,8,128]{3,2,1,0:T(8,128)S(1)}, u32[]{:S(2)}, u32[]{:S(2)}) collective-permute-start(f32[6,12,8,128]{3,2,1,0:T(8,128)S(1)} %get-tuple-element.24), channel_id=1, source_target_pairs={{0,224},{32,0},{64,32},{96,64},{128,96},{160,128},{192,160},{224,1... | collective-permute-start | bytes 884744 | tf_op jit(solution)/shard_map/ppermute | solution.py:245
  40.2 12.5 %collective-permute-start.12 = (f32[12,12,8,128]{3,2,1,0:T(8,128)S(1)}, f32[12,12,8,128]{3,2,1,0:T(8,128)S(1)}, u32[]{:S(2)}, u32[]{:S(2)}) collective-permute-start(f32[12,12,8,128]{3,2,1,0:T(8,128)S(1)} %get-tuple-element.25.refs_0_), channel_id=1, source_target_pairs={{0,2},{2,4},{4,6},{6,8},{8,10},{10,12},{12,14},{14,0},{1,3},{3,5},... | collective-permute-start | bytes 1769480 | tf_op jit(solution)/shard_map/ppermute | solution.py:242
  40.3 12.5 %collective-permute-start.13 = (f32[12,12,8,128]{3,2,1,0:T(8,128)S(1)}, f32[12,12,8,128]{3,2,1,0:T(8,128)S(1)}, u32[]{:S(2)}, u32[]{:S(2)}) collective-permute-start(f32[12,12,8,128]{3,2,1,0:T(8,128)S(1)} %get-tuple-element.25.refs_0_), channel_id=1, source_target_pairs={{0,14},{2,0},{4,2},{6,4},{8,6},{10,8},{12,10},{14,12},{1,15},{3,1}... | collective-permute-start | bytes 1769480 | tf_op jit(solution)/shard_map/ppermute | solution.py:243
  43.2 8.6 %collective-permute-start.10 = (f32[6,12,8,128]{3,2,1,0:T(8,128)S(1)}, f32[6,12,8,128]{3,2,1,0:T(8,128)S(1)}, u32[]{:S(2)}, u32[]{:S(2)}) collective-permute-start(f32[6,12,8,128]{3,2,1,0:T(8,128)S(1)} %get-tuple-element.26), channel_id=1, source_target_pairs={{0,32},{32,64},{64,96},{96,128},{128,160},{160,192},{192,224},{224... | collective-permute-start | bytes 884744 | tf_op jit(solution)/shard_map/ppermute | solution.py:244
  45.6 7.1 %collective-permute-start.11 = (f32[6,12,8,128]{3,2,1,0:T(8,128)S(1)}, f32[6,12,8,128]{3,2,1,0:T(8,128)S(1)}, u32[]{:S(2)}, u32[]{:S(2)}) collective-permute-start(f32[6,12,8,128]{3,2,1,0:T(8,128)S(1)} %get-tuple-element.27), channel_id=1, source_target_pairs={{0,224},{32,0},{64,32},{96,64},{128,96},{160,128},{192,160},{224,1... | collective-permute-start | bytes 884744 | tf_op jit(solution)/shard_map/ppermute | solution.py:245
  53.7 8.7 %collective-permute-start.16 = (f32[6,12,8,128]{3,2,1,0:T(8,128)S(1)}, f32[6,12,8,128]{3,2,1,0:T(8,128)S(1)}, u32[]{:S(2)}, u32[]{:S(2)}) collective-permute-start(f32[6,12,8,128]{3,2,1,0:T(8,128)S(1)} %get-tuple-element.29.high), channel_id=1, source_target_pairs={{0,32},{32,64},{64,96},{96,128},{128,160},{160,192},{192,224},{224... | collective-permute-start | bytes 884744 | tf_op jit(solution)/shard_map/ppermute | solution.py:244
  55.5 17.3 %collective-permute-start.18 = (f32[12,12,8,128]{3,2,1,0:T(8,128)S(1)}, f32[12,12,8,128]{3,2,1,0:T(8,128)S(1)}, u32[]{:S(2)}, u32[]{:S(2)}) collective-permute-start(f32[12,12,8,128]{3,2,1,0:T(8,128)S(1)} %get-tuple-element.30.refs_0_), channel_id=1, source_target_pairs={{0,2},{2,4},{4,6},{6,8},{8,10},{10,12},{12,14},{14,0},{1,3},{3,5},... | collective-permute-start | bytes 1769480 | tf_op jit(solution)/shard_map/ppermute | solution.py:242
  55.5 19.9 %collective-permute-start.19 = (f32[12,12,8,128]{3,2,1,0:T(8,128)S(1)}, f32[12,12,8,128]{3,2,1,0:T(8,128)S(1)}, u32[]{:S(2)}, u32[]{:S(2)}) collective-permute-start(f32[12,12,8,128]{3,2,1,0:T(8,128)S(1)} %get-tuple-element.30.refs_0_), channel_id=1, source_target_pairs={{0,14},{2,0},{4,2},{6,4},{8,6},{10,8},{12,10},{14,12},{1,15},{3,1}... | collective-permute-start | bytes 1769480 | tf_op jit(solution)/shard_map/ppermute | solution.py:243
  58.5 6.7 %collective-permute-start.17 = (f32[6,12,8,128]{3,2,1,0:T(8,128)S(1)}, f32[6,12,8,128]{3,2,1,0:T(8,128)S(1)}, u32[]{:S(2)}, u32[]{:S(2)}) collective-permute-start(f32[6,12,8,128]{3,2,1,0:T(8,128)S(1)} %get-tuple-element.28.low), channel_id=1, source_target_pairs={{0,224},{32,0},{64,32},{96,64},{128,96},{160,128},{192,160},{224,1... | collective-permute-start | bytes 884744 | tf_op jit(solution)/shard_map/ppermute | solution.py:245
  60.0 8.9 %collective-permute-start.14 = (f32[6,12,8,128]{3,2,1,0:T(8,128)S(1)}, f32[6,12,8,128]{3,2,1,0:T(8,128)S(1)}, u32[]{:S(2)}, u32[]{:S(2)}) collective-permute-start(f32[6,12,8,128]{3,2,1,0:T(8,128)S(1)} %get-tuple-element.28.low), channel_id=1, source_target_pairs={{0,17},{16,0},{1,16},{17,1},{2,19},{18,2},{3,18},{19,3},{4,21},{20... | collective-permute-start | bytes 884744 | tf_op jit(solution)/shard_map/ppermute | solution.py:264
  62.4 9.9 %collective-permute-start.15 = (f32[6,12,8,128]{3,2,1,0:T(8,128)S(1)}, f32[6,12,8,128]{3,2,1,0:T(8,128)S(1)}, u32[]{:S(2)}, u32[]{:S(2)}) collective-permute-start(f32[6,12,8,128]{3,2,1,0:T(8,128)S(1)} %get-tuple-element.29.high), channel_id=1, source_target_pairs={{0,16},{16,1},{1,17},{17,0},{2,18},{18,3},{3,19},{19,2},{4,20},{20... | collective-permute-start | bytes 884744 | tf_op jit(solution)/shard_map/ppermute | solution.py:265
  65.2 11.2 %collective-permute-start.22 = (f32[6,12,8,128]{3,2,1,0:T(8,128)S(1)}, f32[6,12,8,128]{3,2,1,0:T(8,128)S(1)}, u32[]{:S(2)}, u32[]{:S(2)}) collective-permute-start(f32[6,12,8,128]{3,2,1,0:T(8,128)S(1)} %get-tuple-element.29.high), channel_id=1, source_target_pairs={{0,17},{16,0},{1,16},{17,1},{2,19},{18,2},{3,18},{19,3},{4,21},{20... | collective-permute-start | bytes 884744 | tf_op jit(solution)/shard_map/ppermute | solution.py:266
  68.9 9.5 %collective-permute-start.23 = (f32[6,12,8,128]{3,2,1,0:T(8,128)S(1)}, f32[6,12,8,128]{3,2,1,0:T(8,128)S(1)}, u32[]{:S(2)}, u32[]{:S(2)}) collective-permute-start(f32[6,12,8,128]{3,2,1,0:T(8,128)S(1)} %get-tuple-element.28.low), channel_id=1, source_target_pairs={{0,16},{16,1},{1,17},{17,0},{2,18},{18,3},{3,19},{19,2},{4,20},{20... | collective-permute-start | bytes 884744 | tf_op jit(solution)/shard_map/ppermute | solution.py:267
  72.4 7.5 %collective-permute-start.20 = (f32[6,12,8,128]{3,2,1,0:T(8,128)S(1)}, f32[6,12,8,128]{3,2,1,0:T(8,128)S(1)}, u32[]{:S(2)}, u32[]{:S(2)}) collective-permute-start(f32[6,12,8,128]{3,2,1,0:T(8,128)S(1)} %collective-permute-done.14.next_low), channel_id=1, source_target_pairs={{0,17},{16,0},{1,16},{17,1},{2,19},{18,2},{3,18},{19,3},{4,21},{20... | collective-permute-start | bytes 884744 | tf_op jit(solution)/shard_map/ppermute | solution.py:268
  72.8 8.7 %collective-permute-start.21 = (f32[6,12,8,128]{3,2,1,0:T(8,128)S(1)}, f32[6,12,8,128]{3,2,1,0:T(8,128)S(1)}, u32[]{:S(2)}, u32[]{:S(2)}) collective-permute-start(f32[6,12,8,128]{3,2,1,0:T(8,128)S(1)} %collective-permute-done.15.last_high), channel_id=1, source_target_pairs={{0,16},{16,1},{1,17},{17,0},{2,18},{18,3},{3,19},{19,2},{4,20},{20... | collective-permute-start | bytes 884744 | tf_op jit(solution)/shard_map/ppermute | solution.py:269
  96.3 15.7 %all-to-all-start.1 = ((f32[8,32,128]{2,1,0:T(8,128)}), f32[8,32,128]{2,1,0:T(8,128)S(1)}, u32[]{:S(2)}, u32[]{:S(2)}) async-start(f32[8,32,128]{2,1,0:T(8,128)} %shard_map.61), calls=%async_computation.1 | async-start | bytes 262144 | tf_op jit(solution)/shard_map/all_to_all | solution.py:293

commit v5 on v4

--- a/solution.py
+++ b/solution.py
@@ -40,14 +40,14 @@
     )(*inputs)
 
 
-def assemble_body(place, keep, received, own_field, other_field, full, low, high, field):
+def assemble_body(place, mine, received, own_field, other_field, full, low, high, field):
     first = place[0] == 0
     for xi in range(6):
         for yi in range(6):
             r = xi * 6 + yi
             for g in range(2):
                 rows = pl.ds(g * 288 + r, 8, stride=36)
-                a = keep[rows, :]
+                a = jnp.where(first, mine[rows, :], mine[pl.ds(576 + g * 288 + r, 8, stride=36), :])
                 b = received[rows, :]
                 n = yi * 2 + g
                 left = jnp.where(first, a, b)
@@ -140,9 +140,9 @@
     return jnp.concatenate([jnp.concatenate(left, axis=0), jnp.concatenate(right, axis=0)], axis=1)
 
 
-def products(left, right):
+def products(left, right, halves=(0, 1)):
     total = None
-    for half in range(2):
+    for half in halves:
         for xi in range(6):
             for yi in range(0, 6, 2):
                 term = lax.dot_general(
@@ -166,8 +166,13 @@
     out[...] = jnp.concatenate([total, jnp.zeros((32, 80), F32)], axis=1)
 
 
-def far_gram_body(place, low, high, applied, far_low, far_high, near, copies):
-    far = products([(low, high), halves_of(applied)], [(far_low, far_high)])
+def far_low_body(low, high, applied, far_low, out):
+    far = products([(low, high), halves_of(applied)], [(far_low, None)], (0,))
+    out[...] = jnp.concatenate([far, jnp.zeros((32, 112), F32)], axis=1)
+
+
+def far_gram_body(place, low, high, applied, far_high, near, far_part, copies):
+    far = far_part[:, 0:16] + products([(low, high), halves_of(applied)], [(None, far_high)], (1,))
     blocks = [near[:, 0:16], near[:, 16:32], far, near[:, 32:48]]
     total = None
     for p in range(4):
@@ -228,15 +233,14 @@
     own_field = potential.reshape(36, 128)
     received = lax.ppermute(lax.dynamic_slice_in_dim(mine, (1 - side) * 576, 576), "xl", SWAP)
     other_field = lax.ppermute(own_field, "xl", SWAP)
-    keep = lax.dynamic_slice_in_dim(mine, side * 576, 576)
     full, low, high, field = call(
         assemble_body,
         [FULL, HALF, HALF, jax.ShapeDtypeStruct((12, 6, 8, 128), F32)],
-        [place, keep, received, own_field, other_field],
+        [place, mine, received, own_field, other_field],
         [SM] + [VM] * 4,
     )
 
-    def step(numbers, planes, previous, outs):
+    def step(numbers, planes, previous, outs, others=()):
         full, low, high = planes
         halos = (
             lax.ppermute(full, ROWS, UP),
@@ -250,6 +254,9 @@
 
         acc = call(interior, FULL, [full, field, *previous], flops=400_000_000)
 
+        if others:
+            acc = lax.optimization_barrier((acc, *others))[0]
+
         def edge(*refs):
             edge_body(numbers[0], *refs)
 
@@ -259,12 +266,12 @@
     y1 = step(first, y0, (), [FULL, HALF, HALF])
     y2 = step(second, y1, (y0[0],), [FULL, HALF, HALF])
     y3 = step(third, y2, (y1[0],), [FULL, HALF, HALF])
-    applied = step(plain, y3, (), [FULL])[0]
     full, low, high = y3
     next_low = lax.ppermute(low, RING, LAST)
     last_high = lax.ppermute(high, RING, NEXT)
     next_high = lax.ppermute(high, RING, LAST)
     last_low = lax.ppermute(low, RING, NEXT)
+    applied = step(plain, y3, (), [FULL], (next_low, last_high, next_high, last_low))[0]
     far_low = lax.ppermute(next_low, RING, LAST)
     far_high = lax.ppermute(last_high, RING, NEXT)
     filtered = call(
@@ -282,10 +289,16 @@
         [low, high, applied, next_low, next_high, last_low, last_high],
         flops=400_000_000,
     )
+    far_part = call(
+        far_low_body,
+        jax.ShapeDtypeStruct((32, 128), F32),
+        [low, high, applied, far_low],
+        flops=400_000_000,
+    )
     copies = call(
         far_gram_body,
         jax.ShapeDtypeStruct((16, 16, 128), F32),
-        [place, low, high, applied, far_low, far_high, near],
+        [place, low, high, applied, far_high, near, far_part],
         [SM] + [VM] * 6,
     )
     parts = lax.all_to_all(copies, ("xl",) + ROWS, split_axis=0, concat_axis=0, tiled=True)

time: 113 us -> 111 us (0.982)
  waiting for transfers between devices: 40.4 us -> 39.2 us
    ppermute x1, waiting for transfers between devices: 1.95 us -> 0.01 us  [local(): last_low = lax.ppermute(low, RING, NEXT)]
    ppermute x1, starting transfers between devices: 1.56 us -> 0.01 us  [local(): far_high = lax.ppermute(last_high, RING, NEXT)]
    ppermute x4, waiting for transfers between devices: 2.56 us -> 1.26 us  [step(): lax.ppermute(low, 'z', DOWN)]
    ppermute x1, waiting for transfers between devices: 3.14 us -> 4.42 us  [local(): next_low = lax.ppermute(low, RING, LAST)]
    ppermute x4, waiting for transfers between devices: 15.4 us -> 16.5 us  [step(): lax.ppermute(high, 'z', UP)]
    pallas_call x14 -> x15, Pallas kernels: 14.9 us -> 15 us  [call(): pl.pallas_call(body, out_shape=outs, in_specs=specs or [VM] * len(inputs)...]
  transfers between devices with their start and end apart: 25 -> 25, of which waited for: 12 -> 11; matrix products, arithmetic and copies ran while one was open for 0% -> 0% of each run, Pallas kernels for 7% -> 8%
where the time goes in v5:
time: 111 us; the launch traced here: 110 us
  starting transfers between devices  41.9 us (38%)
  waiting for transfers between devices  39.2 us (35%)
  Pallas kernels  15 us (14%)
  blocking collectives  12.3 us (11%)
    ppermute x4, waiting for transfers between devices, step(): lax.ppermute(high, 'z', UP)  16.5 us
    pallas_call x15, Pallas kernels, call(): pl.pallas_call(body, out_shape=outs, in_specs=specs or [VM] * len(inputs)...  15 us
    all_to_all x1, blocking collectives, local(): lax.all_to_all(copies, ('xl',) + ROWS, split_axis=0, concat_axis=0, tiled...  12.3 us
    ppermute x4, starting transfers between devices, step(): lax.ppermute(full, ROWS, DOWN)  11.8 us
    ppermute x4, starting transfers between devices, step(): lax.ppermute(low, 'z', DOWN)  10.5 us
    all_to_all x1, waiting for transfers between devices, local(): parts = lax.all_to_all(copies, 'z', split_axis=0, concat_axis=0, tiled=True)  7.69 us
    ppermute x1, waiting for transfers between devices, local(): other_field = lax.ppermute(own_field, 'xl', SWAP)  6.93 us
    ppermute x4, starting transfers between devices, step(): lax.ppermute(high, 'z', UP)  6.11 us
  transfers between devices with their start and end apart: 25, of which 11 were waited for; matrix products, arithmetic and copies ran while one was open for 0% of the time, Pallas kernels for 8%

profile of v5, /device:TPU:4, one launch (start us, length us, event | category | flops | bytes accessed | tf_op | source)
XLA Modules:
  0.0 110.5 jit_solution(9818818582984137845)
XLA Ops:
  0.7 1.0 constant_dynamic-slice_fusion
  1.7 1.3 %collective-permute-start = (f32[576,128]{1,0:T(8,128)S(1)}, f32[576,128]{1,0:T(8,128)S(1)}, u32[]{:S(2)}, u32[]{:S(2)}) collective-permute-start(f32[576,128]{1,0:T(8,128)S(1)} %constant_dynamic-slice_fusion), channel_id=1, source_target_pairs={{0,16},{16,0},{1,17},{17,1},{2,18},{18,2},{3,19},{19,3},{4,20},{20... | collective-permute-start | bytes 884744 | tf_op jit(solution)/shard_map/ppermute | solution.py:234
  3.1 0.9 collective-permute-start.1
  4.0 0.1 pad_add_fusion.place
  4.0 6.9 %collective-permute-done.1.other_field = f32[36,128]{1,0:T(8,128)S(1)} collective-permute-done((f32[36,128]{1,0:T(8,128)S(1)}, f32[36,128]{1,0:T(8,128)S(1)}, u32[]{:S(2)}, u32[]{:S(2)}) %collective-permute-start.1) | collective-permute-done | bytes 18464 | tf_op jit(solution)/shard_map/ppermute | solution.py:235
  11.0 0.6 shard_map.49
  11.6 0.0 collective-permute-start.4
  11.7 2.9 %collective-permute-start.5 = (f32[12,12,8,128]{3,2,1,0:T(8,128)S(1)}, f32[12,12,8,128]{3,2,1,0:T(8,128)S(1)}, u32[]{:S(2)}, u32[]{:S(2)}) collective-permute-start(f32[12,12,8,128]{3,2,1,0:T(8,128)S(1)} %get-tuple-element.19.refs_0_.refs_2_), channel_id=1, source_target_pairs={{0,14},{2,0},{4,2},{6,4},{8,6},{10,8},{12,10},{14,12},{1,15},{3,1}... | collective-permute-start | bytes 1769480 | tf_op jit(solution)/shard_map/ppermute | solution.py:247
  14.6 1.9 %collective-permute-start.2 = (f32[6,12,8,128]{3,2,1,0:T(8,128)S(1)}, f32[6,12,8,128]{3,2,1,0:T(8,128)S(1)}, u32[]{:S(2)}, u32[]{:S(2)}) collective-permute-start(f32[6,12,8,128]{3,2,1,0:T(8,128)S(1)} %get-tuple-element.21), channel_id=1, source_target_pairs={{0,32},{32,64},{64,96},{96,128},{128,160},{160,192},{192,224},{224... | collective-permute-start | bytes 884744 | tf_op jit(solution)/shard_map/ppermute | solution.py:248
  16.5 3.9 %collective-permute-start.3 = (f32[6,12,8,128]{3,2,1,0:T(8,128)S(1)}, f32[6,12,8,128]{3,2,1,0:T(8,128)S(1)}, u32[]{:S(2)}, u32[]{:S(2)}) collective-permute-start(f32[6,12,8,128]{3,2,1,0:T(8,128)S(1)} %get-tuple-element.22), channel_id=1, source_target_pairs={{0,224},{32,0},{64,32},{96,64},{128,96},{160,128},{192,160},{224,1... | collective-permute-start | bytes 884744 | tf_op jit(solution)/shard_map/ppermute | solution.py:249
  20.5 0.1 add_convert_fusion.refs_0_
  20.5 1.0 shard_map.50.refs_1_
  21.6 4.8 %collective-permute-done.2.refs_2_ = f32[6,12,8,128]{3,2,1,0:T(8,128)S(1)} collective-permute-done((f32[6,12,8,128]{3,2,1,0:T(8,128)S(1)}, f32[6,12,8,128]{3,2,1,0:T(8,128)S(1)}, u32[]{:S(2)}, u32[]{:S(2)}) %collective-permute-start.2) | collective-permute-done | bytes 294944 | tf_op jit(solution)/shard_map/ppermute | solution.py:248
  26.4 0.0 collective-permute-done.3.refs_3_
  26.4 0.0 collective-permute-done.4.refs_4_
  26.4 0.0 collective-permute-done.5.refs_5_
  26.4 1.0 shard_map.51
  27.4 0.0 collective-permute-start.8
  27.4 2.9 %collective-permute-start.9 = (f32[12,12,8,128]{3,2,1,0:T(8,128)S(1)}, f32[12,12,8,128]{3,2,1,0:T(8,128)S(1)}, u32[]{:S(2)}, u32[]{:S(2)}) collective-permute-start(f32[12,12,8,128]{3,2,1,0:T(8,128)S(1)} %get-tuple-element.23.refs_0_.refs_2_), channel_id=1, source_target_pairs={{0,14},{2,0},{4,2},{6,4},{8,6},{10,8},{12,10},{14,12},{1,15},{3,1}... | collective-permute-start | bytes 1769480 | tf_op jit(solution)/shard_map/ppermute | solution.py:247
  30.3 0.0 collective-permute-start.6
  30.3 3.2 %collective-permute-start.7 = (f32[6,12,8,128]{3,2,1,0:T(8,128)S(1)}, f32[6,12,8,128]{3,2,1,0:T(8,128)S(1)}, u32[]{:S(2)}, u32[]{:S(2)}) collective-permute-start(f32[6,12,8,128]{3,2,1,0:T(8,128)S(1)} %get-tuple-element.25), channel_id=1, source_target_pairs={{0,224},{32,0},{64,32},{96,64},{128,96},{160,128},{192,160},{224,1... | collective-permute-start | bytes 884744 | tf_op jit(solution)/shard_map/ppermute | solution.py:249
  33.6 1.1 %shard_map.52.refs_1_ = f32[12,12,8,128]{3,2,1,0:T(8,128)S(1)} custom-call(f32[12,12,8,128]{3,2,1,0:T(8,128)S(1)} %get-tuple-element.23.refs_0_.refs_2_, f32[12,6,8,128]{3,2,1,0:T(8,128)S(1)} %get-tuple-element.20.refs_1_, f32[12,12,8,128]{3,2,1,0:T(8,128)S(1)} %get-tuple-element.19.refs_0_.refs_2_), custom_call_target="tpu_custom_call" | custom-call | flops 400000000 | bytes 2000000 | tf_op jit(solution)/shard_map/pallas_call | solution.py:32
  34.7 4.5 %collective-permute-done.6.refs_2_ = f32[6,12,8,128]{3,2,1,0:T(8,128)S(1)} collective-permute-done((f32[6,12,8,128]{3,2,1,0:T(8,128)S(1)}, f32[6,12,8,128]{3,2,1,0:T(8,128)S(1)}, u32[]{:S(2)}, u32[]{:S(2)}) %collective-permute-start.6) | collective-permute-done | bytes 294944 | tf_op jit(solution)/shard_map/ppermute | solution.py:248
  39.2 0.0 collective-permute-done.7.refs_3_
  39.2 0.0 collective-permute-done.8.refs_4_
  39.2 0.0 collective-permute-done.9.refs_5_
  39.2 1.0 shard_map.53
  40.2 0.0 collective-permute-start.12
  40.2 2.9 %collective-permute-start.13 = (f32[12,12,8,128]{3,2,1,0:T(8,128)S(1)}, f32[12,12,8,128]{3,2,1,0:T(8,128)S(1)}, u32[]{:S(2)}, u32[]{:S(2)}) collective-permute-start(f32[12,12,8,128]{3,2,1,0:T(8,128)S(1)} %get-tuple-element.26.refs_0_), channel_id=1, source_target_pairs={{0,14},{2,0},{4,2},{6,4},{8,6},{10,8},{12,10},{14,12},{1,15},{3,1}... | collective-permute-start | bytes 1769480 | tf_op jit(solution)/shard_map/ppermute | solution.py:247
  43.2 2.5 %collective-permute-start.10 = (f32[6,12,8,128]{3,2,1,0:T(8,128)S(1)}, f32[6,12,8,128]{3,2,1,0:T(8,128)S(1)}, u32[]{:S(2)}, u32[]{:S(2)}) collective-permute-start(f32[6,12,8,128]{3,2,1,0:T(8,128)S(1)} %get-tuple-element.27), channel_id=1, source_target_pairs={{0,32},{32,64},{64,96},{96,128},{128,160},{160,192},{192,224},{224... | collective-permute-start | bytes 884744 | tf_op jit(solution)/shard_map/ppermute | solution.py:248
  45.6 0.8 collective-permute-start.11
  46.4 1.1 %shard_map.54.refs_1_ = f32[12,12,8,128]{3,2,1,0:T(8,128)S(1)} custom-call(f32[12,12,8,128]{3,2,1,0:T(8,128)S(1)} %get-tuple-element.26.refs_0_, f32[12,6,8,128]{3,2,1,0:T(8,128)S(1)} %get-tuple-element.20.refs_1_, f32[12,12,8,128]{3,2,1,0:T(8,128)S(1)} %get-tuple-element.23.refs_0_.refs_2_), custom_call_target="tpu_custom_call" | custom-call | flops 400000000 | bytes 2000000 | tf_op jit(solution)/shard_map/pallas_call | solution.py:32
  47.5 4.2 %collective-permute-done.10.refs_2_ = f32[6,12,8,128]{3,2,1,0:T(8,128)S(1)} collective-permute-done((f32[6,12,8,128]{3,2,1,0:T(8,128)S(1)}, f32[6,12,8,128]{3,2,1,0:T(8,128)S(1)}, u32[]{:S(2)}, u32[]{:S(2)}) %collective-permute-start.10) | collective-permute-done | bytes 294944 | tf_op jit(solution)/shard_map/ppermute | solution.py:248
  51.7 1.0 collective-permute-done.11.refs_3_
  52.7 0.0 collective-permute-done.12.refs_4_
  52.7 0.0 collective-permute-done.13.refs_5_
  52.7 1.0 shard_map.55
  53.7 0.6 collective-permute-start.14
  54.3 1.5 %collective-permute-start.15 = (f32[6,12,8,128]{3,2,1,0:T(8,128)S(1)}, f32[6,12,8,128]{3,2,1,0:T(8,128)S(1)}, u32[]{:S(2)}, u32[]{:S(2)}) collective-permute-start(f32[6,12,8,128]{3,2,1,0:T(8,128)S(1)} %get-tuple-element.30.high), channel_id=1, source_target_pairs={{0,16},{16,1},{1,17},{17,0},{2,18},{18,3},{3,19},{19,2},{4,20},{20... | collective-permute-start | bytes 884744 | tf_op jit(solution)/shard_map/ppermute | solution.py:271
  55.8 0.5 collective-permute-start.16
  56.3 0.0 collective-permute-start.20
  56.3 3.0 %collective-permute-start.21 = (f32[12,12,8,128]{3,2,1,0:T(8,128)S(1)}, f32[12,12,8,128]{3,2,1,0:T(8,128)S(1)}, u32[]{:S(2)}, u32[]{:S(2)}) collective-permute-start(f32[12,12,8,128]{3,2,1,0:T(8,128)S(1)} %get-tuple-element.31.refs_0_), channel_id=1, source_target_pairs={{0,14},{2,0},{4,2},{6,4},{8,6},{10,8},{12,10},{14,12},{1,15},{3,1}... | collective-permute-start | bytes 1769480 | tf_op jit(solution)/shard_map/ppermute | solution.py:247
  59.3 4.4 %collective-permute-done.14.next_low = f32[6,12,8,128]{3,2,1,0:T(8,128)S(1)} collective-permute-done((f32[6,12,8,128]{3,2,1,0:T(8,128)S(1)}, f32[6,12,8,128]{3,2,1,0:T(8,128)S(1)}, u32[]{:S(2)}, u32[]{:S(2)}) %collective-permute-start.14) | collective-permute-done | bytes 294944 | tf_op jit(solution)/shard_map/ppermute | solution.py:270
  63.7 2.4 %collective-permute-start.17 = (f32[6,12,8,128]{3,2,1,0:T(8,128)S(1)}, f32[6,12,8,128]{3,2,1,0:T(8,128)S(1)}, u32[]{:S(2)}, u32[]{:S(2)}) collective-permute-start(f32[6,12,8,128]{3,2,1,0:T(8,128)S(1)} %get-tuple-element.29.low), channel_id=1, source_target_pairs={{0,16},{16,1},{1,17},{17,0},{2,18},{18,3},{3,19},{19,2},{4,20},{20... | collective-permute-start | bytes 884744 | tf_op jit(solution)/shard_map/ppermute | solution.py:273
  66.1 1.7 %collective-permute-start.18 = (f32[6,12,8,128]{3,2,1,0:T(8,128)S(1)}, f32[6,12,8,128]{3,2,1,0:T(8,128)S(1)}, u32[]{:S(2)}, u32[]{:S(2)}) collective-permute-start(f32[6,12,8,128]{3,2,1,0:T(8,128)S(1)} %get-tuple-element.30.high), channel_id=1, source_target_pairs={{0,32},{32,64},{64,96},{96,128},{128,160},{160,192},{192,224},{224... | collective-permute-start | bytes 884744 | tf_op jit(solution)/shard_map/ppermute | solution.py:248
  67.9 2.6 %collective-permute-start.19 = (f32[6,12,8,128]{3,2,1,0:T(8,128)S(1)}, f32[6,12,8,128]{3,2,1,0:T(8,128)S(1)}, u32[]{:S(2)}, u32[]{:S(2)}) collective-permute-start(f32[6,12,8,128]{3,2,1,0:T(8,128)S(1)} %get-tuple-element.29.low), channel_id=1, source_target_pairs={{0,224},{32,0},{64,32},{96,64},{128,96},{160,128},{192,160},{224,1... | collective-permute-start | bytes 884744 | tf_op jit(solution)/shard_map/ppermute | solution.py:249
  70.4 0.0 collective-permute-done.17.last_low
  70.4 0.5 collective-permute-start.23
  71.0 3.1 %collective-permute-done.18.refs_2_ = f32[6,12,8,128]{3,2,1,0:T(8,128)S(1)} collective-permute-done((f32[6,12,8,128]{3,2,1,0:T(8,128)S(1)}, f32[6,12,8,128]{3,2,1,0:T(8,128)S(1)}, u32[]{:S(2)}, u32[]{:S(2)}) %collective-permute-start.18) | collective-permute-done | bytes 294944 | tf_op jit(solution)/shard_map/ppermute | solution.py:248
  74.0 0.0 collective-permute-start.22
  74.1 1.1 shard_map.57.refs_1_
  75.1 0.3 collective-permute-done.19.refs_3_
  75.4 1.0 shard_map.58.applied
  76.4 1.5 %shard_map.59.near = f32[32,128]{1,0:T(8,128)S(1)} custom-call(f32[6,12,8,128]{3,2,1,0:T(8,128)S(1)} %get-tuple-element.29.low, f32[6,12,8,128]{3,2,1,0:T(8,128)S(1)} %get-tuple-element.30.high, f32[12,12,8,128]{3,2,1,0:T(8,128)S(1)} %shard_map.58.applied, f32[6,12,8,128]{3,2,1,0:T(8,128)S(1)} %collective-permute-done.14.next_low, ...), custom_call_target="tpu_custom_call" | custom-call | flops 400000000 | bytes 2000000 | tf_op jit(solution)/shard_map/pallas_call | solution.py:32
  77.9 0.4 collective-permute-done.23.far_low
  78.3 0.6 shard_map.60.far_part
  78.9 1.9 %collective-permute-done.22.far_high = f32[6,12,8,128]{3,2,1,0:T(8,128)S(1)} collective-permute-done((f32[6,12,8,128]{3,2,1,0:T(8,128)S(1)}, f32[6,12,8,128]{3,2,1,0:T(8,128)S(1)}, u32[]{:S(2)}, u32[]{:S(2)}) %collective-permute-start.22) | collective-permute-done | bytes 294944 | tf_op jit(solution)/shard_map/ppermute | solution.py:276
  80.8 1.3 %shard_map.61 = f32[16,16,128]{2,1,0:T(8,128)S(1)} custom-call(s32[2]{0:T(128)S(1)} %pad_add_fusion.place, f32[6,12,8,128]{3,2,1,0:T(8,128)S(1)} %get-tuple-element.29.low, f32[6,12,8,128]{3,2,1,0:T(8,128)S(1)} %get-tuple-element.30.high, f32[12,12,8,128]{3,2,1,0:T(8,128)S(1)} %shard_map.58.applied, f32[6,12,8,128]{3,2,1,0:T(8,128)S(1)} %collective-permute-done.22.far_high, ...), custom_call_target="tpu_custom_call" | custom-call | flops 1000000 | bytes 2000000 | tf_op jit(solution)/shard_map/pallas_call | solution.py:32
  82.1 12.3 %all_to_all.10.parts = f32[16,16,128]{2,1,0:T(8,128)S(1)} all-to-all(f32[16,16,128]{2,1,0:T(8,128)S(1)} %shard_map.61), channel_id=1, replica_groups=mesh['z'=8,'xl'=2,'y'=4,'core'=2,'xh'=2] {'xl','y','core'}, dimensions={0} | all-to-all | bytes 262144 | tf_op jit(solution)/shard_map/all_to_all | solution.py:304
  94.4 0.7 shard_map.62
  95.0 5.7 %all-to-all-start.1 = ((f32[8,32,128]{2,1,0:T(8,128)}), f32[8,32,128]{2,1,0:T(8,128)S(1)}, u32[]{:S(2)}, u32[]{:S(2)}) async-start(f32[8,32,128]{2,1,0:T(8,128)} %shard_map.62), calls=%async_computation.1 | async-start | bytes 262144 | tf_op jit(solution)/shard_map/all_to_all | solution.py:306
  100.7 1.4 %shard_map.56 = f32[1152,128]{1,0:T(8,128)} custom-call(s32[2]{0:T(128)S(1)} %pad_add_fusion.place, f32[6,12,8,128]{3,2,1,0:T(8,128)S(1)} %get-tuple-element.29.low, f32[6,12,8,128]{3,2,1,0:T(8,128)S(1)} %get-tuple-element.30.high, f32[6,12,8,128]{3,2,1,0:T(8,128)S(1)} %collective-permute-done.14.next_low, ...), custom_call_target="tpu_custom_call" | custom-call | flops 400000000 | bytes 2000000 | tf_op jit(solution)/shard_map/pallas_call | solution.py:32
  102.1 7.7 %all-to-all-done.1.parts = f32[8,32,128]{2,1,0:T(8,128)S(1)} async-done(((f32[8,32,128]{2,1,0:T(8,128)}), f32[8,32,128]{2,1,0:T(8,128)S(1)}, u32[]{:S(2)}, u32[]{:S(2)}) %all-to-all-start.1) | async-done | bytes 131104 | tf_op jit(solution)/shard_map/all_to_all | solution.py:306
  109.8 0.7 shard_map.63
  (11 shorter events, 0.1 us)
Async XLA Ops:
  0.6 10.4 %copy-start = (f32[32,1,6,6,128]{4,1,3,2,0:T(1,128)S(1)}, f32[32,1,6,6,128]{4,1,3,2,0:T(1,128)}, u32[]{:S(2)}) copy-start(f32[32,1,6,6,128]{4,1,3,2,0:T(1,128)} %param.2) | copy-start | bytes 1769476
  0.6 2.3 %copy-start.1 = (f32[1,6,6,128]{3,0,2,1:T(1,128)S(1)}, f32[1,6,6,128]{3,0,2,1:T(1,128)}, u32[]{:S(2)}) copy-start(f32[1,6,6,128]{3,0,2,1:T(1,128)} %param.3) | copy-start | bytes 55300
  1.7 9.3 %collective-permute-start = (f32[576,128]{1,0:T(8,128)S(1)}, f32[576,128]{1,0:T(8,128)S(1)}, u32[]{:S(2)}, u32[]{:S(2)}) collective-permute-start(f32[576,128]{1,0:T(8,128)S(1)} %constant_dynamic-slice_fusion), channel_id=1, source_target_pairs={{0,16},{16,0},{1,17},{17,1},{2,18},{18,2},{3,19},{19,3},{4,20},{20... | collective-permute-start | bytes 884744 | tf_op jit(solution)/shard_map/ppermute | solution.py:234
  3.1 7.9 %collective-permute-start.1 = (f32[36,128]{1,0:T(8,128)S(1)}, f32[36,128]{1,0:T(8,128)S(1)}, u32[]{:S(2)}, u32[]{:S(2)}) collective-permute-start(f32[36,128]{1,0:T(8,128)S(1)} %reshape.16.own_field), channel_id=1, source_target_pairs={{0,16},{16,0},{1,17},{17,1},{2,18},{18,2},{3,19},{19,3},{4,20},{20... | collective-permute-start | bytes 55304 | tf_op jit(solution)/shard_map/ppermute | solution.py:235
  11.6 14.7 %collective-permute-start.4 = (f32[12,12,8,128]{3,2,1,0:T(8,128)S(1)}, f32[12,12,8,128]{3,2,1,0:T(8,128)S(1)}, u32[]{:S(2)}, u32[]{:S(2)}) collective-permute-start(f32[12,12,8,128]{3,2,1,0:T(8,128)S(1)} %get-tuple-element.19.refs_0_.refs_2_), channel_id=1, source_target_pairs={{0,2},{2,4},{4,6},{6,8},{8,10},{10,12},{12,14},{14,0},{1,3},{3,5},... | collective-permute-start | bytes 1769480 | tf_op jit(solution)/shard_map/ppermute | solution.py:246
  11.7 14.7 %collective-permute-start.5 = (f32[12,12,8,128]{3,2,1,0:T(8,128)S(1)}, f32[12,12,8,128]{3,2,1,0:T(8,128)S(1)}, u32[]{:S(2)}, u32[]{:S(2)}) collective-permute-start(f32[12,12,8,128]{3,2,1,0:T(8,128)S(1)} %get-tuple-element.19.refs_0_.refs_2_), channel_id=1, source_target_pairs={{0,14},{2,0},{4,2},{6,4},{8,6},{10,8},{12,10},{14,12},{1,15},{3,1}... | collective-permute-start | bytes 1769480 | tf_op jit(solution)/shard_map/ppermute | solution.py:247
  14.6 11.8 %collective-permute-start.2 = (f32[6,12,8,128]{3,2,1,0:T(8,128)S(1)}, f32[6,12,8,128]{3,2,1,0:T(8,128)S(1)}, u32[]{:S(2)}, u32[]{:S(2)}) collective-permute-start(f32[6,12,8,128]{3,2,1,0:T(8,128)S(1)} %get-tuple-element.21), channel_id=1, source_target_pairs={{0,32},{32,64},{64,96},{96,128},{128,160},{160,192},{192,224},{224... | collective-permute-start | bytes 884744 | tf_op jit(solution)/shard_map/ppermute | solution.py:248
  16.5 9.8 %collective-permute-start.3 = (f32[6,12,8,128]{3,2,1,0:T(8,128)S(1)}, f32[6,12,8,128]{3,2,1,0:T(8,128)S(1)}, u32[]{:S(2)}, u32[]{:S(2)}) collective-permute-start(f32[6,12,8,128]{3,2,1,0:T(8,128)S(1)} %get-tuple-element.22), channel_id=1, source_target_pairs={{0,224},{32,0},{64,32},{96,64},{128,96},{160,128},{192,160},{224,1... | collective-permute-start | bytes 884744 | tf_op jit(solution)/shard_map/ppermute | solution.py:249
  27.4 11.8 %collective-permute-start.8 = (f32[12,12,8,128]{3,2,1,0:T(8,128)S(1)}, f32[12,12,8,128]{3,2,1,0:T(8,128)S(1)}, u32[]{:S(2)}, u32[]{:S(2)}) collective-permute-start(f32[12,12,8,128]{3,2,1,0:T(8,128)S(1)} %get-tuple-element.23.refs_0_.refs_2_), channel_id=1, source_target_pairs={{0,2},{2,4},{4,6},{6,8},{8,10},{10,12},{12,14},{14,0},{1,3},{3,5},... | collective-permute-start | bytes 1769480 | tf_op jit(solution)/shard_map/ppermute | solution.py:246
  27.4 11.8 %collective-permute-start.9 = (f32[12,12,8,128]{3,2,1,0:T(8,128)S(1)}, f32[12,12,8,128]{3,2,1,0:T(8,128)S(1)}, u32[]{:S(2)}, u32[]{:S(2)}) collective-permute-start(f32[12,12,8,128]{3,2,1,0:T(8,128)S(1)} %get-tuple-element.23.refs_0_.refs_2_), channel_id=1, source_target_pairs={{0,14},{2,0},{4,2},{6,4},{8,6},{10,8},{12,10},{14,12},{1,15},{3,1}... | collective-permute-start | bytes 1769480 | tf_op jit(solution)/shard_map/ppermute | solution.py:247
  30.3 8.9 %collective-permute-start.6 = (f32[6,12,8,128]{3,2,1,0:T(8,128)S(1)}, f32[6,12,8,128]{3,2,1,0:T(8,128)S(1)}, u32[]{:S(2)}, u32[]{:S(2)}) collective-permute-start(f32[6,12,8,128]{3,2,1,0:T(8,128)S(1)} %get-tuple-element.24), channel_id=1, source_target_pairs={{0,32},{32,64},{64,96},{96,128},{128,160},{160,192},{192,224},{224... | collective-permute-start | bytes 884744 | tf_op jit(solution)/shard_map/ppermute | solution.py:248
  30.3 8.9 %collective-permute-start.7 = (f32[6,12,8,128]{3,2,1,0:T(8,128)S(1)}, f32[6,12,8,128]{3,2,1,0:T(8,128)S(1)}, u32[]{:S(2)}, u32[]{:S(2)}) collective-permute-start(f32[6,12,8,128]{3,2,1,0:T(8,128)S(1)} %get-tuple-element.25), channel_id=1, source_target_pairs={{0,224},{32,0},{64,32},{96,64},{128,96},{160,128},{192,160},{224,1... | collective-permute-start | bytes 884744 | tf_op jit(solution)/shard_map/ppermute | solution.py:249
  40.2 12.5 %collective-permute-start.12 = (f32[12,12,8,128]{3,2,1,0:T(8,128)S(1)}, f32[12,12,8,128]{3,2,1,0:T(8,128)S(1)}, u32[]{:S(2)}, u32[]{:S(2)}) collective-permute-start(f32[12,12,8,128]{3,2,1,0:T(8,128)S(1)} %get-tuple-element.26.refs_0_), channel_id=1, source_target_pairs={{0,2},{2,4},{4,6},{6,8},{8,10},{10,12},{12,14},{14,0},{1,3},{3,5},... | collective-permute-start | bytes 1769480 | tf_op jit(solution)/shard_map/ppermute | solution.py:246
  40.2 12.5 %collective-permute-start.13 = (f32[12,12,8,128]{3,2,1,0:T(8,128)S(1)}, f32[12,12,8,128]{3,2,1,0:T(8,128)S(1)}, u32[]{:S(2)}, u32[]{:S(2)}) collective-permute-start(f32[12,12,8,128]{3,2,1,0:T(8,128)S(1)} %get-tuple-element.26.refs_0_), channel_id=1, source_target_pairs={{0,14},{2,0},{4,2},{6,4},{8,6},{10,8},{12,10},{14,12},{1,15},{3,1}... | collective-permute-start | bytes 1769480 | tf_op jit(solution)/shard_map/ppermute | solution.py:247
  43.2 8.6 %collective-permute-start.10 = (f32[6,12,8,128]{3,2,1,0:T(8,128)S(1)}, f32[6,12,8,128]{3,2,1,0:T(8,128)S(1)}, u32[]{:S(2)}, u32[]{:S(2)}) collective-permute-start(f32[6,12,8,128]{3,2,1,0:T(8,128)S(1)} %get-tuple-element.27), channel_id=1, source_target_pairs={{0,32},{32,64},{64,96},{96,128},{128,160},{160,192},{192,224},{224... | collective-permute-start | bytes 884744 | tf_op jit(solution)/shard_map/ppermute | solution.py:248
  45.6 7.1 %collective-permute-start.11 = (f32[6,12,8,128]{3,2,1,0:T(8,128)S(1)}, f32[6,12,8,128]{3,2,1,0:T(8,128)S(1)}, u32[]{:S(2)}, u32[]{:S(2)}) collective-permute-start(f32[6,12,8,128]{3,2,1,0:T(8,128)S(1)} %get-tuple-element.28), channel_id=1, source_target_pairs={{0,224},{32,0},{64,32},{96,64},{128,96},{160,128},{192,160},{224,1... | collective-permute-start | bytes 884744 | tf_op jit(solution)/shard_map/ppermute | solution.py:249
  53.7 10.0 %collective-permute-start.14 = (f32[6,12,8,128]{3,2,1,0:T(8,128)S(1)}, f32[6,12,8,128]{3,2,1,0:T(8,128)S(1)}, u32[]{:S(2)}, u32[]{:S(2)}) collective-permute-start(f32[6,12,8,128]{3,2,1,0:T(8,128)S(1)} %get-tuple-element.29.low), channel_id=1, source_target_pairs={{0,17},{16,0},{1,16},{17,1},{2,19},{18,2},{3,18},{19,3},{4,21},{20... | collective-permute-start | bytes 884744 | tf_op jit(solution)/shard_map/ppermute | solution.py:270
  54.3 11.8 %collective-permute-start.15 = (f32[6,12,8,128]{3,2,1,0:T(8,128)S(1)}, f32[6,12,8,128]{3,2,1,0:T(8,128)S(1)}, u32[]{:S(2)}, u32[]{:S(2)}) collective-permute-start(f32[6,12,8,128]{3,2,1,0:T(8,128)S(1)} %get-tuple-element.30.high), channel_id=1, source_target_pairs={{0,16},{16,1},{1,17},{17,0},{2,18},{18,3},{3,19},{19,2},{4,20},{20... | collective-permute-start | bytes 884744 | tf_op jit(solution)/shard_map/ppermute | solution.py:271
  55.8 12.1 %collective-permute-start.16 = (f32[6,12,8,128]{3,2,1,0:T(8,128)S(1)}, f32[6,12,8,128]{3,2,1,0:T(8,128)S(1)}, u32[]{:S(2)}, u32[]{:S(2)}) collective-permute-start(f32[6,12,8,128]{3,2,1,0:T(8,128)S(1)} %get-tuple-element.30.high), channel_id=1, source_target_pairs={{0,17},{16,0},{1,16},{17,1},{2,19},{18,2},{3,18},{19,3},{4,21},{20... | collective-permute-start | bytes 884744 | tf_op jit(solution)/shard_map/ppermute | solution.py:272
  56.3 19.1 %collective-permute-start.20 = (f32[12,12,8,128]{3,2,1,0:T(8,128)S(1)}, f32[12,12,8,128]{3,2,1,0:T(8,128)S(1)}, u32[]{:S(2)}, u32[]{:S(2)}) collective-permute-start(f32[12,12,8,128]{3,2,1,0:T(8,128)S(1)} %get-tuple-element.31.refs_0_), channel_id=1, source_target_pairs={{0,2},{2,4},{4,6},{6,8},{8,10},{10,12},{12,14},{14,0},{1,3},{3,5},... | collective-permute-start | bytes 1769480 | tf_op jit(solution)/shard_map/ppermute | solution.py:246
  56.3 19.1 %collective-permute-start.21 = (f32[12,12,8,128]{3,2,1,0:T(8,128)S(1)}, f32[12,12,8,128]{3,2,1,0:T(8,128)S(1)}, u32[]{:S(2)}, u32[]{:S(2)}) collective-permute-start(f32[12,12,8,128]{3,2,1,0:T(8,128)S(1)} %get-tuple-element.31.refs_0_), channel_id=1, source_target_pairs={{0,14},{2,0},{4,2},{6,4},{8,6},{10,8},{12,10},{14,12},{1,15},{3,1}... | collective-permute-start | bytes 1769480 | tf_op jit(solution)/shard_map/ppermute | solution.py:247
  63.7 6.7 %collective-permute-start.17 = (f32[6,12,8,128]{3,2,1,0:T(8,128)S(1)}, f32[6,12,8,128]{3,2,1,0:T(8,128)S(1)}, u32[]{:S(2)}, u32[]{:S(2)}) collective-permute-start(f32[6,12,8,128]{3,2,1,0:T(8,128)S(1)} %get-tuple-element.29.low), channel_id=1, source_target_pairs={{0,16},{16,1},{1,17},{17,0},{2,18},{18,3},{3,19},{19,2},{4,20},{20... | collective-permute-start | bytes 884744 | tf_op jit(solution)/shard_map/ppermute | solution.py:273
  66.1 7.9 %collective-permute-start.18 = (f32[6,12,8,128]{3,2,1,0:T(8,128)S(1)}, f32[6,12,8,128]{3,2,1,0:T(8,128)S(1)}, u32[]{:S(2)}, u32[]{:S(2)}) collective-permute-start(f32[6,12,8,128]{3,2,1,0:T(8,128)S(1)} %get-tuple-element.30.high), channel_id=1, source_target_pairs={{0,32},{32,64},{64,96},{96,128},{128,160},{160,192},{192,224},{224... | collective-permute-start | bytes 884744 | tf_op jit(solution)/shard_map/ppermute | solution.py:248
  67.9 7.6 %collective-permute-start.19 = (f32[6,12,8,128]{3,2,1,0:T(8,128)S(1)}, f32[6,12,8,128]{3,2,1,0:T(8,128)S(1)}, u32[]{:S(2)}, u32[]{:S(2)}) collective-permute-start(f32[6,12,8,128]{3,2,1,0:T(8,128)S(1)} %get-tuple-element.29.low), channel_id=1, source_target_pairs={{0,224},{32,0},{64,32},{96,64},{128,96},{160,128},{192,160},{224,1... | collective-permute-start | bytes 884744 | tf_op jit(solution)/shard_map/ppermute | solution.py:249
  70.4 7.8 %collective-permute-start.23 = (f32[6,12,8,128]{3,2,1,0:T(8,128)S(1)}, f32[6,12,8,128]{3,2,1,0:T(8,128)S(1)}, u32[]{:S(2)}, u32[]{:S(2)}) collective-permute-start(f32[6,12,8,128]{3,2,1,0:T(8,128)S(1)} %collective-permute-done.14.next_low), channel_id=1, source_target_pairs={{0,17},{16,0},{1,16},{17,1},{2,19},{18,2},{3,18},{19,3},{4,21},{20... | collective-permute-start | bytes 884744 | tf_op jit(solution)/shard_map/ppermute | solution.py:275
  74.0 6.7 %collective-permute-start.22 = (f32[6,12,8,128]{3,2,1,0:T(8,128)S(1)}, f32[6,12,8,128]{3,2,1,0:T(8,128)S(1)}, u32[]{:S(2)}, u32[]{:S(2)}) collective-permute-start(f32[6,12,8,128]{3,2,1,0:T(8,128)S(1)} %collective-permute-done.15.last_high), channel_id=1, source_target_pairs={{0,16},{16,1},{1,17},{17,0},{2,18},{18,3},{3,19},{19,2},{4,20},{20... | collective-permute-start | bytes 884744 | tf_op jit(solution)/shard_map/ppermute | solution.py:276
  95.0 14.8 %all-to-all-start.1 = ((f32[8,32,128]{2,1,0:T(8,128)}), f32[8,32,128]{2,1,0:T(8,128)S(1)}, u32[]{:S(2)}, u32[]{:S(2)}) async-start(f32[8,32,128]{2,1,0:T(8,128)} %shard_map.62), calls=%async_computation.1 | async-start | bytes 262144 | tf_op jit(solution)/shard_map/all_to_all | solution.py:306

commit v6 on v5

--- a/solution.py
+++ b/solution.py
@@ -94,41 +94,53 @@
                 acc[x, n] = total
 
 
-def edge_body(alpha, inside, acc, before_x, after_x, before_y, after_y, full, *halves):
+def edge_y_body(alpha, inside, acc, before, after, out):
     scaled = [-0.5 * alpha * w for w in weights]
-    from_x = [[inside[i] * F32(s) for s in scaled] for i in range(2)]
-    from_y = [[inside[2 + i] * F32(s) for s in scaled] for i in range(2)]
+    lower = [inside[2] * F32(s) for s in scaled]
+    upper = [inside[3] * F32(s) for s in scaled]
     for x in range(12):
         for g in range(2):
-            lows = [before_y[x, j * 2 + g] for j in range(6)]
-            highs = [after_y[x, j * 2 + g] for j in range(6)]
+            lows = [before[x, j * 2 + g] for j in range(6)]
+            highs = [after[x, j * 2 + g] for j in range(6)]
             for yi in range(6):
                 n = yi * 2 + g
                 total = acc[x, n]
                 for k in range(yi + 1, 7):
-                    total = total + from_y[0][k] * lows[6 + yi - k]
+                    total = total + lower[k] * lows[6 + yi - k]
                 for k in range(6 - yi, 7):
-                    total = total + from_y[1][k] * highs[yi + k - 6]
-                if x < 6:
-                    for k in range(x + 1, 7):
-                        total = total + from_x[0][k] * before_x[6 + x - k, n]
-                else:
-                    for k in range(12 - x, 7):
-                        total = total + from_x[1][k] * after_x[x + k - 12, n]
-                full[x, n] = total
-                if halves:
-                    halves[x // 6][x % 6, n] = total
-
-
-def bricks_body(place, low, high, next_low, last_high, out, rows, sem):
+                    total = total + upper[k] * highs[yi + k - 6]
+                out[x, n] = total
+
+
+def edge_x_body(alpha, inside, acc, before, after, full, *halves):
+    scaled = [-0.5 * alpha * w for w in weights]
+    lower = [inside[0] * F32(s) for s in scaled]
+    upper = [inside[1] * F32(s) for s in scaled]
+    for n in range(12):
+        lows = [before[j, n] for j in range(6)]
+        highs = [after[j, n] for j in range(6)]
+        for x in range(12):
+            total = acc[x, n]
+            if x < 6:
+                for k in range(x + 1, 7):
+                    total = total + lower[k] * lows[6 + x - k]
+            else:
+                for k in range(12 - x, 7):
+                    total = total + upper[k] * highs[x + k - 12]
+            full[x, n] = total
+            if halves:
+                halves[x // 6][x % 6, n] = total
+
+
+def bricks_body(place, low, high, following, preceding, out, rows, sem):
     first = place[0] == 0
     for xi in range(6):
         for yi in range(6):
             for g in range(2):
                 n = yi * 2 + g
                 start = g * 288 + xi * 6 + yi
-                rows[pl.ds(start, 8, stride=36), :] = jnp.where(first, low[xi, n], last_high[xi, n])
-                rows[pl.ds(576 + start, 8, stride=36), :] = jnp.where(first, next_low[xi, n], high[xi, n])
+                rows[pl.ds(start, 8, stride=36), :] = jnp.where(first, low[xi, n], preceding[6 + xi, n])
+                rows[pl.ds(576 + start, 8, stride=36), :] = jnp.where(first, following[xi, n], high[xi, n])
     write = pltpu.make_async_copy(rows, out, sem)
     write.start()
     write.wait()
@@ -160,9 +172,9 @@
     return full.at[pl.ds(0, 6)], full.at[pl.ds(6, 6)]
 
 
-def near_gram_body(low, high, applied, next_low, next_high, last_low, last_high, out):
+def near_gram_body(low, high, applied, following, preceding, out):
     mine = (low, high)
-    total = products([mine, halves_of(applied)], [mine, (next_low, next_high), (last_low, last_high)])
+    total = products([mine, halves_of(applied)], [mine, halves_of(following), halves_of(preceding)])
     out[...] = jnp.concatenate([total, jnp.zeros((32, 80), F32)], axis=1)
 
 
@@ -240,44 +252,43 @@
         [SM] + [VM] * 4,
     )
 
-    def step(numbers, planes, previous, outs, others=()):
+    def step(numbers, planes, previous, outs, last=False):
         full, low, high = planes
-        halos = (
-            lax.ppermute(full, ROWS, UP),
-            lax.ppermute(full, ROWS, DOWN),
-            lax.ppermute(high, "z", UP),
-            lax.ppermute(low, "z", DOWN),
-        )
+        before_x = lax.ppermute(high, "z", UP)
+        after_x = lax.ppermute(low, "z", DOWN)
+        later = full
+        if last:
+            later = lax.optimization_barrier((full, before_x))[0]
+        halos = (lax.ppermute(full, ROWS, UP), lax.ppermute(later, ROWS, DOWN), before_x, after_x)
 
         def interior(*refs):
             interior_body(*numbers, *refs)
 
         acc = call(interior, FULL, [full, field, *previous], flops=400_000_000)
 
-        if others:
-            acc = lax.optimization_barrier((acc, *others))[0]
-
-        def edge(*refs):
-            edge_body(numbers[0], *refs)
-
-        return call(edge, outs, [inside, acc, *halos[2:], *halos[:2]], [SM] + [VM] * 5)
+        def edge_y(*refs):
+            edge_y_body(numbers[0], *refs)
+
+        def edge_x(*refs):
+            edge_x_body(numbers[0], *refs)
+
+        acc = call(edge_y, FULL, [inside, acc, *halos[:2]], [SM] + [VM] * 3, flops=200_000_000)
+        return call(edge_x, outs, [inside, acc, *halos[2:]], [SM] + [VM] * 3)
 
     y0 = (full, low, high)
     y1 = step(first, y0, (), [FULL, HALF, HALF])
     y2 = step(second, y1, (y0[0],), [FULL, HALF, HALF])
     y3 = step(third, y2, (y1[0],), [FULL, HALF, HALF])
     full, low, high = y3
-    next_low = lax.ppermute(low, RING, LAST)
-    last_high = lax.ppermute(high, RING, NEXT)
-    next_high = lax.ppermute(high, RING, LAST)
-    last_low = lax.ppermute(low, RING, NEXT)
-    applied = step(plain, y3, (), [FULL], (next_low, last_high, next_high, last_low))[0]
-    far_low = lax.ppermute(next_low, RING, LAST)
-    far_high = lax.ppermute(last_high, RING, NEXT)
+    following = lax.ppermute(full, RING, LAST)
+    preceding = lax.ppermute(full, RING, NEXT)
+    far_low = lax.ppermute(following[:6], RING, LAST)
+    far_high = lax.ppermute(preceding[6:], RING, NEXT)
+    applied = step(plain, y3, (), [FULL], True)[0]
     filtered = call(
         bricks_body,
         jax.ShapeDtypeStruct((1152, 128), F32),
-        [place, low, high, next_low, last_high],
+        [place, low, high, following, preceding],
         [SM] + [VM] * 4,
         out_specs=pl.BlockSpec(memory_space=pl.ANY),
         scratch=[pltpu.VMEM((1152, 128), F32), pltpu.SemaphoreType.DMA],
@@ -286,7 +297,7 @@
     near = call(
         near_gram_body,
         jax.ShapeDtypeStruct((32, 128), F32),
-        [low, high, applied, next_low, next_high, last_low, last_high],
+        [low, high, applied, following, preceding],
         flops=400_000_000,
     )
     far_part = call(

time: 111 us -> 111 us (level)
  starting transfers between devices: 41.9 us -> 38.3 us
  Pallas kernels: 15 us -> 18 us
  waiting for transfers between devices: 39.2 us -> 37.4 us
  blocking collectives: 12.3 us -> 14.1 us
    ppermute x18 -> x16, waiting for transfers between devices: 24.5 us -> 15.8 us  [the longest x4 10.2 us: step(): before_x = lax.ppermute(high, 'z', UP)]
    ppermute x4, waiting for transfers between devices: 0.01 us -> 6.97 us  [step(): lax.ppermute(full, ROWS, UP)]
    pallas_call x15 -> x19, Pallas kernels: 15 us -> 18 us  [call(): pl.pallas_call(body, out_shape=outs, in_specs=specs or [VM] * len(inputs)...]
    ppermute x18 -> x16, starting transfers between devices: 34 us -> 31.4 us  [the longest x4 10.7 us: step(): lax.ppermute(later, ROWS, DOWN)]
    all_to_all x1, blocking collectives: 12.3 us -> 14.1 us  [local(): lax.all_to_all(copies, ('xl',) + ROWS, split_axis=0, concat_axis=0, tiled...]
    all_to_all x1, starting transfers between devices: 5.66 us -> 4.36 us  [local(): parts = lax.all_to_all(copies, 'z', split_axis=0, concat_axis=0, tiled=True)]
  transfers between devices with their start and end apart: 25 -> 23, of which waited for: 11 -> 12; matrix products, arithmetic and copies ran while one was open for 0% -> 0% of each run, Pallas kernels for 8% -> 11%
where the time goes in v6:
time: 111 us; the launch traced here: 110 us
  starting transfers between devices  38.3 us (35%)
  waiting for transfers between devices  37.4 us (34%)
  Pallas kernels  18 us (16%)
  blocking collectives  14.1 us (13%)
    pallas_call x19, Pallas kernels, call(): pl.pallas_call(body, out_shape=outs, in_specs=specs or [VM] * len(inputs)...  18 us
    all_to_all x1, blocking collectives, local(): lax.all_to_all(copies, ('xl',) + ROWS, split_axis=0, concat_axis=0, tiled...  14.1 us
    ppermute x4, starting transfers between devices, step(): lax.ppermute(later, ROWS, DOWN)  10.7 us
    ppermute x4, waiting for transfers between devices, step(): before_x = lax.ppermute(high, 'z', UP)  10.2 us
    ppermute x4, starting transfers between devices, step(): after_x = lax.ppermute(low, 'z', DOWN)  10.1 us
    all_to_all x1, waiting for transfers between devices, local(): parts = lax.all_to_all(copies, 'z', split_axis=0, concat_axis=0, tiled=True)  7.69 us
    ppermute x4, waiting for transfers between devices, step(): lax.ppermute(full, ROWS, UP)  6.97 us
    ppermute x1, waiting for transfers between devices, local(): other_field = lax.ppermute(own_field, 'xl', SWAP)  6.93 us
  transfers between devices with their start and end apart: 23, of which 12 were waited for; matrix products, arithmetic and copies ran while one was open for 0% of the time, Pallas kernels for 11%

profile of v6, /device:TPU:4, one launch (start us, length us, event | category | flops | bytes accessed | tf_op | source)
XLA Modules:
  0.0 109.9 jit_solution(7645746792057307345)
XLA Ops:
  0.7 1.0 constant_dynamic-slice_fusion
  1.7 1.3 %collective-permute-start = (f32[576,128]{1,0:T(8,128)S(1)}, f32[576,128]{1,0:T(8,128)S(1)}, u32[]{:S(2)}, u32[]{:S(2)}) collective-permute-start(f32[576,128]{1,0:T(8,128)S(1)} %constant_dynamic-slice_fusion), channel_id=1, source_target_pairs={{0,16},{16,0},{1,17},{17,1},{2,18},{18,2},{3,19},{19,3},{4,20},{20... | collective-permute-start | bytes 884744 | tf_op jit(solution)/shard_map/ppermute | solution.py:246
  3.1 0.9 collective-permute-start.1
  4.0 0.1 pad_add_fusion.place
  4.0 6.9 %collective-permute-done.1.other_field = f32[36,128]{1,0:T(8,128)S(1)} collective-permute-done((f32[36,128]{1,0:T(8,128)S(1)}, f32[36,128]{1,0:T(8,128)S(1)}, u32[]{:S(2)}, u32[]{:S(2)}) %collective-permute-start.1) | collective-permute-done | bytes 18464 | tf_op jit(solution)/shard_map/ppermute | solution.py:247
  11.0 0.0 collective-permute-done.received
  11.0 1.4 %shard_map.49 = (f32[12,12,8,128]{3,2,1,0:T(8,128)S(1)}, f32[6,12,8,128]{3,2,1,0:T(8,128)S(1)}, f32[6,12,8,128]{3,2,1,0:T(8,128)}, f32[12,6,8,128]{3,2,1,0:T(8,128)S(1)}) custom-call(s32[2]{0:T(128)S(1)} %pad_add_fusion.place, f32[1152,128]{1,0:T(8,128)S(1)} %bitcast.9, f32[576,128]{1,0:T(8,128)S(1)} %collective-permute-done.received, ...), custom_call_target="tpu_custom_call" | custom-call | flops 1000000 | bytes 2000000 | tf_op jit(solution)/shard_map/pallas_call | solution.py:32
  12.3 0.0 collective-permute-start.2
  12.3 3.0 %collective-permute-start.3 = (f32[12,12,8,128]{3,2,1,0:T(8,128)S(1)}, f32[12,12,8,128]{3,2,1,0:T(8,128)S(1)}, u32[]{:S(2)}, u32[]{:S(2)}) collective-permute-start(f32[12,12,8,128]{3,2,1,0:T(8,128)S(1)} %get-tuple-element.19.refs_0_.refs_2_), channel_id=1, source_target_pairs={{0,14},{2,0},{4,2},{6,4},{8,6},{10,8},{12,10},{14,12},{1,15},{3,1}... | collective-permute-start | bytes 1769480 | tf_op jit(solution)/shard_map/ppermute | solution.py:262
  15.3 1.9 %collective-permute-start.4 = (f32[6,12,8,128]{3,2,1,0:T(8,128)}, f32[6,12,8,128]{3,2,1,0:T(8,128)S(1)}, u32[]{:S(2)}, u32[]{:S(2)}) collective-permute-start(f32[6,12,8,128]{3,2,1,0:T(8,128)} %get-tuple-element.21), channel_id=1, source_target_pairs={{0,32},{32,64},{64,96},{96,128},{128,160},{160,192},{192,224},{224... | collective-permute-start | bytes 884744 | tf_op jit(solution)/shard_map/ppermute | solution.py:257
  17.2 3.9 %collective-permute-start.5 = (f32[6,12,8,128]{3,2,1,0:T(8,128)S(1)}, f32[6,12,8,128]{3,2,1,0:T(8,128)S(1)}, u32[]{:S(2)}, u32[]{:S(2)}) collective-permute-start(f32[6,12,8,128]{3,2,1,0:T(8,128)S(1)} %get-tuple-element.22), channel_id=1, source_target_pairs={{0,224},{32,0},{64,32},{96,64},{128,96},{160,128},{192,160},{224,1... | collective-permute-start | bytes 884744 | tf_op jit(solution)/shard_map/ppermute | solution.py:258
  21.2 0.1 add_convert_fusion.refs_0_
  21.2 1.0 shard_map.50.refs_1_
  22.2 0.6 collective-permute-done.2.refs_2_
  22.9 0.0 collective-permute-done.3.refs_3_
  22.9 0.8 shard_map.51.refs_1_
  23.7 3.6 %collective-permute-done.4.refs_2_ = f32[6,12,8,128]{3,2,1,0:T(8,128)S(1)} collective-permute-done((f32[6,12,8,128]{3,2,1,0:T(8,128)}, f32[6,12,8,128]{3,2,1,0:T(8,128)S(1)}, u32[]{:S(2)}, u32[]{:S(2)}) %collective-permute-start.4) | collective-permute-done | bytes 294944 | tf_op jit(solution)/shard_map/ppermute | solution.py:257
  27.3 0.0 collective-permute-done.5.refs_3_
  27.3 0.7 shard_map.52
  28.0 0.0 collective-permute-start.6
  28.0 2.9 %collective-permute-start.7 = (f32[12,12,8,128]{3,2,1,0:T(8,128)S(1)}, f32[12,12,8,128]{3,2,1,0:T(8,128)S(1)}, u32[]{:S(2)}, u32[]{:S(2)}) collective-permute-start(f32[12,12,8,128]{3,2,1,0:T(8,128)S(1)} %get-tuple-element.23.refs_0_.refs_2_), channel_id=1, source_target_pairs={{0,14},{2,0},{4,2},{6,4},{8,6},{10,8},{12,10},{14,12},{1,15},{3,1}... | collective-permute-start | bytes 1769480 | tf_op jit(solution)/shard_map/ppermute | solution.py:262
  31.0 0.0 collective-permute-start.8
  31.0 3.2 %collective-permute-start.9 = (f32[6,12,8,128]{3,2,1,0:T(8,128)S(1)}, f32[6,12,8,128]{3,2,1,0:T(8,128)S(1)}, u32[]{:S(2)}, u32[]{:S(2)}) collective-permute-start(f32[6,12,8,128]{3,2,1,0:T(8,128)S(1)} %get-tuple-element.25), channel_id=1, source_target_pairs={{0,224},{32,0},{64,32},{96,64},{128,96},{160,128},{192,160},{224,1... | collective-permute-start | bytes 884744 | tf_op jit(solution)/shard_map/ppermute | solution.py:258
  34.2 1.1 %shard_map.53.refs_1_ = f32[12,12,8,128]{3,2,1,0:T(8,128)S(1)} custom-call(f32[12,12,8,128]{3,2,1,0:T(8,128)S(1)} %get-tuple-element.23.refs_0_.refs_2_, f32[12,6,8,128]{3,2,1,0:T(8,128)S(1)} %get-tuple-element.20.refs_1_, f32[12,12,8,128]{3,2,1,0:T(8,128)S(1)} %get-tuple-element.19.refs_0_.refs_2_), custom_call_target="tpu_custom_call" | custom-call | flops 400000000 | bytes 2000000 | tf_op jit(solution)/shard_map/pallas_call | solution.py:32
  35.4 3.2 %collective-permute-done.6.refs_2_ = f32[12,12,8,128]{3,2,1,0:T(8,128)S(1)} collective-permute-done((f32[12,12,8,128]{3,2,1,0:T(8,128)S(1)}, f32[12,12,8,128]{3,2,1,0:T(8,128)S(1)}, u32[]{:S(2)}, u32[]{:S(2)}) %collective-permute-start.6) | collective-permute-done | bytes 589856 | tf_op jit(solution)/shard_map/ppermute | solution.py:262
  38.5 0.0 collective-permute-done.7.refs_3_
  38.6 0.8 shard_map.54.refs_1_
  39.4 0.5 collective-permute-done.8.refs_2_
  39.9 0.7 shard_map.55
  40.6 0.3 collective-permute-start.10
  40.9 2.6 %collective-permute-start.11 = (f32[12,12,8,128]{3,2,1,0:T(8,128)S(1)}, f32[12,12,8,128]{3,2,1,0:T(8,128)S(1)}, u32[]{:S(2)}, u32[]{:S(2)}) collective-permute-start(f32[12,12,8,128]{3,2,1,0:T(8,128)S(1)} %get-tuple-element.26.refs_0_), channel_id=1, source_target_pairs={{0,14},{2,0},{4,2},{6,4},{8,6},{10,8},{12,10},{14,12},{1,15},{3,1}... | collective-permute-start | bytes 1769480 | tf_op jit(solution)/shard_map/ppermute | solution.py:262
  43.6 2.2 %collective-permute-start.12 = (f32[6,12,8,128]{3,2,1,0:T(8,128)S(1)}, f32[6,12,8,128]{3,2,1,0:T(8,128)S(1)}, u32[]{:S(2)}, u32[]{:S(2)}) collective-permute-start(f32[6,12,8,128]{3,2,1,0:T(8,128)S(1)} %get-tuple-element.27), channel_id=1, source_target_pairs={{0,32},{32,64},{64,96},{96,128},{128,160},{160,192},{192,224},{224... | collective-permute-start | bytes 884744 | tf_op jit(solution)/shard_map/ppermute | solution.py:257
  45.8 1.0 collective-permute-start.13
  46.8 1.1 %shard_map.56.refs_1_ = f32[12,12,8,128]{3,2,1,0:T(8,128)S(1)} custom-call(f32[12,12,8,128]{3,2,1,0:T(8,128)S(1)} %get-tuple-element.26.refs_0_, f32[12,6,8,128]{3,2,1,0:T(8,128)S(1)} %get-tuple-element.20.refs_1_, f32[12,12,8,128]{3,2,1,0:T(8,128)S(1)} %get-tuple-element.23.refs_0_.refs_2_), custom_call_target="tpu_custom_call" | custom-call | flops 400000000 | bytes 2000000 | tf_op jit(solution)/shard_map/pallas_call | solution.py:32
  47.9 3.2 %collective-permute-done.10.refs_2_ = f32[12,12,8,128]{3,2,1,0:T(8,128)S(1)} collective-permute-done((f32[12,12,8,128]{3,2,1,0:T(8,128)S(1)}, f32[12,12,8,128]{3,2,1,0:T(8,128)S(1)}, u32[]{:S(2)}, u32[]{:S(2)}) %collective-permute-start.10) | collective-permute-done | bytes 589856 | tf_op jit(solution)/shard_map/ppermute | solution.py:262
  51.1 0.8 shard_map.57.refs_1_
  51.9 0.2 collective-permute-done.12.refs_2_
  52.1 0.8 collective-permute-done.13.refs_3_
  52.9 0.7 shard_map.58
  53.6 1.8 %collective-permute-start.17 = (f32[6,12,8,128]{3,2,1,0:T(8,128)S(1)}, f32[6,12,8,128]{3,2,1,0:T(8,128)S(1)}, u32[]{:S(2)}, u32[]{:S(2)}) collective-permute-start(f32[6,12,8,128]{3,2,1,0:T(8,128)S(1)} %get-tuple-element.30.high), channel_id=1, source_target_pairs={{0,32},{32,64},{64,96},{96,128},{128,160},{160,192},{192,224},{224... | collective-permute-start | bytes 884744 | tf_op jit(solution)/shard_map/ppermute | solution.py:257
  55.4 0.5 collective-permute-start.14
  56.0 1.5 %collective-permute-start.15 = (f32[12,12,8,128]{3,2,1,0:T(8,128)S(1)}, f32[12,12,8,128]{3,2,1,0:T(8,128)S(1)}, u32[]{:S(2)}, u32[]{:S(2)}) collective-permute-start(f32[12,12,8,128]{3,2,1,0:T(8,128)S(1)} %get-tuple-element.32.refs_0_), channel_id=1, source_target_pairs={{0,16},{16,1},{1,17},{17,0},{2,18},{18,3},{3,19},{19,2},{4,20},{20... | collective-permute-start | bytes 1769480 | tf_op jit(solution)/shard_map/ppermute | solution.py:284
  57.5 5.9 %collective-permute-done.17.refs_2_ = f32[6,12,8,128]{3,2,1,0:T(8,128)S(1)} collective-permute-done((f32[6,12,8,128]{3,2,1,0:T(8,128)S(1)}, f32[6,12,8,128]{3,2,1,0:T(8,128)S(1)}, u32[]{:S(2)}, u32[]{:S(2)}) %collective-permute-start.17) | collective-permute-done | bytes 294944 | tf_op jit(solution)/shard_map/ppermute | solution.py:257
  63.4 2.2 %collective-permute-start.18 = (f32[12,12,8,128]{3,2,1,0:T(8,128)S(1)}, f32[12,12,8,128]{3,2,1,0:T(8,128)S(1)}, u32[]{:S(2)}, u32[]{:S(2)}) collective-permute-start(f32[12,12,8,128]{3,2,1,0:T(8,128)S(1)} %get-tuple-element.32.refs_0_), channel_id=1, source_target_pairs={{0,14},{2,0},{4,2},{6,4},{8,6},{10,8},{12,10},{14,12},{1,15},{3,1}... | collective-permute-start | bytes 1769480 | tf_op jit(solution)/shard_map/ppermute | solution.py:262
  65.6 1.9 %collective-permute-start.19 = (f32[6,12,8,128]{3,2,1,0:T(8,128)S(1)}, f32[6,12,8,128]{3,2,1,0:T(8,128)S(1)}, u32[]{:S(2)}, u32[]{:S(2)}) collective-permute-start(f32[6,12,8,128]{3,2,1,0:T(8,128)S(1)} %get-tuple-element.29.low), channel_id=1, source_target_pairs={{0,224},{32,0},{64,32},{96,64},{128,96},{160,128},{192,160},{224,1... | collective-permute-start | bytes 884744 | tf_op jit(solution)/shard_map/ppermute | solution.py:258
  67.5 3.0 %collective-permute-done.14.following = f32[12,12,8,128]{3,2,1,0:T(8,128)S(1)} collective-permute-done((f32[12,12,8,128]{3,2,1,0:T(8,128)S(1)}, f32[12,12,8,128]{3,2,1,0:T(8,128)S(1)}, u32[]{:S(2)}, u32[]{:S(2)}) %collective-permute-start.14) | collective-permute-done | bytes 589856 | tf_op jit(solution)/shard_map/ppermute | solution.py:283
  70.5 0.6 collective-permute-start.21
  71.1 0.0 collective-permute-done.15.preceding
  71.1 2.0 %collective-permute-start.20 = (f32[6,12,8,128]{3,2,1,0:T(8,128)S(1)}, f32[6,12,8,128]{3,2,1,0:T(8,128)S(1)}, u32[]{:S(2)}, u32[]{:S(2)}) collective-permute-start(f32[6,12,8,128]{3,2,1,0:T(8,128)S(1)} %slice.8), channel_id=1, source_target_pairs={{0,16},{16,1},{1,17},{17,0},{2,18},{18,3},{3,19},{19,2},{4,20},{20... | collective-permute-start | bytes 884744 | tf_op jit(solution)/shard_map/ppermute | solution.py:286
  73.1 1.0 shard_map.60.refs_1_
  74.1 0.0 collective-permute-done.16.refs_2_
  74.1 0.8 shard_map.61.refs_1_
  75.0 0.7 shard_map.62.applied
  75.7 1.5 %shard_map.63.near = f32[32,128]{1,0:T(8,128)S(1)} custom-call(f32[6,12,8,128]{3,2,1,0:T(8,128)S(1)} %get-tuple-element.29.low, f32[6,12,8,128]{3,2,1,0:T(8,128)S(1)} %get-tuple-element.30.high, f32[12,12,8,128]{3,2,1,0:T(8,128)S(1)} %shard_map.62.applied, f32[12,12,8,128]{3,2,1,0:T(8,128)S(1)} %collective-permute-done.14.following, ...), custom_call_target="tpu_custom_call" | custom-call | flops 400000000 | bytes 2000000 | tf_op jit(solution)/shard_map/pallas_call | solution.py:32
  77.2 1.9 %collective-permute-done.21.far_low = f32[6,12,8,128]{3,2,1,0:T(8,128)S(1)} collective-permute-done((f32[6,12,8,128]{3,2,1,0:T(8,128)S(1)}, f32[6,12,8,128]{3,2,1,0:T(8,128)S(1)}, u32[]{:S(2)}, u32[]{:S(2)}) %collective-permute-start.21) | collective-permute-done | bytes 294944 | tf_op jit(solution)/shard_map/ppermute | solution.py:285
  79.1 0.6 shard_map.64.far_part
  79.7 0.0 collective-permute-done.20.far_high
  79.7 1.3 %shard_map.65 = f32[16,16,128]{2,1,0:T(8,128)S(1)} custom-call(s32[2]{0:T(128)S(1)} %pad_add_fusion.place, f32[6,12,8,128]{3,2,1,0:T(8,128)S(1)} %get-tuple-element.29.low, f32[6,12,8,128]{3,2,1,0:T(8,128)S(1)} %get-tuple-element.30.high, f32[12,12,8,128]{3,2,1,0:T(8,128)S(1)} %shard_map.62.applied, f32[6,12,8,128]{3,2,1,0:T(8,128)S(1)} %collective-permute-done.20.far_high, ...), custom_call_target="tpu_custom_call" | custom-call | flops 1000000 | bytes 2000000 | tf_op jit(solution)/shard_map/pallas_call | solution.py:32
  81.0 14.1 %all_to_all.10.parts = f32[16,16,128]{2,1,0:T(8,128)S(1)} all-to-all(f32[16,16,128]{2,1,0:T(8,128)S(1)} %shard_map.65), channel_id=1, replica_groups=mesh['z'=8,'xl'=2,'y'=4,'core'=2,'xh'=2] {'xl','y','core'}, dimensions={0} | all-to-all | bytes 262144 | tf_op jit(solution)/shard_map/all_to_all | solution.py:315
  95.1 0.7 shard_map.66
  95.7 4.4 %all-to-all-start.1 = ((f32[8,32,128]{2,1,0:T(8,128)}), f32[8,32,128]{2,1,0:T(8,128)S(1)}, u32[]{:S(2)}, u32[]{:S(2)}) async-start(f32[8,32,128]{2,1,0:T(8,128)} %shard_map.66), calls=%async_computation.1 | async-start | bytes 262144 | tf_op jit(solution)/shard_map/all_to_all | solution.py:317
  100.1 1.4 %shard_map.59 = f32[1152,128]{1,0:T(8,128)} custom-call(s32[2]{0:T(128)S(1)} %pad_add_fusion.place, f32[6,12,8,128]{3,2,1,0:T(8,128)S(1)} %get-tuple-element.29.low, f32[6,12,8,128]{3,2,1,0:T(8,128)S(1)} %get-tuple-element.30.high, f32[12,12,8,128]{3,2,1,0:T(8,128)S(1)} %collective-permute-done.14.following, ...), custom_call_target="tpu_custom_call" | custom-call | flops 400000000 | bytes 2000000 | tf_op jit(solution)/shard_map/pallas_call | solution.py:32
  101.5 7.7 %all-to-all-done.1.parts = f32[8,32,128]{2,1,0:T(8,128)S(1)} async-done(((f32[8,32,128]{2,1,0:T(8,128)}), f32[8,32,128]{2,1,0:T(8,128)S(1)}, u32[]{:S(2)}, u32[]{:S(2)}) %all-to-all-start.1) | async-done | bytes 131104 | tf_op jit(solution)/shard_map/all_to_all | solution.py:317
  109.2 0.7 shard_map.67
  (13 shorter events, 0.1 us)
Async XLA Ops:
  0.6 10.4 %copy-start = (f32[32,1,6,6,128]{4,1,3,2,0:T(1,128)S(1)}, f32[32,1,6,6,128]{4,1,3,2,0:T(1,128)}, u32[]{:S(2)}) copy-start(f32[32,1,6,6,128]{4,1,3,2,0:T(1,128)} %param.2) | copy-start | bytes 1769476
  0.6 2.3 %copy-start.1 = (f32[1,6,6,128]{3,0,2,1:T(1,128)S(1)}, f32[1,6,6,128]{3,0,2,1:T(1,128)}, u32[]{:S(2)}) copy-start(f32[1,6,6,128]{3,0,2,1:T(1,128)} %param.3) | copy-start | bytes 55300
  1.7 9.3 %collective-permute-start = (f32[576,128]{1,0:T(8,128)S(1)}, f32[576,128]{1,0:T(8,128)S(1)}, u32[]{:S(2)}, u32[]{:S(2)}) collective-permute-start(f32[576,128]{1,0:T(8,128)S(1)} %constant_dynamic-slice_fusion), channel_id=1, source_target_pairs={{0,16},{16,0},{1,17},{17,1},{2,18},{18,2},{3,19},{19,3},{4,20},{20... | collective-permute-start | bytes 884744 | tf_op jit(solution)/shard_map/ppermute | solution.py:246
  3.1 7.9 %collective-permute-start.1 = (f32[36,128]{1,0:T(8,128)S(1)}, f32[36,128]{1,0:T(8,128)S(1)}, u32[]{:S(2)}, u32[]{:S(2)}) collective-permute-start(f32[36,128]{1,0:T(8,128)S(1)} %reshape.16.own_field), channel_id=1, source_target_pairs={{0,16},{16,0},{1,17},{17,1},{2,18},{18,2},{3,19},{19,3},{4,20},{20... | collective-permute-start | bytes 55304 | tf_op jit(solution)/shard_map/ppermute | solution.py:247
  12.3 10.5 %collective-permute-start.2 = (f32[12,12,8,128]{3,2,1,0:T(8,128)S(1)}, f32[12,12,8,128]{3,2,1,0:T(8,128)S(1)}, u32[]{:S(2)}, u32[]{:S(2)}) collective-permute-start(f32[12,12,8,128]{3,2,1,0:T(8,128)S(1)} %get-tuple-element.19.refs_0_.refs_2_), channel_id=1, source_target_pairs={{0,2},{2,4},{4,6},{6,8},{8,10},{10,12},{12,14},{14,0},{1,3},{3,5},... | collective-permute-start | bytes 1769480 | tf_op jit(solution)/shard_map/ppermute | solution.py:262
  12.3 10.5 %collective-permute-start.3 = (f32[12,12,8,128]{3,2,1,0:T(8,128)S(1)}, f32[12,12,8,128]{3,2,1,0:T(8,128)S(1)}, u32[]{:S(2)}, u32[]{:S(2)}) collective-permute-start(f32[12,12,8,128]{3,2,1,0:T(8,128)S(1)} %get-tuple-element.19.refs_0_.refs_2_), channel_id=1, source_target_pairs={{0,14},{2,0},{4,2},{6,4},{8,6},{10,8},{12,10},{14,12},{1,15},{3,1}... | collective-permute-start | bytes 1769480 | tf_op jit(solution)/shard_map/ppermute | solution.py:262
  15.3 12.0 %collective-permute-start.4 = (f32[6,12,8,128]{3,2,1,0:T(8,128)}, f32[6,12,8,128]{3,2,1,0:T(8,128)S(1)}, u32[]{:S(2)}, u32[]{:S(2)}) collective-permute-start(f32[6,12,8,128]{3,2,1,0:T(8,128)} %get-tuple-element.21), channel_id=1, source_target_pairs={{0,32},{32,64},{64,96},{96,128},{128,160},{160,192},{192,224},{224... | collective-permute-start | bytes 884744 | tf_op jit(solution)/shard_map/ppermute | solution.py:257
  17.2 10.1 %collective-permute-start.5 = (f32[6,12,8,128]{3,2,1,0:T(8,128)S(1)}, f32[6,12,8,128]{3,2,1,0:T(8,128)S(1)}, u32[]{:S(2)}, u32[]{:S(2)}) collective-permute-start(f32[6,12,8,128]{3,2,1,0:T(8,128)S(1)} %get-tuple-element.22), channel_id=1, source_target_pairs={{0,224},{32,0},{64,32},{96,64},{128,96},{160,128},{192,160},{224,1... | collective-permute-start | bytes 884744 | tf_op jit(solution)/shard_map/ppermute | solution.py:258
  28.0 10.5 %collective-permute-start.6 = (f32[12,12,8,128]{3,2,1,0:T(8,128)S(1)}, f32[12,12,8,128]{3,2,1,0:T(8,128)S(1)}, u32[]{:S(2)}, u32[]{:S(2)}) collective-permute-start(f32[12,12,8,128]{3,2,1,0:T(8,128)S(1)} %get-tuple-element.23.refs_0_.refs_2_), channel_id=1, source_target_pairs={{0,2},{2,4},{4,6},{6,8},{8,10},{10,12},{12,14},{14,0},{1,3},{3,5},... | collective-permute-start | bytes 1769480 | tf_op jit(solution)/shard_map/ppermute | solution.py:262
  28.0 10.5 %collective-permute-start.7 = (f32[12,12,8,128]{3,2,1,0:T(8,128)S(1)}, f32[12,12,8,128]{3,2,1,0:T(8,128)S(1)}, u32[]{:S(2)}, u32[]{:S(2)}) collective-permute-start(f32[12,12,8,128]{3,2,1,0:T(8,128)S(1)} %get-tuple-element.23.refs_0_.refs_2_), channel_id=1, source_target_pairs={{0,14},{2,0},{4,2},{6,4},{8,6},{10,8},{12,10},{14,12},{1,15},{3,1}... | collective-permute-start | bytes 1769480 | tf_op jit(solution)/shard_map/ppermute | solution.py:262
  31.0 8.9 %collective-permute-start.8 = (f32[6,12,8,128]{3,2,1,0:T(8,128)S(1)}, f32[6,12,8,128]{3,2,1,0:T(8,128)S(1)}, u32[]{:S(2)}, u32[]{:S(2)}) collective-permute-start(f32[6,12,8,128]{3,2,1,0:T(8,128)S(1)} %get-tuple-element.24), channel_id=1, source_target_pairs={{0,32},{32,64},{64,96},{96,128},{128,160},{160,192},{192,224},{224... | collective-permute-start | bytes 884744 | tf_op jit(solution)/shard_map/ppermute | solution.py:257
  31.0 8.9 %collective-permute-start.9 = (f32[6,12,8,128]{3,2,1,0:T(8,128)S(1)}, f32[6,12,8,128]{3,2,1,0:T(8,128)S(1)}, u32[]{:S(2)}, u32[]{:S(2)}) collective-permute-start(f32[6,12,8,128]{3,2,1,0:T(8,128)S(1)} %get-tuple-element.25), channel_id=1, source_target_pairs={{0,224},{32,0},{64,32},{96,64},{128,96},{160,128},{192,160},{224,1... | collective-permute-start | bytes 884744 | tf_op jit(solution)/shard_map/ppermute | solution.py:258
  40.6 10.5 %collective-permute-start.10 = (f32[12,12,8,128]{3,2,1,0:T(8,128)S(1)}, f32[12,12,8,128]{3,2,1,0:T(8,128)S(1)}, u32[]{:S(2)}, u32[]{:S(2)}) collective-permute-start(f32[12,12,8,128]{3,2,1,0:T(8,128)S(1)} %get-tuple-element.26.refs_0_), channel_id=1, source_target_pairs={{0,2},{2,4},{4,6},{6,8},{8,10},{10,12},{12,14},{14,0},{1,3},{3,5},... | collective-permute-start | bytes 1769480 | tf_op jit(solution)/shard_map/ppermute | solution.py:262
  40.9 10.2 %collective-permute-start.11 = (f32[12,12,8,128]{3,2,1,0:T(8,128)S(1)}, f32[12,12,8,128]{3,2,1,0:T(8,128)S(1)}, u32[]{:S(2)}, u32[]{:S(2)}) collective-permute-start(f32[12,12,8,128]{3,2,1,0:T(8,128)S(1)} %get-tuple-element.26.refs_0_), channel_id=1, source_target_pairs={{0,14},{2,0},{4,2},{6,4},{8,6},{10,8},{12,10},{14,12},{1,15},{3,1}... | collective-permute-start | bytes 1769480 | tf_op jit(solution)/shard_map/ppermute | solution.py:262
  43.6 8.6 %collective-permute-start.12 = (f32[6,12,8,128]{3,2,1,0:T(8,128)S(1)}, f32[6,12,8,128]{3,2,1,0:T(8,128)S(1)}, u32[]{:S(2)}, u32[]{:S(2)}) collective-permute-start(f32[6,12,8,128]{3,2,1,0:T(8,128)S(1)} %get-tuple-element.27), channel_id=1, source_target_pairs={{0,32},{32,64},{64,96},{96,128},{128,160},{160,192},{192,224},{224... | collective-permute-start | bytes 884744 | tf_op jit(solution)/shard_map/ppermute | solution.py:257
  45.8 7.1 %collective-permute-start.13 = (f32[6,12,8,128]{3,2,1,0:T(8,128)S(1)}, f32[6,12,8,128]{3,2,1,0:T(8,128)S(1)}, u32[]{:S(2)}, u32[]{:S(2)}) collective-permute-start(f32[6,12,8,128]{3,2,1,0:T(8,128)S(1)} %get-tuple-element.28), channel_id=1, source_target_pairs={{0,224},{32,0},{64,32},{96,64},{128,96},{160,128},{192,160},{224,1... | collective-permute-start | bytes 884744 | tf_op jit(solution)/shard_map/ppermute | solution.py:258
  53.6 9.8 %collective-permute-start.17 = (f32[6,12,8,128]{3,2,1,0:T(8,128)S(1)}, f32[6,12,8,128]{3,2,1,0:T(8,128)S(1)}, u32[]{:S(2)}, u32[]{:S(2)}) collective-permute-start(f32[6,12,8,128]{3,2,1,0:T(8,128)S(1)} %get-tuple-element.30.high), channel_id=1, source_target_pairs={{0,32},{32,64},{64,96},{96,128},{128,160},{160,192},{192,224},{224... | collective-permute-start | bytes 884744 | tf_op jit(solution)/shard_map/ppermute | solution.py:257
  55.4 15.0 %collective-permute-start.14 = (f32[12,12,8,128]{3,2,1,0:T(8,128)S(1)}, f32[12,12,8,128]{3,2,1,0:T(8,128)S(1)}, u32[]{:S(2)}, u32[]{:S(2)}) collective-permute-start(f32[12,12,8,128]{3,2,1,0:T(8,128)S(1)} %get-tuple-element.32.refs_0_), channel_id=1, source_target_pairs={{0,17},{16,0},{1,16},{17,1},{2,19},{18,2},{3,18},{19,3},{4,21},{20... | collective-permute-start | bytes 1769480 | tf_op jit(solution)/shard_map/ppermute | solution.py:283
  56.0 15.1 %collective-permute-start.15 = (f32[12,12,8,128]{3,2,1,0:T(8,128)S(1)}, f32[12,12,8,128]{3,2,1,0:T(8,128)S(1)}, u32[]{:S(2)}, u32[]{:S(2)}) collective-permute-start(f32[12,12,8,128]{3,2,1,0:T(8,128)S(1)} %get-tuple-element.32.refs_0_), channel_id=1, source_target_pairs={{0,16},{16,1},{1,17},{17,0},{2,18},{18,3},{3,19},{19,2},{4,20},{20... | collective-permute-start | bytes 1769480 | tf_op jit(solution)/shard_map/ppermute | solution.py:284
  57.5 16.6 %collective-permute-start.16 = (f32[12,12,8,128]{3,2,1,0:T(8,128)S(1)}, f32[12,12,8,128]{3,2,1,0:T(8,128)S(1)}, u32[]{:S(2)}, u32[]{:S(2)}) collective-permute-start(f32[12,12,8,128]{3,2,1,0:T(8,128)S(1)} %get-tuple-element.32.refs_0_), channel_id=1, source_target_pairs={{0,2},{2,4},{4,6},{6,8},{8,10},{10,12},{12,14},{14,0},{1,3},{3,5},... | collective-permute-start | bytes 1769480 | tf_op jit(solution)/shard_map/ppermute | solution.py:262
  63.4 10.7 %collective-permute-start.18 = (f32[12,12,8,128]{3,2,1,0:T(8,128)S(1)}, f32[12,12,8,128]{3,2,1,0:T(8,128)S(1)}, u32[]{:S(2)}, u32[]{:S(2)}) collective-permute-start(f32[12,12,8,128]{3,2,1,0:T(8,128)S(1)} %get-tuple-element.32.refs_0_), channel_id=1, source_target_pairs={{0,14},{2,0},{4,2},{6,4},{8,6},{10,8},{12,10},{14,12},{1,15},{3,1}... | collective-permute-start | bytes 1769480 | tf_op jit(solution)/shard_map/ppermute | solution.py:262
  65.6 9.4 %collective-permute-start.19 = (f32[6,12,8,128]{3,2,1,0:T(8,128)S(1)}, f32[6,12,8,128]{3,2,1,0:T(8,128)S(1)}, u32[]{:S(2)}, u32[]{:S(2)}) collective-permute-start(f32[6,12,8,128]{3,2,1,0:T(8,128)S(1)} %get-tuple-element.29.low), channel_id=1, source_target_pairs={{0,224},{32,0},{64,32},{96,64},{128,96},{160,128},{192,160},{224,1... | collective-permute-start | bytes 884744 | tf_op jit(solution)/shard_map/ppermute | solution.py:258
  70.5 8.6 %collective-permute-start.21 = (f32[6,12,8,128]{3,2,1,0:T(8,128)S(1)}, f32[6,12,8,128]{3,2,1,0:T(8,128)S(1)}, u32[]{:S(2)}, u32[]{:S(2)}) collective-permute-start(f32[6,12,8,128]{3,2,1,0:T(8,128)S(1)} %slice.9), channel_id=1, source_target_pairs={{0,17},{16,0},{1,16},{17,1},{2,19},{18,2},{3,18},{19,3},{4,21},{20... | collective-permute-start | bytes 884744 | tf_op jit(solution)/shard_map/ppermute | solution.py:285
  71.1 8.5 %collective-permute-start.20 = (f32[6,12,8,128]{3,2,1,0:T(8,128)S(1)}, f32[6,12,8,128]{3,2,1,0:T(8,128)S(1)}, u32[]{:S(2)}, u32[]{:S(2)}) collective-permute-start(f32[6,12,8,128]{3,2,1,0:T(8,128)S(1)} %slice.8), channel_id=1, source_target_pairs={{0,16},{16,1},{1,17},{17,0},{2,18},{18,3},{3,19},{19,2},{4,20},{20... | collective-permute-start | bytes 884744 | tf_op jit(solution)/shard_map/ppermute | solution.py:286
  95.7 13.5 %all-to-all-start.1 = ((f32[8,32,128]{2,1,0:T(8,128)}), f32[8,32,128]{2,1,0:T(8,128)S(1)}, u32[]{:S(2)}, u32[]{:S(2)}) async-start(f32[8,32,128]{2,1,0:T(8,128)} %shard_map.66), calls=%async_computation.1 | async-start | bytes 262144 | tf_op jit(solution)/shard_map/all_to_all | solution.py:317

commit v7 on v6

--- a/solution.py
+++ b/solution.py
@@ -21,7 +21,7 @@
 
 VM = pl.BlockSpec(memory_space=pltpu.VMEM)
 SM = pl.BlockSpec(memory_space=pltpu.SMEM)
-PARAMS = pltpu.CompilerParams(vmem_limit_bytes=32 * 1024 * 1024)
+PARAMS = pltpu.CompilerParams(vmem_limit_bytes=8 * 1024 * 1024)
 F32 = jnp.float32
 
 HALF = jax.ShapeDtypeStruct((6, 12, 8, 128), F32)
@@ -294,6 +294,7 @@
         scratch=[pltpu.VMEM((1152, 128), F32), pltpu.SemaphoreType.DMA],
         flops=400_000_000,
     )
+    applied = lax.optimization_barrier((applied, filtered))[0]
     near = call(
         near_gram_body,
         jax.ShapeDtypeStruct((32, 128), F32),

time: 111 us -> 109 us (0.982)
  blocking collectives: 14.1 us -> 27.1 us
  waiting for transfers between devices: 37.4 us -> 28.3 us
  starting transfers between devices: 38.3 us -> 34 us
  Pallas kernels: 18 us -> 16.6 us
    all_to_all x0 -> x1, blocking collectives: none -> 13.1 us  [local(): parts = lax.all_to_all(copies, 'z', split_axis=0, concat_axis=0, tiled=True)]
    all_to_all x1 -> x0, waiting for transfers between devices: 7.69 us -> none  [local(): parts = lax.all_to_all(copies, 'z', split_axis=0, concat_axis=0, tiled=True)]
    all_to_all x1 -> x0, starting transfers between devices: 4.36 us -> none  [local(): parts = lax.all_to_all(copies, 'z', split_axis=0, concat_axis=0, tiled=True)]
    ppermute x1, waiting for transfers between devices: 1.9 us -> 0.47 us  [local(): far_low = lax.ppermute(following[:6], RING, LAST)]
    pallas_call x19, Pallas kernels: 18 us -> 16.6 us  [call(): pl.pallas_call(body, out_shape=outs, in_specs=specs or [VM] * len(inputs)...]
  transfers between devices with their start and end apart: 23 -> 22, of which waited for: 12 -> 11; matrix products, arithmetic and copies ran while one was open for 0% -> 0% of each run, Pallas kernels for 11% -> 11%
where the time goes in v7:
time: 109 us; the launch traced here: 108 us
  starting transfers between devices  34 us (31%)
  waiting for transfers between devices  28.3 us (26%)
  blocking collectives  27.1 us (25%)
  Pallas kernels  16.6 us (15%)
  local copies, waits for them, and re-layouts  1.1 us (1%)
    pallas_call x19, Pallas kernels, call(): pl.pallas_call(body, out_shape=outs, in_specs=specs or [VM] * len(inputs)...  16.6 us
    all_to_all x1, blocking collectives, local(): lax.all_to_all(copies, ('xl',) + ROWS, split_axis=0, concat_axis=0, tiled...  14.1 us
    all_to_all x1, blocking collectives, local(): parts = lax.all_to_all(copies, 'z', split_axis=0, concat_axis=0, tiled=True)  13.1 us
    ppermute x4, starting transfers between devices, step(): lax.ppermute(later, ROWS, DOWN)  10.5 us
    ppermute x4, starting transfers between devices, step(): after_x = lax.ppermute(low, 'z', DOWN)  10.1 us
    ppermute x4, waiting for transfers between devices, step(): before_x = lax.ppermute(high, 'z', UP)  9.73 us
    ppermute x4, waiting for transfers between devices, step(): lax.ppermute(full, ROWS, UP)  6.97 us
    ppermute x1, waiting for transfers between devices, local(): other_field = lax.ppermute(own_field, 'xl', SWAP)  6.93 us
  transfers between devices with their start and end apart: 22, of which 11 were waited for; matrix products, arithmetic and copies ran while one was open for 0% of the time, Pallas kernels for 11%

profile of v7, /device:TPU:4, one launch (start us, length us, event | category | flops | bytes accessed | tf_op | source)
XLA Modules:
  0.0 108.1 jit_solution(13295602317661417573)
XLA Ops:
  0.7 1.0 constant_dynamic-slice_fusion
  1.7 1.3 %collective-permute-start = (f32[576,128]{1,0:T(8,128)S(1)}, f32[576,128]{1,0:T(8,128)S(1)}, u32[]{:S(2)}, u32[]{:S(2)}) collective-permute-start(f32[576,128]{1,0:T(8,128)S(1)} %constant_dynamic-slice_fusion), channel_id=1, source_target_pairs={{0,16},{16,0},{1,17},{17,1},{2,18},{18,2},{3,19},{19,3},{4,20},{20... | collective-permute-start | bytes 884744 | tf_op jit(solution)/shard_map/ppermute | solution.py:246
  3.1 0.9 collective-permute-start.1
  4.0 0.1 pad_add_fusion.place
  4.0 6.9 %collective-permute-done.1.other_field = f32[36,128]{1,0:T(8,128)S(1)} collective-permute-done((f32[36,128]{1,0:T(8,128)S(1)}, f32[36,128]{1,0:T(8,128)S(1)}, u32[]{:S(2)}, u32[]{:S(2)}) %collective-permute-start.1) | collective-permute-done | bytes 18464 | tf_op jit(solution)/shard_map/ppermute | solution.py:247
  11.0 0.0 collective-permute-done.received
  11.0 0.6 shard_map.49
  11.6 0.0 collective-permute-start.2
  11.7 2.9 %collective-permute-start.3 = (f32[12,12,8,128]{3,2,1,0:T(8,128)S(1)}, f32[12,12,8,128]{3,2,1,0:T(8,128)S(1)}, u32[]{:S(2)}, u32[]{:S(2)}) collective-permute-start(f32[12,12,8,128]{3,2,1,0:T(8,128)S(1)} %get-tuple-element.20.refs_0_.refs_2_), channel_id=1, source_target_pairs={{0,14},{2,0},{4,2},{6,4},{8,6},{10,8},{12,10},{14,12},{1,15},{3,1}... | collective-permute-start | bytes 1769480 | tf_op jit(solution)/shard_map/ppermute | solution.py:262
  14.6 1.9 %collective-permute-start.4 = (f32[6,12,8,128]{3,2,1,0:T(8,128)S(1)}, f32[6,12,8,128]{3,2,1,0:T(8,128)S(1)}, u32[]{:S(2)}, u32[]{:S(2)}) collective-permute-start(f32[6,12,8,128]{3,2,1,0:T(8,128)S(1)} %get-tuple-element.22), channel_id=1, source_target_pairs={{0,32},{32,64},{64,96},{96,128},{128,160},{160,192},{192,224},{224... | collective-permute-start | bytes 884744 | tf_op jit(solution)/shard_map/ppermute | solution.py:257
  16.5 3.9 %collective-permute-start.5 = (f32[6,12,8,128]{3,2,1,0:T(8,128)S(1)}, f32[6,12,8,128]{3,2,1,0:T(8,128)S(1)}, u32[]{:S(2)}, u32[]{:S(2)}) collective-permute-start(f32[6,12,8,128]{3,2,1,0:T(8,128)S(1)} %get-tuple-element.23), channel_id=1, source_target_pairs={{0,224},{32,0},{64,32},{96,64},{128,96},{160,128},{192,160},{224,1... | collective-permute-start | bytes 884744 | tf_op jit(solution)/shard_map/ppermute | solution.py:258
  20.5 0.1 add_convert_fusion.refs_0_
  20.5 1.0 shard_map.50.refs_1_
  21.6 0.6 collective-permute-done.2.refs_2_
  22.2 0.0 collective-permute-done.3.refs_3_
  22.2 0.8 shard_map.51.refs_1_
  23.0 3.4 %collective-permute-done.4.refs_2_ = f32[6,12,8,128]{3,2,1,0:T(8,128)S(1)} collective-permute-done((f32[6,12,8,128]{3,2,1,0:T(8,128)S(1)}, f32[6,12,8,128]{3,2,1,0:T(8,128)S(1)}, u32[]{:S(2)}, u32[]{:S(2)}) %collective-permute-start.4) | collective-permute-done | bytes 294944 | tf_op jit(solution)/shard_map/ppermute | solution.py:257
  26.4 0.0 collective-permute-done.5.refs_3_
  26.4 0.7 shard_map.52
  27.1 0.0 collective-permute-start.6
  27.1 2.9 %collective-permute-start.7 = (f32[12,12,8,128]{3,2,1,0:T(8,128)S(1)}, f32[12,12,8,128]{3,2,1,0:T(8,128)S(1)}, u32[]{:S(2)}, u32[]{:S(2)}) collective-permute-start(f32[12,12,8,128]{3,2,1,0:T(8,128)S(1)} %get-tuple-element.24.refs_0_.refs_2_), channel_id=1, source_target_pairs={{0,14},{2,0},{4,2},{6,4},{8,6},{10,8},{12,10},{14,12},{1,15},{3,1}... | collective-permute-start | bytes 1769480 | tf_op jit(solution)/shard_map/ppermute | solution.py:262
  30.1 0.0 collective-permute-start.8
  30.1 3.2 %collective-permute-start.9 = (f32[6,12,8,128]{3,2,1,0:T(8,128)S(1)}, f32[6,12,8,128]{3,2,1,0:T(8,128)S(1)}, u32[]{:S(2)}, u32[]{:S(2)}) collective-permute-start(f32[6,12,8,128]{3,2,1,0:T(8,128)S(1)} %get-tuple-element.26), channel_id=1, source_target_pairs={{0,224},{32,0},{64,32},{96,64},{128,96},{160,128},{192,160},{224,1... | collective-permute-start | bytes 884744 | tf_op jit(solution)/shard_map/ppermute | solution.py:258
  33.3 1.1 %shard_map.53.refs_1_ = f32[12,12,8,128]{3,2,1,0:T(8,128)S(1)} custom-call(f32[12,12,8,128]{3,2,1,0:T(8,128)S(1)} %get-tuple-element.24.refs_0_.refs_2_, f32[12,6,8,128]{3,2,1,0:T(8,128)S(1)} %get-tuple-element.21.refs_1_, f32[12,12,8,128]{3,2,1,0:T(8,128)S(1)} %get-tuple-element.20.refs_0_.refs_2_), custom_call_target="tpu_custom_call" | custom-call | flops 400000000 | bytes 2000000 | tf_op jit(solution)/shard_map/pallas_call | solution.py:32
  34.5 3.2 %collective-permute-done.6.refs_2_ = f32[12,12,8,128]{3,2,1,0:T(8,128)S(1)} collective-permute-done((f32[12,12,8,128]{3,2,1,0:T(8,128)S(1)}, f32[12,12,8,128]{3,2,1,0:T(8,128)S(1)}, u32[]{:S(2)}, u32[]{:S(2)}) %collective-permute-start.6) | collective-permute-done | bytes 589856 | tf_op jit(solution)/shard_map/ppermute | solution.py:262
  37.6 0.0 collective-permute-done.7.refs_3_
  37.6 0.8 shard_map.54.refs_1_
  38.5 0.5 collective-permute-done.8.refs_2_
  38.9 0.0 collective-permute-done.9.refs_3_
  38.9 0.7 shard_map.55
  39.7 0.3 collective-permute-start.10
  40.0 2.6 %collective-permute-start.11 = (f32[12,12,8,128]{3,2,1,0:T(8,128)S(1)}, f32[12,12,8,128]{3,2,1,0:T(8,128)S(1)}, u32[]{:S(2)}, u32[]{:S(2)}) collective-permute-start(f32[12,12,8,128]{3,2,1,0:T(8,128)S(1)} %get-tuple-element.27.refs_0_), channel_id=1, source_target_pairs={{0,14},{2,0},{4,2},{6,4},{8,6},{10,8},{12,10},{14,12},{1,15},{3,1}... | collective-permute-start | bytes 1769480 | tf_op jit(solution)/shard_map/ppermute | solution.py:262
  42.6 2.5 %collective-permute-start.12 = (f32[6,12,8,128]{3,2,1,0:T(8,128)S(1)}, f32[6,12,8,128]{3,2,1,0:T(8,128)S(1)}, u32[]{:S(2)}, u32[]{:S(2)}) collective-permute-start(f32[6,12,8,128]{3,2,1,0:T(8,128)S(1)} %get-tuple-element.28), channel_id=1, source_target_pairs={{0,32},{32,64},{64,96},{96,128},{128,160},{160,192},{192,224},{224... | collective-permute-start | bytes 884744 | tf_op jit(solution)/shard_map/ppermute | solution.py:257
  45.1 0.8 collective-permute-start.13
  45.9 1.1 %shard_map.56.refs_1_ = f32[12,12,8,128]{3,2,1,0:T(8,128)S(1)} custom-call(f32[12,12,8,128]{3,2,1,0:T(8,128)S(1)} %get-tuple-element.27.refs_0_, f32[12,6,8,128]{3,2,1,0:T(8,128)S(1)} %get-tuple-element.21.refs_1_, f32[12,12,8,128]{3,2,1,0:T(8,128)S(1)} %get-tuple-element.24.refs_0_.refs_2_), custom_call_target="tpu_custom_call" | custom-call | flops 400000000 | bytes 2000000 | tf_op jit(solution)/shard_map/pallas_call | solution.py:32
  47.0 3.2 %collective-permute-done.10.refs_2_ = f32[12,12,8,128]{3,2,1,0:T(8,128)S(1)} collective-permute-done((f32[12,12,8,128]{3,2,1,0:T(8,128)S(1)}, f32[12,12,8,128]{3,2,1,0:T(8,128)S(1)}, u32[]{:S(2)}, u32[]{:S(2)}) %collective-permute-start.10) | collective-permute-done | bytes 589856 | tf_op jit(solution)/shard_map/ppermute | solution.py:262
  50.2 0.0 collective-permute-done.11.refs_3_
  50.2 0.8 shard_map.57.refs_1_
  51.0 0.2 collective-permute-done.12.refs_2_
  51.2 1.0 collective-permute-done.13.refs_3_
  52.2 0.7 shard_map.58
  52.9 1.8 %collective-permute-start.17 = (f32[6,12,8,128]{3,2,1,0:T(8,128)S(1)}, f32[6,12,8,128]{3,2,1,0:T(8,128)S(1)}, u32[]{:S(2)}, u32[]{:S(2)}) collective-permute-start(f32[6,12,8,128]{3,2,1,0:T(8,128)S(1)} %get-tuple-element.31.high), channel_id=1, source_target_pairs={{0,32},{32,64},{64,96},{96,128},{128,160},{160,192},{192,224},{224... | collective-permute-start | bytes 884744 | tf_op jit(solution)/shard_map/ppermute | solution.py:257
  54.7 0.5 collective-permute-start.14
  55.2 1.5 %collective-permute-start.15 = (f32[12,12,8,128]{3,2,1,0:T(8,128)S(1)}, f32[12,12,8,128]{3,2,1,0:T(8,128)S(1)}, u32[]{:S(2)}, u32[]{:S(2)}) collective-permute-start(f32[12,12,8,128]{3,2,1,0:T(8,128)S(1)} %get-tuple-element.33.refs_0_), channel_id=1, source_target_pairs={{0,16},{16,1},{1,17},{17,0},{2,18},{18,3},{3,19},{19,2},{4,20},{20... | collective-permute-start | bytes 1769480 | tf_op jit(solution)/shard_map/ppermute | solution.py:284
  56.7 0.0 collective-permute-start.16
  56.7 5.7 %collective-permute-done.17.refs_2_ = f32[6,12,8,128]{3,2,1,0:T(8,128)S(1)} collective-permute-done((f32[6,12,8,128]{3,2,1,0:T(8,128)S(1)}, f32[6,12,8,128]{3,2,1,0:T(8,128)S(1)}, u32[]{:S(2)}, u32[]{:S(2)}) %collective-permute-start.17) | collective-permute-done | bytes 294944 | tf_op jit(solution)/shard_map/ppermute | solution.py:257
  62.4 1.9 %collective-permute-start.18 = (f32[12,12,8,128]{3,2,1,0:T(8,128)S(1)}, f32[12,12,8,128]{3,2,1,0:T(8,128)S(1)}, u32[]{:S(2)}, u32[]{:S(2)}) collective-permute-start(f32[12,12,8,128]{3,2,1,0:T(8,128)S(1)} %get-tuple-element.33.refs_0_), channel_id=1, source_target_pairs={{0,14},{2,0},{4,2},{6,4},{8,6},{10,8},{12,10},{14,12},{1,15},{3,1}... | collective-permute-start | bytes 1769480 | tf_op jit(solution)/shard_map/ppermute | solution.py:262
  64.4 2.2 %collective-permute-start.19 = (f32[6,12,8,128]{3,2,1,0:T(8,128)S(1)}, f32[6,12,8,128]{3,2,1,0:T(8,128)S(1)}, u32[]{:S(2)}, u32[]{:S(2)}) collective-permute-start(f32[6,12,8,128]{3,2,1,0:T(8,128)S(1)} %get-tuple-element.30.low), channel_id=1, source_target_pairs={{0,224},{32,0},{64,32},{96,64},{128,96},{160,128},{192,160},{224,1... | collective-permute-start | bytes 884744 | tf_op jit(solution)/shard_map/ppermute | solution.py:258
  66.6 3.2 %collective-permute-done.14.following = f32[12,12,8,128]{3,2,1,0:T(8,128)S(1)} collective-permute-done((f32[12,12,8,128]{3,2,1,0:T(8,128)S(1)}, f32[12,12,8,128]{3,2,1,0:T(8,128)S(1)}, u32[]{:S(2)}, u32[]{:S(2)}) %collective-permute-start.14) | collective-permute-done | bytes 589856 | tf_op jit(solution)/shard_map/ppermute | solution.py:283
  69.8 0.6 collective-permute-start.21
  70.4 0.0 collective-permute-done.15.preceding
  70.4 2.0 %collective-permute-start.20 = (f32[6,12,8,128]{3,2,1,0:T(8,128)S(1)}, f32[6,12,8,128]{3,2,1,0:T(8,128)S(1)}, u32[]{:S(2)}, u32[]{:S(2)}) collective-permute-start(f32[6,12,8,128]{3,2,1,0:T(8,128)S(1)} %slice.8), channel_id=1, source_target_pairs={{0,16},{16,1},{1,17},{17,0},{2,18},{18,3},{3,19},{19,2},{4,20},{20... | collective-permute-start | bytes 884744 | tf_op jit(solution)/shard_map/ppermute | solution.py:286
  72.4 1.0 shard_map.60.refs_1_
  73.4 1.4 %shard_map.59 = f32[1152,128]{1,0:T(8,128)} custom-call(s32[2]{0:T(128)S(1)} %pad_add_fusion.place, f32[6,12,8,128]{3,2,1,0:T(8,128)S(1)} %get-tuple-element.30.low, f32[6,12,8,128]{3,2,1,0:T(8,128)S(1)} %get-tuple-element.31.high, f32[12,12,8,128]{3,2,1,0:T(8,128)S(1)} %collective-permute-done.14.following, ...), custom_call_target="tpu_custom_call" | custom-call | flops 400000000 | bytes 2000000 | tf_op jit(solution)/shard_map/pallas_call | solution.py:32
  74.8 0.8 shard_map.61.refs_1_
  75.7 0.7 shard_map.62.applied
  76.4 1.5 %shard_map.63.near = f32[32,128]{1,0:T(8,128)S(1)} custom-call(f32[6,12,8,128]{3,2,1,0:T(8,128)S(1)} %get-tuple-element.30.low, f32[6,12,8,128]{3,2,1,0:T(8,128)S(1)} %get-tuple-element.31.high, f32[12,12,8,128]{3,2,1,0:T(8,128)S(1)} %shard_map.62.applied, f32[12,12,8,128]{3,2,1,0:T(8,128)S(1)} %collective-permute-done.14.following, ...), custom_call_target="tpu_custom_call" | custom-call | flops 400000000 | bytes 2000000 | tf_op jit(solution)/shard_map/pallas_call | solution.py:32
  77.9 0.5 collective-permute-done.21.far_low
  78.3 0.6 shard_map.64.far_part
  78.9 0.0 collective-permute-done.20.far_high
  78.9 1.3 %shard_map.65 = f32[16,16,128]{2,1,0:T(8,128)S(1)} custom-call(s32[2]{0:T(128)S(1)} %pad_add_fusion.place, f32[6,12,8,128]{3,2,1,0:T(8,128)S(1)} %get-tuple-element.30.low, f32[6,12,8,128]{3,2,1,0:T(8,128)S(1)} %get-tuple-element.31.high, f32[12,12,8,128]{3,2,1,0:T(8,128)S(1)} %shard_map.62.applied, f32[6,12,8,128]{3,2,1,0:T(8,128)S(1)} %collective-permute-done.20.far_high, ...), custom_call_target="tpu_custom_call" | custom-call | flops 1000000 | bytes 2000000 | tf_op jit(solution)/shard_map/pallas_call | solution.py:32
  80.2 14.1 %all_to_all.10.parts = f32[16,16,128]{2,1,0:T(8,128)S(1)} all-to-all(f32[16,16,128]{2,1,0:T(8,128)S(1)} %shard_map.65), channel_id=1, replica_groups=mesh['z'=8,'xl'=2,'y'=4,'core'=2,'xh'=2] {'xl','y','core'}, dimensions={0} | all-to-all | bytes 262144 | tf_op jit(solution)/shard_map/all_to_all | solution.py:316
  94.3 13.1 %all_to_all.11.parts = f32[8,32,128]{2,1,0:T(8,128)S(1)} all-to-all(f32[8,32,128]{2,1,0:T(8,128)S(1)} %shard_map.66), channel_id=1, replica_groups=mesh['z'=8,'xl'=2,'y'=4,'core'=2,'xh'=2] {'z'}, dimensions={0} | all-to-all | bytes 262144 | tf_op jit(solution)/shard_map/all_to_all | solution.py:318
  107.4 0.7 shard_map.67
  (12 shorter events, 0.1 us)
Async XLA Ops:
  0.6 10.4 %copy-start = (f32[32,1,6,6,128]{4,1,3,2,0:T(1,128)S(1)}, f32[32,1,6,6,128]{4,1,3,2,0:T(1,128)}, u32[]{:S(2)}) copy-start(f32[32,1,6,6,128]{4,1,3,2,0:T(1,128)} %param.2) | copy-start | bytes 1769476
  0.6 2.3 %copy-start.1 = (f32[1,6,6,128]{3,0,2,1:T(1,128)S(1)}, f32[1,6,6,128]{3,0,2,1:T(1,128)}, u32[]{:S(2)}) copy-start(f32[1,6,6,128]{3,0,2,1:T(1,128)} %param.3) | copy-start | bytes 55300
  1.7 9.3 %collective-permute-start = (f32[576,128]{1,0:T(8,128)S(1)}, f32[576,128]{1,0:T(8,128)S(1)}, u32[]{:S(2)}, u32[]{:S(2)}) collective-permute-start(f32[576,128]{1,0:T(8,128)S(1)} %constant_dynamic-slice_fusion), channel_id=1, source_target_pairs={{0,16},{16,0},{1,17},{17,1},{2,18},{18,2},{3,19},{19,3},{4,20},{20... | collective-permute-start | bytes 884744 | tf_op jit(solution)/shard_map/ppermute | solution.py:246
  3.1 7.9 %collective-permute-start.1 = (f32[36,128]{1,0:T(8,128)S(1)}, f32[36,128]{1,0:T(8,128)S(1)}, u32[]{:S(2)}, u32[]{:S(2)}) collective-permute-start(f32[36,128]{1,0:T(8,128)S(1)} %reshape.16.own_field), channel_id=1, source_target_pairs={{0,16},{16,0},{1,17},{17,1},{2,18},{18,2},{3,19},{19,3},{4,20},{20... | collective-permute-start | bytes 55304 | tf_op jit(solution)/shard_map/ppermute | solution.py:247
  11.6 10.5 %collective-permute-start.2 = (f32[12,12,8,128]{3,2,1,0:T(8,128)S(1)}, f32[12,12,8,128]{3,2,1,0:T(8,128)S(1)}, u32[]{:S(2)}, u32[]{:S(2)}) collective-permute-start(f32[12,12,8,128]{3,2,1,0:T(8,128)S(1)} %get-tuple-element.20.refs_0_.refs_2_), channel_id=1, source_target_pairs={{0,2},{2,4},{4,6},{6,8},{8,10},{10,12},{12,14},{14,0},{1,3},{3,5},... | collective-permute-start | bytes 1769480 | tf_op jit(solution)/shard_map/ppermute | solution.py:262
  11.7 10.5 %collective-permute-start.3 = (f32[12,12,8,128]{3,2,1,0:T(8,128)S(1)}, f32[12,12,8,128]{3,2,1,0:T(8,128)S(1)}, u32[]{:S(2)}, u32[]{:S(2)}) collective-permute-start(f32[12,12,8,128]{3,2,1,0:T(8,128)S(1)} %get-tuple-element.20.refs_0_.refs_2_), channel_id=1, source_target_pairs={{0,14},{2,0},{4,2},{6,4},{8,6},{10,8},{12,10},{14,12},{1,15},{3,1}... | collective-permute-start | bytes 1769480 | tf_op jit(solution)/shard_map/ppermute | solution.py:262
  14.6 11.8 %collective-permute-start.4 = (f32[6,12,8,128]{3,2,1,0:T(8,128)S(1)}, f32[6,12,8,128]{3,2,1,0:T(8,128)S(1)}, u32[]{:S(2)}, u32[]{:S(2)}) collective-permute-start(f32[6,12,8,128]{3,2,1,0:T(8,128)S(1)} %get-tuple-element.22), channel_id=1, source_target_pairs={{0,32},{32,64},{64,96},{96,128},{128,160},{160,192},{192,224},{224... | collective-permute-start | bytes 884744 | tf_op jit(solution)/shard_map/ppermute | solution.py:257
  16.5 9.8 %collective-permute-start.5 = (f32[6,12,8,128]{3,2,1,0:T(8,128)S(1)}, f32[6,12,8,128]{3,2,1,0:T(8,128)S(1)}, u32[]{:S(2)}, u32[]{:S(2)}) collective-permute-start(f32[6,12,8,128]{3,2,1,0:T(8,128)S(1)} %get-tuple-element.23), channel_id=1, source_target_pairs={{0,224},{32,0},{64,32},{96,64},{128,96},{160,128},{192,160},{224,1... | collective-permute-start | bytes 884744 | tf_op jit(solution)/shard_map/ppermute | solution.py:258
  27.1 10.5 %collective-permute-start.6 = (f32[12,12,8,128]{3,2,1,0:T(8,128)S(1)}, f32[12,12,8,128]{3,2,1,0:T(8,128)S(1)}, u32[]{:S(2)}, u32[]{:S(2)}) collective-permute-start(f32[12,12,8,128]{3,2,1,0:T(8,128)S(1)} %get-tuple-element.24.refs_0_.refs_2_), channel_id=1, source_target_pairs={{0,2},{2,4},{4,6},{6,8},{8,10},{10,12},{12,14},{14,0},{1,3},{3,5},... | collective-permute-start | bytes 1769480 | tf_op jit(solution)/shard_map/ppermute | solution.py:262
  27.1 10.5 %collective-permute-start.7 = (f32[12,12,8,128]{3,2,1,0:T(8,128)S(1)}, f32[12,12,8,128]{3,2,1,0:T(8,128)S(1)}, u32[]{:S(2)}, u32[]{:S(2)}) collective-permute-start(f32[12,12,8,128]{3,2,1,0:T(8,128)S(1)} %get-tuple-element.24.refs_0_.refs_2_), channel_id=1, source_target_pairs={{0,14},{2,0},{4,2},{6,4},{8,6},{10,8},{12,10},{14,12},{1,15},{3,1}... | collective-permute-start | bytes 1769480 | tf_op jit(solution)/shard_map/ppermute | solution.py:262
  30.1 8.9 %collective-permute-start.8 = (f32[6,12,8,128]{3,2,1,0:T(8,128)S(1)}, f32[6,12,8,128]{3,2,1,0:T(8,128)S(1)}, u32[]{:S(2)}, u32[]{:S(2)}) collective-permute-start(f32[6,12,8,128]{3,2,1,0:T(8,128)S(1)} %get-tuple-element.25), channel_id=1, source_target_pairs={{0,32},{32,64},{64,96},{96,128},{128,160},{160,192},{192,224},{224... | collective-permute-start | bytes 884744 | tf_op jit(solution)/shard_map/ppermute | solution.py:257
  30.1 8.9 %collective-permute-start.9 = (f32[6,12,8,128]{3,2,1,0:T(8,128)S(1)}, f32[6,12,8,128]{3,2,1,0:T(8,128)S(1)}, u32[]{:S(2)}, u32[]{:S(2)}) collective-permute-start(f32[6,12,8,128]{3,2,1,0:T(8,128)S(1)} %get-tuple-element.26), channel_id=1, source_target_pairs={{0,224},{32,0},{64,32},{96,64},{128,96},{160,128},{192,160},{224,1... | collective-permute-start | bytes 884744 | tf_op jit(solution)/shard_map/ppermute | solution.py:258
  39.7 10.5 %collective-permute-start.10 = (f32[12,12,8,128]{3,2,1,0:T(8,128)S(1)}, f32[12,12,8,128]{3,2,1,0:T(8,128)S(1)}, u32[]{:S(2)}, u32[]{:S(2)}) collective-permute-start(f32[12,12,8,128]{3,2,1,0:T(8,128)S(1)} %get-tuple-element.27.refs_0_), channel_id=1, source_target_pairs={{0,2},{2,4},{4,6},{6,8},{8,10},{10,12},{12,14},{14,0},{1,3},{3,5},... | collective-permute-start | bytes 1769480 | tf_op jit(solution)/shard_map/ppermute | solution.py:262
  40.0 10.2 %collective-permute-start.11 = (f32[12,12,8,128]{3,2,1,0:T(8,128)S(1)}, f32[12,12,8,128]{3,2,1,0:T(8,128)S(1)}, u32[]{:S(2)}, u32[]{:S(2)}) collective-permute-start(f32[12,12,8,128]{3,2,1,0:T(8,128)S(1)} %get-tuple-element.27.refs_0_), channel_id=1, source_target_pairs={{0,14},{2,0},{4,2},{6,4},{8,6},{10,8},{12,10},{14,12},{1,15},{3,1}... | collective-permute-start | bytes 1769480 | tf_op jit(solution)/shard_map/ppermute | solution.py:262
  42.6 8.6 %collective-permute-start.12 = (f32[6,12,8,128]{3,2,1,0:T(8,128)S(1)}, f32[6,12,8,128]{3,2,1,0:T(8,128)S(1)}, u32[]{:S(2)}, u32[]{:S(2)}) collective-permute-start(f32[6,12,8,128]{3,2,1,0:T(8,128)S(1)} %get-tuple-element.28), channel_id=1, source_target_pairs={{0,32},{32,64},{64,96},{96,128},{128,160},{160,192},{192,224},{224... | collective-permute-start | bytes 884744 | tf_op jit(solution)/shard_map/ppermute | solution.py:257
  45.1 7.1 %collective-permute-start.13 = (f32[6,12,8,128]{3,2,1,0:T(8,128)S(1)}, f32[6,12,8,128]{3,2,1,0:T(8,128)S(1)}, u32[]{:S(2)}, u32[]{:S(2)}) collective-permute-start(f32[6,12,8,128]{3,2,1,0:T(8,128)S(1)} %get-tuple-element.29), channel_id=1, source_target_pairs={{0,224},{32,0},{64,32},{96,64},{128,96},{160,128},{192,160},{224,1... | collective-permute-start | bytes 884744 | tf_op jit(solution)/shard_map/ppermute | solution.py:258
  52.9 9.6 %collective-permute-start.17 = (f32[6,12,8,128]{3,2,1,0:T(8,128)S(1)}, f32[6,12,8,128]{3,2,1,0:T(8,128)S(1)}, u32[]{:S(2)}, u32[]{:S(2)}) collective-permute-start(f32[6,12,8,128]{3,2,1,0:T(8,128)S(1)} %get-tuple-element.31.high), channel_id=1, source_target_pairs={{0,32},{32,64},{64,96},{96,128},{128,160},{160,192},{192,224},{224... | collective-permute-start | bytes 884744 | tf_op jit(solution)/shard_map/ppermute | solution.py:257
  54.7 15.0 %collective-permute-start.14 = (f32[12,12,8,128]{3,2,1,0:T(8,128)S(1)}, f32[12,12,8,128]{3,2,1,0:T(8,128)S(1)}, u32[]{:S(2)}, u32[]{:S(2)}) collective-permute-start(f32[12,12,8,128]{3,2,1,0:T(8,128)S(1)} %get-tuple-element.33.refs_0_), channel_id=1, source_target_pairs={{0,17},{16,0},{1,16},{17,1},{2,19},{18,2},{3,18},{19,3},{4,21},{20... | collective-permute-start | bytes 1769480 | tf_op jit(solution)/shard_map/ppermute | solution.py:283
  55.2 15.1 %collective-permute-start.15 = (f32[12,12,8,128]{3,2,1,0:T(8,128)S(1)}, f32[12,12,8,128]{3,2,1,0:T(8,128)S(1)}, u32[]{:S(2)}, u32[]{:S(2)}) collective-permute-start(f32[12,12,8,128]{3,2,1,0:T(8,128)S(1)} %get-tuple-element.33.refs_0_), channel_id=1, source_target_pairs={{0,16},{16,1},{1,17},{17,0},{2,18},{18,3},{3,19},{19,2},{4,20},{20... | collective-permute-start | bytes 1769480 | tf_op jit(solution)/shard_map/ppermute | solution.py:284
  56.7 18.1 %collective-permute-start.16 = (f32[12,12,8,128]{3,2,1,0:T(8,128)S(1)}, f32[12,12,8,128]{3,2,1,0:T(8,128)S(1)}, u32[]{:S(2)}, u32[]{:S(2)}) collective-permute-start(f32[12,12,8,128]{3,2,1,0:T(8,128)S(1)} %get-tuple-element.33.refs_0_), channel_id=1, source_target_pairs={{0,2},{2,4},{4,6},{6,8},{8,10},{10,12},{12,14},{14,0},{1,3},{3,5},... | collective-permute-start | bytes 1769480 | tf_op jit(solution)/shard_map/ppermute | solution.py:262
  62.4 12.4 %collective-permute-start.18 = (f32[12,12,8,128]{3,2,1,0:T(8,128)S(1)}, f32[12,12,8,128]{3,2,1,0:T(8,128)S(1)}, u32[]{:S(2)}, u32[]{:S(2)}) collective-permute-start(f32[12,12,8,128]{3,2,1,0:T(8,128)S(1)} %get-tuple-element.33.refs_0_), channel_id=1, source_target_pairs={{0,14},{2,0},{4,2},{6,4},{8,6},{10,8},{12,10},{14,12},{1,15},{3,1}... | collective-permute-start | bytes 1769480 | tf_op jit(solution)/shard_map/ppermute | solution.py:262
  64.4 11.3 %collective-permute-start.19 = (f32[6,12,8,128]{3,2,1,0:T(8,128)S(1)}, f32[6,12,8,128]{3,2,1,0:T(8,128)S(1)}, u32[]{:S(2)}, u32[]{:S(2)}) collective-permute-start(f32[6,12,8,128]{3,2,1,0:T(8,128)S(1)} %get-tuple-element.30.low), channel_id=1, source_target_pairs={{0,224},{32,0},{64,32},{96,64},{128,96},{160,128},{192,160},{224,1... | collective-permute-start | bytes 884744 | tf_op jit(solution)/shard_map/ppermute | solution.py:258
  69.8 8.6 %collective-permute-start.21 = (f32[6,12,8,128]{3,2,1,0:T(8,128)S(1)}, f32[6,12,8,128]{3,2,1,0:T(8,128)S(1)}, u32[]{:S(2)}, u32[]{:S(2)}) collective-permute-start(f32[6,12,8,128]{3,2,1,0:T(8,128)S(1)} %slice.9), channel_id=1, source_target_pairs={{0,17},{16,0},{1,16},{17,1},{2,19},{18,2},{3,18},{19,3},{4,21},{20... | collective-permute-start | bytes 884744 | tf_op jit(solution)/shard_map/ppermute | solution.py:285
  70.4 8.5 %collective-permute-start.20 = (f32[6,12,8,128]{3,2,1,0:T(8,128)S(1)}, f32[6,12,8,128]{3,2,1,0:T(8,128)S(1)}, u32[]{:S(2)}, u32[]{:S(2)}) collective-permute-start(f32[6,12,8,128]{3,2,1,0:T(8,128)S(1)} %slice.8), channel_id=1, source_target_pairs={{0,16},{16,1},{1,17},{17,0},{2,18},{18,3},{3,19},{19,2},{4,20},{20... | collective-permute-start | bytes 884744 | tf_op jit(solution)/shard_map/ppermute | solution.py:286

commit v8 on v7

--- a/solution.py
+++ b/solution.py
@@ -40,22 +40,20 @@
     )(*inputs)
 
 
-def assemble_body(place, mine, received, own_field, other_field, full, low, high, field):
+def assemble_body(place, keep, received, own_field, other_field, full, field):
     first = place[0] == 0
     for xi in range(6):
         for yi in range(6):
             r = xi * 6 + yi
             for g in range(2):
                 rows = pl.ds(g * 288 + r, 8, stride=36)
-                a = jnp.where(first, mine[rows, :], mine[pl.ds(576 + g * 288 + r, 8, stride=36), :])
+                a = keep[rows, :]
                 b = received[rows, :]
                 n = yi * 2 + g
                 left = jnp.where(first, a, b)
                 right = jnp.where(first, b, a)
                 full[xi, n] = left
-                low[xi, n] = left
                 full[6 + xi, n] = right
-                high[xi, n] = right
             a = jnp.broadcast_to(own_field[pl.ds(r, 1), :], (8, 128))
             b = jnp.broadcast_to(other_field[pl.ds(r, 1), :], (8, 128))
             field[xi, yi] = jnp.where(first, a, b)
@@ -132,6 +130,51 @@
                 halves[x // 6][x % 6, n] = total
 
 
+def first_edge_body(alpha, inside, place, acc, keep_y, got_y, keep_x, got_x, full, low, high):
+    scaled = [-0.5 * alpha * w for w in weights]
+    from_x = [[inside[i] * F32(s) for s in scaled] for i in range(2)]
+    from_y = [[inside[2 + i] * F32(s) for s in scaled] for i in range(2)]
+
+    def with_order(first):
+        before_x, after_x = (got_x, keep_x) if first else (keep_x, got_x)
+
+        def rows(ref, xi, yi, g):
+            return ref[pl.ds(g * 288 + xi * 6 + yi, 8, stride=36), :]
+
+        for x in range(12):
+            source = keep_y if (x < 6) == first else got_y
+            for g in range(2):
+                lows = [rows(source[0], x % 6, j, g) for j in range(6)]
+                highs = [rows(source[1], x % 6, j, g) for j in range(6)]
+                for yi in range(6):
+                    n = yi * 2 + g
+                    total = acc[x, n]
+                    for k in range(yi + 1, 7):
+                        total = total + from_y[0][k] * lows[6 + yi - k]
+                    for k in range(6 - yi, 7):
+                        total = total + from_y[1][k] * highs[yi + k - 6]
+                    full[x, n] = total
+        for g in range(2):
+            for yi in range(6):
+                n = yi * 2 + g
+                lows = [rows(before_x, j, yi, g) for j in range(6)]
+                highs = [rows(after_x, j, yi, g) for j in range(6)]
+                for x in range(6):
+                    total = full[x, n]
+                    for k in range(x + 1, 7):
+                        total = total + from_x[0][k] * lows[6 + x - k]
+                    full[x, n] = total
+                    low[x, n] = total
+                    total = full[11 - x, n]
+                    for k in range(x + 1, 7):
+                        total = total + from_x[1][k] * highs[k - x - 1]
+                    full[11 - x, n] = total
+                    high[5 - x, n] = total
+
+    pl.when(place[0] == 0)(lambda: with_order(True))
+    pl.when(place[0] != 0)(lambda: with_order(False))
+
+
 def bricks_body(place, low, high, following, preceding, out, rows, sem):
     first = place[0] == 0
     for xi in range(6):
@@ -243,13 +286,41 @@
 
     mine = orbitals.reshape(1152, 128)
     own_field = potential.reshape(36, 128)
+    keep = lax.dynamic_slice_in_dim(mine, side * 576, 576)
     received = lax.ppermute(lax.dynamic_slice_in_dim(mine, (1 - side) * 576, 576), "xl", SWAP)
     other_field = lax.ppermute(own_field, "xl", SWAP)
-    full, low, high, field = call(
+
+    def first_halos(values, way):
+        along_x = [((z, s), ((z + (2 * s - 1) * way) % 8, s)) for z in range(8) for s in range(2)]
+        along_x = [(2 * a + b, 2 * c + d) for (a, b), (c, d) in along_x]
+        return (
+            lax.ppermute(values, ("z", "xl"), along_x),
+            lax.ppermute(values, ROWS, UP),
+            lax.ppermute(values, ROWS, DOWN),
+        )
+
+    keep_x, *keep_y = first_halos(keep, 1)
+    got_x, *got_y = first_halos(received, -1)
+    full, field = call(
         assemble_body,
-        [FULL, HALF, HALF, jax.ShapeDtypeStruct((12, 6, 8, 128), F32)],
-        [place, mine, received, own_field, other_field],
+        [FULL, jax.ShapeDtypeStruct((12, 6, 8, 128), F32)],
+        [place, keep, received, own_field, other_field],
         [SM] + [VM] * 4,
+    )
+
+    def first_interior(*refs):
+        interior_body(*first, *refs)
+
+    def first_edge(inside, place, acc, a, b, c, d, e, f, *outs):
+        first_edge_body(first[0], inside, place, acc, (a, b), (c, d), e, f, *outs)
+
+    acc = call(first_interior, FULL, [full, field], flops=400_000_000)
+    y0 = (full,)
+    y1 = call(
+        first_edge,
+        [FULL, HALF, HALF],
+        [inside, place, acc, *keep_y, *got_y, keep_x, got_x],
+        [SM, SM] + [VM] * 7,
     )
 
     def step(numbers, planes, previous, outs, last=False):
@@ -275,8 +346,6 @@
         acc = call(edge_y, FULL, [inside, acc, *halos[:2]], [SM] + [VM] * 3, flops=200_000_000)
         return call(edge_x, outs, [inside, acc, *halos[2:]], [SM] + [VM] * 3)
 
-    y0 = (full, low, high)
-    y1 = step(first, y0, (), [FULL, HALF, HALF])
     y2 = step(second, y1, (y0[0],), [FULL, HALF, HALF])
     y3 = step(third, y2, (y1[0],), [FULL, HALF, HALF])
     full, low, high = y3

time: 109 us -> 105 us (0.963)
  starting transfers between devices: 34 us -> 30.4 us
  waiting for transfers between devices: 28.3 us -> 27 us
  blocking collectives: 27.1 us -> 28.2 us
    ppermute x0 -> x6, starting transfers between devices: none -> 10.6 us  [the longest x2 7.61 us: first_halos(): lax.ppermute(values, ('z', 'xl'), along_x)]
    ppermute x1, waiting for transfers between devices: 6.93 us -> 0.1 us  [local(): other_field = lax.ppermute(own_field, 'xl', SWAP)]
    ppermute x0 -> x6, waiting for transfers between devices: none -> 6.8 us  [the longest x2 5.19 us: first_halos(): lax.ppermute(values, ('z', 'xl'), along_x)]
    ppermute x4 -> x3, waiting for transfers between devices: 0.01 us -> 6.04 us  [step(): lax.ppermute(later, ROWS, DOWN)]
    ppermute x4 -> x3, starting transfers between devices: 10.5 us -> 4.91 us  [step(): lax.ppermute(later, ROWS, DOWN)]
    ppermute x4 -> x3, waiting for transfers between devices: 9.73 us -> 4.97 us  [step(): before_x = lax.ppermute(high, 'z', UP)]
    ppermute x4 -> x3, starting transfers between devices: 6.2 us -> 2.08 us  [step(): before_x = lax.ppermute(high, 'z', UP)]
    ppermute x4 -> x3, starting transfers between devices: 10.1 us -> 7.21 us  [step(): after_x = lax.ppermute(low, 'z', DOWN)]
  transfers between devices with their start and end apart: 22 -> 24, of which waited for: 11 -> 10; matrix products, arithmetic and copies ran while one was open for 0% -> 0% of each run, Pallas kernels for 11% -> 11%
where the time goes in v8:
time: 105 us; the launch traced here: 104 us
  starting transfers between devices  30.4 us (29%)
  blocking collectives  28.2 us (27%)
  waiting for transfers between devices  27 us (26%)
  Pallas kernels  16 us (15%)
  local copies, waits for them, and re-layouts  1.14 us (1%)
    pallas_call x18, Pallas kernels, call(): pl.pallas_call(body, out_shape=outs, in_specs=specs or [VM] * len(inputs)...  16 us
    all_to_all x1, blocking collectives, local(): lax.all_to_all(copies, ('xl',) + ROWS, split_axis=0, concat_axis=0, tiled...  14.2 us
    all_to_all x1, blocking collectives, local(): parts = lax.all_to_all(copies, 'z', split_axis=0, concat_axis=0, tiled=True)  14 us
    ppermute x2, starting transfers between devices, first_halos(): lax.ppermute(values, ('z', 'xl'), along_x)  7.61 us
    ppermute x3, starting transfers between devices, step(): after_x = lax.ppermute(low, 'z', DOWN)  7.21 us
    ppermute x3, waiting for transfers between devices, step(): lax.ppermute(full, ROWS, UP)  6.24 us
    ppermute x3, waiting for transfers between devices, step(): lax.ppermute(later, ROWS, DOWN)  6.04 us
    ppermute x2, waiting for transfers between devices, first_halos(): lax.ppermute(values, ('z', 'xl'), along_x)  5.19 us
  transfers between devices with their start and end apart: 24, of which 10 were waited for; matrix products, arithmetic and copies ran while one was open for 0% of the time, Pallas kernels for 11%

profile of v8, /device:TPU:4, one launch (start us, length us, event | category | flops | bytes accessed | tf_op | source)
XLA Modules:
  0.0 103.8 jit_solution(17963452730490610993)
XLA Ops:
  0.6 1.1 %constant_dynamic-slice_fusion = (f32[576,128]{1,0:T(8,128)S(1)}, f32[576,128]{1,0:T(8,128)S(1)}) fusion(f32[1152,128]{1,0:T(8,128)} %bitcast.9, s32[]{:T(128)S(6)} %select_n.7, s32[]{:T(128)S(6)} %select_n.6), kind=kLoop, calls=%fused_computation.2 | loop fusion | bytes 1179656 | tf_op jit(solution)/shard_map/dynamic_slice | solution.py:290
  1.7 1.3 %collective-permute-start = (f32[576,128]{1,0:T(8,128)S(1)}, f32[576,128]{1,0:T(8,128)S(1)}, u32[]{:S(2)}, u32[]{:S(2)}) collective-permute-start(f32[576,128]{1,0:T(8,128)S(1)} %get-tuple-element.39), channel_id=1, source_target_pairs={{0,16},{16,0},{1,17},{17,1},{2,18},{18,2},{3,19},{19,3},{4,20},{20... | collective-permute-start | bytes 884744 | tf_op jit(solution)/shard_map/ppermute | solution.py:290
  3.0 5.9 %collective-permute-start.6 = (f32[576,128]{1,0:T(8,128)S(1)}, f32[576,128]{1,0:T(8,128)S(1)}, u32[]{:S(2)}, u32[]{:S(2)}) collective-permute-start(f32[576,128]{1,0:T(8,128)S(1)} %get-tuple-element.40.keep), channel_id=1, source_target_pairs={{0,224},{16,48},{32,0},{48,80},{64,32},{80,112},{96,64},{112,144},... | collective-permute-start | bytes 884744 | tf_op jit(solution)/shard_map/ppermute | solution.py:297
  9.0 0.1 collective-permute-start.1
  9.1 1.9 %collective-permute-start.3 = (f32[576,128]{1,0:T(8,128)S(1)}, f32[576,128]{1,0:T(8,128)S(1)}, u32[]{:S(2)}, u32[]{:S(2)}) collective-permute-start(f32[576,128]{1,0:T(8,128)S(1)} %get-tuple-element.40.keep), channel_id=1, source_target_pairs={{0,14},{2,0},{4,2},{6,4},{8,6},{10,8},{12,10},{14,12},{1,15},{3,1}... | collective-permute-start | bytes 884744 | tf_op jit(solution)/shard_map/ppermute | solution.py:299
  11.0 0.0 collective-permute-done.received
  11.0 1.8 %collective-permute-start.7 = (f32[576,128]{1,0:T(8,128)S(1)}, f32[576,128]{1,0:T(8,128)S(1)}, u32[]{:S(2)}, u32[]{:S(2)}) collective-permute-start(f32[576,128]{1,0:T(8,128)S(1)} %collective-permute-done.received), channel_id=1, source_target_pairs={{0,32},{16,240},{32,64},{48,16},{64,96},{80,48},{96,128},{112,80},... | collective-permute-start | bytes 884744 | tf_op jit(solution)/shard_map/ppermute | solution.py:297
  12.7 0.1 collective-permute-done.1.other_field
  12.8 1.1 %collective-permute-start.5 = (f32[576,128]{1,0:T(8,128)S(1)}, f32[576,128]{1,0:T(8,128)S(1)}, u32[]{:S(2)}, u32[]{:S(2)}) collective-permute-start(f32[576,128]{1,0:T(8,128)S(1)} %collective-permute-done.received), channel_id=1, source_target_pairs={{0,14},{2,0},{4,2},{6,4},{8,6},{10,8},{12,10},{14,12},{1,15},{3,1}... | collective-permute-start | bytes 884744 | tf_op jit(solution)/shard_map/ppermute | solution.py:299
  13.9 0.9 collective-permute-done.6.e
  14.9 0.1 pad_add_fusion.place
  15.0 0.1 add_convert_fusion.inside.refs_0_
  15.0 0.6 shard_map.49
  15.6 1.1 %shard_map.50.acc = f32[12,12,8,128]{3,2,1,0:T(8,128)S(1)} custom-call(f32[12,12,8,128]{3,2,1,0:T(8,128)S(1)} %get-tuple-element.18.refs_0_.refs_2_, f32[12,6,8,128]{3,2,1,0:T(8,128)S(1)} %get-tuple-element.19.refs_1_), custom_call_target="tpu_custom_call" | custom-call | flops 400000000 | bytes 2000000 | tf_op jit(solution)/shard_map/pallas_call | solution.py:32
  16.7 1.6 %collective-permute-done.2.a = f32[576,128]{1,0:T(8,128)S(1)} collective-permute-done((f32[576,128]{1,0:T(8,128)S(1)}, f32[576,128]{1,0:T(8,128)S(1)}, u32[]{:S(2)}, u32[]{:S(2)}) %collective-permute-start.2) | collective-permute-done | bytes 294944 | tf_op jit(solution)/shard_map/ppermute | solution.py:298
  18.3 4.3 %collective-permute-done.7.f = f32[576,128]{1,0:T(8,128)S(1)} collective-permute-done((f32[576,128]{1,0:T(8,128)S(1)}, f32[576,128]{1,0:T(8,128)S(1)}, u32[]{:S(2)}, u32[]{:S(2)}) %collective-permute-start.7) | collective-permute-done | bytes 294944 | tf_op jit(solution)/shard_map/ppermute | solution.py:297
  22.6 0.0 collective-permute-done.5.d
  22.6 0.0 collective-permute-done.4.c
  22.6 1.0 shard_map.51
  23.6 0.7 collective-permute-start.9
  24.3 0.3 collective-permute-start.10
  24.6 2.9 %collective-permute-start.11 = (f32[6,12,8,128]{3,2,1,0:T(8,128)S(1)}, f32[6,12,8,128]{3,2,1,0:T(8,128)S(1)}, u32[]{:S(2)}, u32[]{:S(2)}) collective-permute-start(f32[6,12,8,128]{3,2,1,0:T(8,128)S(1)} %get-tuple-element.22), channel_id=1, source_target_pairs={{0,224},{32,0},{64,32},{96,64},{128,96},{160,128},{192,160},{224,1... | collective-permute-start | bytes 884744 | tf_op jit(solution)/shard_map/ppermute | solution.py:329
  27.5 1.1 %shard_map.52.refs_1_ = f32[12,12,8,128]{3,2,1,0:T(8,128)S(1)} custom-call(f32[12,12,8,128]{3,2,1,0:T(8,128)S(1)} %get-tuple-element.20.refs_0_.refs_2_, f32[12,6,8,128]{3,2,1,0:T(8,128)S(1)} %get-tuple-element.19.refs_1_, f32[12,12,8,128]{3,2,1,0:T(8,128)S(1)} %get-tuple-element.18.refs_0_.refs_2_), custom_call_target="tpu_custom_call" | custom-call | flops 400000000 | bytes 2000000 | tf_op jit(solution)/shard_map/pallas_call | solution.py:32
  28.7 3.0 %collective-permute-done.9.refs_3_ = f32[12,12,8,128]{3,2,1,0:T(8,128)S(1)} collective-permute-done((f32[12,12,8,128]{3,2,1,0:T(8,128)S(1)}, f32[12,12,8,128]{3,2,1,0:T(8,128)S(1)}, u32[]{:S(2)}, u32[]{:S(2)}) %collective-permute-start.9) | collective-permute-done | bytes 589856 | tf_op jit(solution)/shard_map/ppermute | solution.py:333
  31.7 3.1 %collective-permute-done.8.refs_2_ = f32[12,12,8,128]{3,2,1,0:T(8,128)S(1)} collective-permute-done((f32[12,12,8,128]{3,2,1,0:T(8,128)S(1)}, f32[12,12,8,128]{3,2,1,0:T(8,128)S(1)}, u32[]{:S(2)}, u32[]{:S(2)}) %collective-permute-start.8) | collective-permute-done | bytes 589856 | tf_op jit(solution)/shard_map/ppermute | solution.py:333
  34.8 0.8 shard_map.53.refs_1_
  35.6 0.0 collective-permute-done.10.refs_2_
  35.7 0.0 collective-permute-done.11.refs_3_
  35.7 0.7 shard_map.54
  36.4 1.5 %collective-permute-start.13 = (f32[12,12,8,128]{3,2,1,0:T(8,128)S(1)}, f32[12,12,8,128]{3,2,1,0:T(8,128)S(1)}, u32[]{:S(2)}, u32[]{:S(2)}) collective-permute-start(f32[12,12,8,128]{3,2,1,0:T(8,128)S(1)} %get-tuple-element.23.refs_0_), channel_id=1, source_target_pairs={{0,14},{2,0},{4,2},{6,4},{8,6},{10,8},{12,10},{14,12},{1,15},{3,1}... | collective-permute-start | bytes 1769480 | tf_op jit(solution)/shard_map/ppermute | solution.py:333
  37.9 0.0 collective-permute-start.12
  37.9 0.5 collective-permute-start.14
  38.4 2.7 %collective-permute-start.15 = (f32[6,12,8,128]{3,2,1,0:T(8,128)S(1)}, f32[6,12,8,128]{3,2,1,0:T(8,128)S(1)}, u32[]{:S(2)}, u32[]{:S(2)}) collective-permute-start(f32[6,12,8,128]{3,2,1,0:T(8,128)S(1)} %get-tuple-element.25), channel_id=1, source_target_pairs={{0,224},{32,0},{64,32},{96,64},{128,96},{160,128},{192,160},{224,1... | collective-permute-start | bytes 884744 | tf_op jit(solution)/shard_map/ppermute | solution.py:329
  41.1 1.1 %shard_map.55.refs_1_ = f32[12,12,8,128]{3,2,1,0:T(8,128)S(1)} custom-call(f32[12,12,8,128]{3,2,1,0:T(8,128)S(1)} %get-tuple-element.23.refs_0_, f32[12,6,8,128]{3,2,1,0:T(8,128)S(1)} %get-tuple-element.19.refs_1_, f32[12,12,8,128]{3,2,1,0:T(8,128)S(1)} %get-tuple-element.20.refs_0_.refs_2_), custom_call_target="tpu_custom_call" | custom-call | flops 400000000 | bytes 2000000 | tf_op jit(solution)/shard_map/pallas_call | solution.py:32
  42.3 3.0 %collective-permute-done.13.refs_3_ = f32[12,12,8,128]{3,2,1,0:T(8,128)S(1)} collective-permute-done((f32[12,12,8,128]{3,2,1,0:T(8,128)S(1)}, f32[12,12,8,128]{3,2,1,0:T(8,128)S(1)}, u32[]{:S(2)}, u32[]{:S(2)}) %collective-permute-start.13) | collective-permute-done | bytes 589856 | tf_op jit(solution)/shard_map/ppermute | solution.py:333
  45.3 3.1 %collective-permute-done.12.refs_2_ = f32[12,12,8,128]{3,2,1,0:T(8,128)S(1)} collective-permute-done((f32[12,12,8,128]{3,2,1,0:T(8,128)S(1)}, f32[12,12,8,128]{3,2,1,0:T(8,128)S(1)}, u32[]{:S(2)}, u32[]{:S(2)}) %collective-permute-start.12) | collective-permute-done | bytes 589856 | tf_op jit(solution)/shard_map/ppermute | solution.py:333
  48.4 0.8 shard_map.56.refs_1_
  49.2 0.0 collective-permute-done.14.refs_2_
  49.3 0.7 shard_map.57
  50.0 1.3 %collective-permute-start.19 = (f32[6,12,8,128]{3,2,1,0:T(8,128)S(1)}, f32[6,12,8,128]{3,2,1,0:T(8,128)S(1)}, u32[]{:S(2)}, u32[]{:S(2)}) collective-permute-start(f32[6,12,8,128]{3,2,1,0:T(8,128)S(1)} %get-tuple-element.27.high), channel_id=1, source_target_pairs={{0,32},{32,64},{64,96},{96,128},{128,160},{160,192},{192,224},{224... | collective-permute-start | bytes 884744 | tf_op jit(solution)/shard_map/ppermute | solution.py:328
  51.3 0.3 collective-permute-start.16
  51.6 1.7 %collective-permute-start.17 = (f32[12,12,8,128]{3,2,1,0:T(8,128)S(1)}, f32[12,12,8,128]{3,2,1,0:T(8,128)S(1)}, u32[]{:S(2)}, u32[]{:S(2)}) collective-permute-start(f32[12,12,8,128]{3,2,1,0:T(8,128)S(1)} %get-tuple-element.29.refs_0_), channel_id=1, source_target_pairs={{0,16},{16,1},{1,17},{17,0},{2,18},{18,3},{3,19},{19,2},{4,20},{20... | collective-permute-start | bytes 1769480 | tf_op jit(solution)/shard_map/ppermute | solution.py:353
  53.3 0.0 collective-permute-start.18
  53.3 5.0 %collective-permute-done.19.refs_2_ = f32[6,12,8,128]{3,2,1,0:T(8,128)S(1)} collective-permute-done((f32[6,12,8,128]{3,2,1,0:T(8,128)S(1)}, f32[6,12,8,128]{3,2,1,0:T(8,128)S(1)}, u32[]{:S(2)}, u32[]{:S(2)}) %collective-permute-start.19) | collective-permute-done | bytes 294944 | tf_op jit(solution)/shard_map/ppermute | solution.py:328
  58.2 2.7 %collective-permute-start.20 = (f32[12,12,8,128]{3,2,1,0:T(8,128)S(1)}, f32[12,12,8,128]{3,2,1,0:T(8,128)S(1)}, u32[]{:S(2)}, u32[]{:S(2)}) collective-permute-start(f32[12,12,8,128]{3,2,1,0:T(8,128)S(1)} %get-tuple-element.29.refs_0_), channel_id=1, source_target_pairs={{0,14},{2,0},{4,2},{6,4},{8,6},{10,8},{12,10},{14,12},{1,15},{3,1}... | collective-permute-start | bytes 1769480 | tf_op jit(solution)/shard_map/ppermute | solution.py:333
  60.9 1.5 %collective-permute-start.21 = (f32[6,12,8,128]{3,2,1,0:T(8,128)S(1)}, f32[6,12,8,128]{3,2,1,0:T(8,128)S(1)}, u32[]{:S(2)}, u32[]{:S(2)}) collective-permute-start(f32[6,12,8,128]{3,2,1,0:T(8,128)S(1)} %get-tuple-element.26.low), channel_id=1, source_target_pairs={{0,224},{32,0},{64,32},{96,64},{128,96},{160,128},{192,160},{224,1... | collective-permute-start | bytes 884744 | tf_op jit(solution)/shard_map/ppermute | solution.py:329
  62.5 2.8 %collective-permute-done.16.following = f32[12,12,8,128]{3,2,1,0:T(8,128)S(1)} collective-permute-done((f32[12,12,8,128]{3,2,1,0:T(8,128)S(1)}, f32[12,12,8,128]{3,2,1,0:T(8,128)S(1)}, u32[]{:S(2)}, u32[]{:S(2)}) %collective-permute-start.16) | collective-permute-done | bytes 589856 | tf_op jit(solution)/shard_map/ppermute | solution.py:352
  65.3 0.4 collective-permute-start.23
  65.6 0.0 collective-permute-done.17.preceding
  65.7 1.8 %collective-permute-start.22 = (f32[6,12,8,128]{3,2,1,0:T(8,128)S(1)}, f32[6,12,8,128]{3,2,1,0:T(8,128)S(1)}, u32[]{:S(2)}, u32[]{:S(2)}) collective-permute-start(f32[6,12,8,128]{3,2,1,0:T(8,128)S(1)} %slice.8), channel_id=1, source_target_pairs={{0,16},{16,1},{1,17},{17,0},{2,18},{18,3},{3,19},{19,2},{4,20},{20... | collective-permute-start | bytes 884744 | tf_op jit(solution)/shard_map/ppermute | solution.py:355
  67.5 1.0 shard_map.59.refs_1_
  68.5 1.4 %shard_map.58 = f32[1152,128]{1,0:T(8,128)} custom-call(s32[2]{0:T(128)S(1)} %pad_add_fusion.place, f32[6,12,8,128]{3,2,1,0:T(8,128)S(1)} %get-tuple-element.26.low, f32[6,12,8,128]{3,2,1,0:T(8,128)S(1)} %get-tuple-element.27.high, f32[12,12,8,128]{3,2,1,0:T(8,128)S(1)} %collective-permute-done.16.following, ...), custom_call_target="tpu_custom_call" | custom-call | flops 400000000 | bytes 2000000 | tf_op jit(solution)/shard_map/pallas_call | solution.py:32
  70.0 0.0 collective-permute-done.18.refs_2_
  70.0 0.0 collective-permute-done.20.refs_3_
  70.0 0.8 shard_map.60.refs_1_
  70.8 0.7 shard_map.61.applied
  71.5 1.5 %shard_map.62.near = f32[32,128]{1,0:T(8,128)S(1)} custom-call(f32[6,12,8,128]{3,2,1,0:T(8,128)S(1)} %get-tuple-element.26.low, f32[6,12,8,128]{3,2,1,0:T(8,128)S(1)} %get-tuple-element.27.high, f32[12,12,8,128]{3,2,1,0:T(8,128)S(1)} %shard_map.61.applied, f32[12,12,8,128]{3,2,1,0:T(8,128)S(1)} %collective-permute-done.16.following, ...), custom_call_target="tpu_custom_call" | custom-call | flops 400000000 | bytes 2000000 | tf_op jit(solution)/shard_map/pallas_call | solution.py:32
  73.0 0.0 collective-permute-done.23.far_low
  73.0 0.6 shard_map.63.far_part
  73.6 0.0 collective-permute-done.22.far_high
  73.6 1.3 %shard_map.64 = f32[16,16,128]{2,1,0:T(8,128)S(1)} custom-call(s32[2]{0:T(128)S(1)} %pad_add_fusion.place, f32[6,12,8,128]{3,2,1,0:T(8,128)S(1)} %get-tuple-element.26.low, f32[6,12,8,128]{3,2,1,0:T(8,128)S(1)} %get-tuple-element.27.high, f32[12,12,8,128]{3,2,1,0:T(8,128)S(1)} %shard_map.61.applied, f32[6,12,8,128]{3,2,1,0:T(8,128)S(1)} %collective-permute-done.22.far_high, ...), custom_call_target="tpu_custom_call" | custom-call | flops 1000000 | bytes 2000000 | tf_op jit(solution)/shard_map/pallas_call | solution.py:32
  74.9 14.2 %all_to_all.10.parts = f32[16,16,128]{2,1,0:T(8,128)S(1)} all-to-all(f32[16,16,128]{2,1,0:T(8,128)S(1)} %shard_map.64), channel_id=1, replica_groups=mesh['z'=8,'xl'=2,'y'=4,'core'=2,'xh'=2] {'xl','y','core'}, dimensions={0} | all-to-all | bytes 262144 | tf_op jit(solution)/shard_map/all_to_all | solution.py:385
  89.1 14.0 %all_to_all.11.parts = f32[8,32,128]{2,1,0:T(8,128)S(1)} all-to-all(f32[8,32,128]{2,1,0:T(8,128)S(1)} %shard_map.65), channel_id=1, replica_groups=mesh['z'=8,'xl'=2,'y'=4,'core'=2,'xh'=2] {'z'}, dimensions={0} | all-to-all | bytes 262144 | tf_op jit(solution)/shard_map/all_to_all | solution.py:387
  103.1 0.7 shard_map.66
  (13 shorter events, 0.1 us)
Async XLA Ops:
  0.6 8.3 %copy-start = (f32[1,6,6,128]{3,0,2,1:T(1,128)S(1)}, f32[1,6,6,128]{3,0,2,1:T(1,128)}, u32[]{:S(2)}) copy-start(f32[1,6,6,128]{3,0,2,1:T(1,128)} %param.3) | copy-start | bytes 55300
  1.7 9.2 %collective-permute-start = (f32[576,128]{1,0:T(8,128)S(1)}, f32[576,128]{1,0:T(8,128)S(1)}, u32[]{:S(2)}, u32[]{:S(2)}) collective-permute-start(f32[576,128]{1,0:T(8,128)S(1)} %get-tuple-element.39), channel_id=1, source_target_pairs={{0,16},{16,0},{1,17},{17,1},{2,18},{18,2},{3,19},{19,3},{4,20},{20... | collective-permute-start | bytes 884744 | tf_op jit(solution)/shard_map/ppermute | solution.py:290
  3.0 11.8 %collective-permute-start.6 = (f32[576,128]{1,0:T(8,128)S(1)}, f32[576,128]{1,0:T(8,128)S(1)}, u32[]{:S(2)}, u32[]{:S(2)}) collective-permute-start(f32[576,128]{1,0:T(8,128)S(1)} %get-tuple-element.40.keep), channel_id=1, source_target_pairs={{0,224},{16,48},{32,0},{48,80},{64,32},{80,112},{96,64},{112,144},... | collective-permute-start | bytes 884744 | tf_op jit(solution)/shard_map/ppermute | solution.py:297
  9.0 3.9 %collective-permute-start.1 = (f32[36,128]{1,0:T(8,128)S(1)}, f32[36,128]{1,0:T(8,128)S(1)}, u32[]{:S(2)}, u32[]{:S(2)}) collective-permute-start(f32[36,128]{1,0:T(8,128)S(1)} %reshape.16.own_field), channel_id=1, source_target_pairs={{0,16},{16,0},{1,17},{17,1},{2,18},{18,2},{3,19},{19,3},{4,20},{20... | collective-permute-start | bytes 55304 | tf_op jit(solution)/shard_map/ppermute | solution.py:291
  9.1 7.7 %collective-permute-start.3 = (f32[576,128]{1,0:T(8,128)S(1)}, f32[576,128]{1,0:T(8,128)S(1)}, u32[]{:S(2)}, u32[]{:S(2)}) collective-permute-start(f32[576,128]{1,0:T(8,128)S(1)} %get-tuple-element.40.keep), channel_id=1, source_target_pairs={{0,14},{2,0},{4,2},{6,4},{8,6},{10,8},{12,10},{14,12},{1,15},{3,1}... | collective-permute-start | bytes 884744 | tf_op jit(solution)/shard_map/ppermute | solution.py:299
  11.0 7.4 %collective-permute-start.2 = (f32[576,128]{1,0:T(8,128)S(1)}, f32[576,128]{1,0:T(8,128)S(1)}, u32[]{:S(2)}, u32[]{:S(2)}) collective-permute-start(f32[576,128]{1,0:T(8,128)S(1)} %get-tuple-element.40.keep), channel_id=1, source_target_pairs={{0,2},{2,4},{4,6},{6,8},{8,10},{10,12},{12,14},{14,0},{1,3},{3,5},... | collective-permute-start | bytes 884744 | tf_op jit(solution)/shard_map/ppermute | solution.py:298
  11.0 11.6 %collective-permute-start.7 = (f32[576,128]{1,0:T(8,128)S(1)}, f32[576,128]{1,0:T(8,128)S(1)}, u32[]{:S(2)}, u32[]{:S(2)}) collective-permute-start(f32[576,128]{1,0:T(8,128)S(1)} %collective-permute-done.received), channel_id=1, source_target_pairs={{0,32},{16,240},{32,64},{48,16},{64,96},{80,48},{96,128},{112,80},... | collective-permute-start | bytes 884744 | tf_op jit(solution)/shard_map/ppermute | solution.py:297
  12.8 9.8 %collective-permute-start.5 = (f32[576,128]{1,0:T(8,128)S(1)}, f32[576,128]{1,0:T(8,128)S(1)}, u32[]{:S(2)}, u32[]{:S(2)}) collective-permute-start(f32[576,128]{1,0:T(8,128)S(1)} %collective-permute-done.received), channel_id=1, source_target_pairs={{0,14},{2,0},{4,2},{6,4},{8,6},{10,8},{12,10},{14,12},{1,15},{3,1}... | collective-permute-start | bytes 884744 | tf_op jit(solution)/shard_map/ppermute | solution.py:299
  14.9 7.7 %collective-permute-start.4 = (f32[576,128]{1,0:T(8,128)S(1)}, f32[576,128]{1,0:T(8,128)S(1)}, u32[]{:S(2)}, u32[]{:S(2)}) collective-permute-start(f32[576,128]{1,0:T(8,128)S(1)} %collective-permute-done.received), channel_id=1, source_target_pairs={{0,2},{2,4},{4,6},{6,8},{8,10},{10,12},{12,14},{14,0},{1,3},{3,5},... | collective-permute-start | bytes 884744 | tf_op jit(solution)/shard_map/ppermute | solution.py:298
  23.6 8.1 %collective-permute-start.9 = (f32[12,12,8,128]{3,2,1,0:T(8,128)S(1)}, f32[12,12,8,128]{3,2,1,0:T(8,128)S(1)}, u32[]{:S(2)}, u32[]{:S(2)}) collective-permute-start(f32[12,12,8,128]{3,2,1,0:T(8,128)S(1)} %get-tuple-element.20.refs_0_.refs_2_), channel_id=1, source_target_pairs={{0,14},{2,0},{4,2},{6,4},{8,6},{10,8},{12,10},{14,12},{1,15},{3,1}... | collective-permute-start | bytes 1769480 | tf_op jit(solution)/shard_map/ppermute | solution.py:333
  24.3 10.5 %collective-permute-start.8 = (f32[12,12,8,128]{3,2,1,0:T(8,128)S(1)}, f32[12,12,8,128]{3,2,1,0:T(8,128)S(1)}, u32[]{:S(2)}, u32[]{:S(2)}) collective-permute-start(f32[12,12,8,128]{3,2,1,0:T(8,128)S(1)} %get-tuple-element.20.refs_0_.refs_2_), channel_id=1, source_target_pairs={{0,2},{2,4},{4,6},{6,8},{8,10},{10,12},{12,14},{14,0},{1,3},{3,5},... | collective-permute-start | bytes 1769480 | tf_op jit(solution)/shard_map/ppermute | solution.py:333
  24.3 11.3 %collective-permute-start.10 = (f32[6,12,8,128]{3,2,1,0:T(8,128)S(1)}, f32[6,12,8,128]{3,2,1,0:T(8,128)S(1)}, u32[]{:S(2)}, u32[]{:S(2)}) collective-permute-start(f32[6,12,8,128]{3,2,1,0:T(8,128)S(1)} %get-tuple-element.21), channel_id=1, source_target_pairs={{0,32},{32,64},{64,96},{96,128},{128,160},{160,192},{192,224},{224... | collective-permute-start | bytes 884744 | tf_op jit(solution)/shard_map/ppermute | solution.py:328
  24.6 11.1 %collective-permute-start.11 = (f32[6,12,8,128]{3,2,1,0:T(8,128)S(1)}, f32[6,12,8,128]{3,2,1,0:T(8,128)S(1)}, u32[]{:S(2)}, u32[]{:S(2)}) collective-permute-start(f32[6,12,8,128]{3,2,1,0:T(8,128)S(1)} %get-tuple-element.22), channel_id=1, source_target_pairs={{0,224},{32,0},{64,32},{96,64},{128,96},{160,128},{192,160},{224,1... | collective-permute-start | bytes 884744 | tf_op jit(solution)/shard_map/ppermute | solution.py:329
  36.4 8.9 %collective-permute-start.13 = (f32[12,12,8,128]{3,2,1,0:T(8,128)S(1)}, f32[12,12,8,128]{3,2,1,0:T(8,128)S(1)}, u32[]{:S(2)}, u32[]{:S(2)}) collective-permute-start(f32[12,12,8,128]{3,2,1,0:T(8,128)S(1)} %get-tuple-element.23.refs_0_), channel_id=1, source_target_pairs={{0,14},{2,0},{4,2},{6,4},{8,6},{10,8},{12,10},{14,12},{1,15},{3,1}... | collective-permute-start | bytes 1769480 | tf_op jit(solution)/shard_map/ppermute | solution.py:333
  37.9 10.5 %collective-permute-start.12 = (f32[12,12,8,128]{3,2,1,0:T(8,128)S(1)}, f32[12,12,8,128]{3,2,1,0:T(8,128)S(1)}, u32[]{:S(2)}, u32[]{:S(2)}) collective-permute-start(f32[12,12,8,128]{3,2,1,0:T(8,128)S(1)} %get-tuple-element.23.refs_0_), channel_id=1, source_target_pairs={{0,2},{2,4},{4,6},{6,8},{8,10},{10,12},{12,14},{14,0},{1,3},{3,5},... | collective-permute-start | bytes 1769480 | tf_op jit(solution)/shard_map/ppermute | solution.py:333
  37.9 11.3 %collective-permute-start.14 = (f32[6,12,8,128]{3,2,1,0:T(8,128)S(1)}, f32[6,12,8,128]{3,2,1,0:T(8,128)S(1)}, u32[]{:S(2)}, u32[]{:S(2)}) collective-permute-start(f32[6,12,8,128]{3,2,1,0:T(8,128)S(1)} %get-tuple-element.24), channel_id=1, source_target_pairs={{0,32},{32,64},{64,96},{96,128},{128,160},{160,192},{192,224},{224... | collective-permute-start | bytes 884744 | tf_op jit(solution)/shard_map/ppermute | solution.py:328
  38.4 10.8 %collective-permute-start.15 = (f32[6,12,8,128]{3,2,1,0:T(8,128)S(1)}, f32[6,12,8,128]{3,2,1,0:T(8,128)S(1)}, u32[]{:S(2)}, u32[]{:S(2)}) collective-permute-start(f32[6,12,8,128]{3,2,1,0:T(8,128)S(1)} %get-tuple-element.25), channel_id=1, source_target_pairs={{0,224},{32,0},{64,32},{96,64},{128,96},{160,128},{192,160},{224,1... | collective-permute-start | bytes 884744 | tf_op jit(solution)/shard_map/ppermute | solution.py:329
  50.0 8.3 %collective-permute-start.19 = (f32[6,12,8,128]{3,2,1,0:T(8,128)S(1)}, f32[6,12,8,128]{3,2,1,0:T(8,128)S(1)}, u32[]{:S(2)}, u32[]{:S(2)}) collective-permute-start(f32[6,12,8,128]{3,2,1,0:T(8,128)S(1)} %get-tuple-element.27.high), channel_id=1, source_target_pairs={{0,32},{32,64},{64,96},{96,128},{128,160},{160,192},{192,224},{224... | collective-permute-start | bytes 884744 | tf_op jit(solution)/shard_map/ppermute | solution.py:328
  51.3 14.0 %collective-permute-start.16 = (f32[12,12,8,128]{3,2,1,0:T(8,128)S(1)}, f32[12,12,8,128]{3,2,1,0:T(8,128)S(1)}, u32[]{:S(2)}, u32[]{:S(2)}) collective-permute-start(f32[12,12,8,128]{3,2,1,0:T(8,128)S(1)} %get-tuple-element.29.refs_0_), channel_id=1, source_target_pairs={{0,17},{16,0},{1,16},{17,1},{2,19},{18,2},{3,18},{19,3},{4,21},{20... | collective-permute-start | bytes 1769480 | tf_op jit(solution)/shard_map/ppermute | solution.py:352
  51.6 14.1 %collective-permute-start.17 = (f32[12,12,8,128]{3,2,1,0:T(8,128)S(1)}, f32[12,12,8,128]{3,2,1,0:T(8,128)S(1)}, u32[]{:S(2)}, u32[]{:S(2)}) collective-permute-start(f32[12,12,8,128]{3,2,1,0:T(8,128)S(1)} %get-tuple-element.29.refs_0_), channel_id=1, source_target_pairs={{0,16},{16,1},{1,17},{17,0},{2,18},{18,3},{3,19},{19,2},{4,20},{20... | collective-permute-start | bytes 1769480 | tf_op jit(solution)/shard_map/ppermute | solution.py:353
  53.3 16.7 %collective-permute-start.18 = (f32[12,12,8,128]{3,2,1,0:T(8,128)S(1)}, f32[12,12,8,128]{3,2,1,0:T(8,128)S(1)}, u32[]{:S(2)}, u32[]{:S(2)}) collective-permute-start(f32[12,12,8,128]{3,2,1,0:T(8,128)S(1)} %get-tuple-element.29.refs_0_), channel_id=1, source_target_pairs={{0,2},{2,4},{4,6},{6,8},{8,10},{10,12},{12,14},{14,0},{1,3},{3,5},... | collective-permute-start | bytes 1769480 | tf_op jit(solution)/shard_map/ppermute | solution.py:333
  58.2 11.7 %collective-permute-start.20 = (f32[12,12,8,128]{3,2,1,0:T(8,128)S(1)}, f32[12,12,8,128]{3,2,1,0:T(8,128)S(1)}, u32[]{:S(2)}, u32[]{:S(2)}) collective-permute-start(f32[12,12,8,128]{3,2,1,0:T(8,128)S(1)} %get-tuple-element.29.refs_0_), channel_id=1, source_target_pairs={{0,14},{2,0},{4,2},{6,4},{8,6},{10,8},{12,10},{14,12},{1,15},{3,1}... | collective-permute-start | bytes 1769480 | tf_op jit(solution)/shard_map/ppermute | solution.py:333
  60.9 9.9 %collective-permute-start.21 = (f32[6,12,8,128]{3,2,1,0:T(8,128)S(1)}, f32[6,12,8,128]{3,2,1,0:T(8,128)S(1)}, u32[]{:S(2)}, u32[]{:S(2)}) collective-permute-start(f32[6,12,8,128]{3,2,1,0:T(8,128)S(1)} %get-tuple-element.26.low), channel_id=1, source_target_pairs={{0,224},{32,0},{64,32},{96,64},{128,96},{160,128},{192,160},{224,1... | collective-permute-start | bytes 884744 | tf_op jit(solution)/shard_map/ppermute | solution.py:329
  65.3 7.7 %collective-permute-start.23 = (f32[6,12,8,128]{3,2,1,0:T(8,128)S(1)}, f32[6,12,8,128]{3,2,1,0:T(8,128)S(1)}, u32[]{:S(2)}, u32[]{:S(2)}) collective-permute-start(f32[6,12,8,128]{3,2,1,0:T(8,128)S(1)} %slice.9), channel_id=1, source_target_pairs={{0,17},{16,0},{1,16},{17,1},{2,19},{18,2},{3,18},{19,3},{4,21},{20... | collective-permute-start | bytes 884744 | tf_op jit(solution)/shard_map/ppermute | solution.py:354
  65.7 8.0 %collective-permute-start.22 = (f32[6,12,8,128]{3,2,1,0:T(8,128)S(1)}, f32[6,12,8,128]{3,2,1,0:T(8,128)S(1)}, u32[]{:S(2)}, u32[]{:S(2)}) collective-permute-start(f32[6,12,8,128]{3,2,1,0:T(8,128)S(1)} %slice.8), channel_id=1, source_target_pairs={{0,16},{16,1},{1,17},{17,0},{2,18},{18,3},{3,19},{19,2},{4,20},{20... | collective-permute-start | bytes 884744 | tf_op jit(solution)/shard_map/ppermute | solution.py:355

commit v9 on v8

--- a/solution.py
+++ b/solution.py
@@ -325,17 +325,16 @@
 
     def step(numbers, planes, previous, outs, last=False):
         full, low, high = planes
+        def interior(*refs):
+            interior_body(*numbers, *refs)
+
         before_x = lax.ppermute(high, "z", UP)
         after_x = lax.ppermute(low, "z", DOWN)
+        acc = call(interior, FULL, [full, field, *previous], flops=400_000_000)
         later = full
         if last:
-            later = lax.optimization_barrier((full, before_x))[0]
+            later, acc, _ = lax.optimization_barrier((full, acc, before_x))
         halos = (lax.ppermute(full, ROWS, UP), lax.ppermute(later, ROWS, DOWN), before_x, after_x)
-
-        def interior(*refs):
-            interior_body(*numbers, *refs)
-
-        acc = call(interior, FULL, [full, field, *previous], flops=400_000_000)
 
         def edge_y(*refs):
             edge_y_body(numbers[0], *refs)

time: 105 us -> 105 us (level)
  transfers between devices with their start and end apart: 24 -> 24, of which waited for: 10 -> 11; matrix products, arithmetic and copies ran while one was open for 0% -> 0% of each run, Pallas kernels for 11% -> 11%
where the time goes in v9:
time: 105 us; the launch traced here: 104 us
  starting transfers between devices  30.4 us (29%)
  blocking collectives  29.1 us (28%)
  waiting for transfers between devices  26.1 us (25%)
  Pallas kernels  16 us (15%)
  local copies, waits for them, and re-layouts  1.14 us (1%)
    pallas_call x18, Pallas kernels, call(): pl.pallas_call(body, out_shape=outs, in_specs=specs or [VM] * len(inputs)...  16 us
    all_to_all x1, blocking collectives, local(): lax.all_to_all(copies, ('xl',) + ROWS, split_axis=0, concat_axis=0, tiled...  15.1 us
    all_to_all x1, blocking collectives, local(): parts = lax.all_to_all(copies, 'z', split_axis=0, concat_axis=0, tiled=True)  14 us
    ppermute x2, starting transfers between devices, first_halos(): lax.ppermute(values, ('z', 'xl'), along_x)  7.61 us
    ppermute x3, starting transfers between devices, step(): after_x = lax.ppermute(low, 'z', DOWN)  7.21 us
    ppermute x3, waiting for transfers between devices, step(): lax.ppermute(full, ROWS, UP)  6.24 us
    ppermute x3, waiting for transfers between devices, step(): lax.ppermute(later, ROWS, DOWN)  6.04 us
    ppermute x2, waiting for transfers between devices, first_halos(): lax.ppermute(values, ('z', 'xl'), along_x)  5.19 us
  transfers between devices with their start and end apart: 24, of which 11 were waited for; matrix products, arithmetic and copies ran while one was open for 0% of the time, Pallas kernels for 11%

profile of v9, /device:TPU:4, one launch (start us, length us, event | category | flops | bytes accessed | tf_op | source)
XLA Modules:
  0.0 103.8 jit_solution(14546650509919326236)
XLA Ops:
  0.6 1.1 %constant_dynamic-slice_fusion = (f32[576,128]{1,0:T(8,128)S(1)}, f32[576,128]{1,0:T(8,128)S(1)}) fusion(f32[1152,128]{1,0:T(8,128)} %bitcast.9, s32[]{:T(128)S(6)} %select_n.7, s32[]{:T(128)S(6)} %select_n.6), kind=kLoop, calls=%fused_computation.2 | loop fusion | bytes 1179656 | tf_op jit(solution)/shard_map/dynamic_slice | solution.py:290
  1.7 1.3 %collective-permute-start = (f32[576,128]{1,0:T(8,128)S(1)}, f32[576,128]{1,0:T(8,128)S(1)}, u32[]{:S(2)}, u32[]{:S(2)}) collective-permute-start(f32[576,128]{1,0:T(8,128)S(1)} %get-tuple-element.41), channel_id=1, source_target_pairs={{0,16},{16,0},{1,17},{17,1},{2,18},{18,2},{3,19},{19,3},{4,20},{20... | collective-permute-start | bytes 884744 | tf_op jit(solution)/shard_map/ppermute | solution.py:290
  3.0 5.9 %collective-permute-start.6 = (f32[576,128]{1,0:T(8,128)S(1)}, f32[576,128]{1,0:T(8,128)S(1)}, u32[]{:S(2)}, u32[]{:S(2)}) collective-permute-start(f32[576,128]{1,0:T(8,128)S(1)} %get-tuple-element.42.keep), channel_id=1, source_target_pairs={{0,224},{16,48},{32,0},{48,80},{64,32},{80,112},{96,64},{112,144},... | collective-permute-start | bytes 884744 | tf_op jit(solution)/shard_map/ppermute | solution.py:297
  9.0 0.1 collective-permute-start.1
  9.1 1.9 %collective-permute-start.3 = (f32[576,128]{1,0:T(8,128)S(1)}, f32[576,128]{1,0:T(8,128)S(1)}, u32[]{:S(2)}, u32[]{:S(2)}) collective-permute-start(f32[576,128]{1,0:T(8,128)S(1)} %get-tuple-element.42.keep), channel_id=1, source_target_pairs={{0,14},{2,0},{4,2},{6,4},{8,6},{10,8},{12,10},{14,12},{1,15},{3,1}... | collective-permute-start | bytes 884744 | tf_op jit(solution)/shard_map/ppermute | solution.py:299
  11.0 0.0 collective-permute-done.received
  11.0 1.8 %collective-permute-start.7 = (f32[576,128]{1,0:T(8,128)S(1)}, f32[576,128]{1,0:T(8,128)S(1)}, u32[]{:S(2)}, u32[]{:S(2)}) collective-permute-start(f32[576,128]{1,0:T(8,128)S(1)} %collective-permute-done.received), channel_id=1, source_target_pairs={{0,32},{16,240},{32,64},{48,16},{64,96},{80,48},{96,128},{112,80},... | collective-permute-start | bytes 884744 | tf_op jit(solution)/shard_map/ppermute | solution.py:297
  12.7 0.1 collective-permute-done.1.other_field
  12.8 1.1 %collective-permute-start.5 = (f32[576,128]{1,0:T(8,128)S(1)}, f32[576,128]{1,0:T(8,128)S(1)}, u32[]{:S(2)}, u32[]{:S(2)}) collective-permute-start(f32[576,128]{1,0:T(8,128)S(1)} %collective-permute-done.received), channel_id=1, source_target_pairs={{0,14},{2,0},{4,2},{6,4},{8,6},{10,8},{12,10},{14,12},{1,15},{3,1}... | collective-permute-start | bytes 884744 | tf_op jit(solution)/shard_map/ppermute | solution.py:299
  13.9 0.9 collective-permute-done.6.e
  14.9 0.1 pad_add_fusion.place
  15.0 0.1 add_convert_fusion.inside.refs_0_
  15.0 0.6 shard_map.49
  15.6 1.1 %shard_map.50.acc = f32[12,12,8,128]{3,2,1,0:T(8,128)S(1)} custom-call(f32[12,12,8,128]{3,2,1,0:T(8,128)S(1)} %get-tuple-element.19.refs_0_.refs_2_, f32[12,6,8,128]{3,2,1,0:T(8,128)S(1)} %get-tuple-element.20.refs_1_), custom_call_target="tpu_custom_call" | custom-call | flops 400000000 | bytes 2000000 | tf_op jit(solution)/shard_map/pallas_call | solution.py:32
  16.7 1.6 %collective-permute-done.2.a = f32[576,128]{1,0:T(8,128)S(1)} collective-permute-done((f32[576,128]{1,0:T(8,128)S(1)}, f32[576,128]{1,0:T(8,128)S(1)}, u32[]{:S(2)}, u32[]{:S(2)}) %collective-permute-start.2) | collective-permute-done | bytes 294944 | tf_op jit(solution)/shard_map/ppermute | solution.py:298
  18.3 4.3 %collective-permute-done.7.f = f32[576,128]{1,0:T(8,128)S(1)} collective-permute-done((f32[576,128]{1,0:T(8,128)S(1)}, f32[576,128]{1,0:T(8,128)S(1)}, u32[]{:S(2)}, u32[]{:S(2)}) %collective-permute-start.7) | collective-permute-done | bytes 294944 | tf_op jit(solution)/shard_map/ppermute | solution.py:297
  22.6 0.0 collective-permute-done.5.d
  22.6 0.0 collective-permute-done.4.c
  22.6 1.0 shard_map.51
  23.6 0.7 collective-permute-start.9
  24.3 0.3 collective-permute-start.10
  24.6 2.9 %collective-permute-start.11 = (f32[6,12,8,128]{3,2,1,0:T(8,128)S(1)}, f32[6,12,8,128]{3,2,1,0:T(8,128)S(1)}, u32[]{:S(2)}, u32[]{:S(2)}) collective-permute-start(f32[6,12,8,128]{3,2,1,0:T(8,128)S(1)} %get-tuple-element.23), channel_id=1, source_target_pairs={{0,224},{32,0},{64,32},{96,64},{128,96},{160,128},{192,160},{224,1... | collective-permute-start | bytes 884744 | tf_op jit(solution)/shard_map/ppermute | solution.py:332
  27.5 1.1 %shard_map.52.refs_1_ = f32[12,12,8,128]{3,2,1,0:T(8,128)S(1)} custom-call(f32[12,12,8,128]{3,2,1,0:T(8,128)S(1)} %get-tuple-element.21.refs_0_.refs_2_, f32[12,6,8,128]{3,2,1,0:T(8,128)S(1)} %get-tuple-element.20.refs_1_, f32[12,12,8,128]{3,2,1,0:T(8,128)S(1)} %get-tuple-element.19.refs_0_.refs_2_), custom_call_target="tpu_custom_call" | custom-call | flops 400000000 | bytes 2000000 | tf_op jit(solution)/shard_map/pallas_call | solution.py:32
  28.7 3.0 %collective-permute-done.9.refs_3_ = f32[12,12,8,128]{3,2,1,0:T(8,128)S(1)} collective-permute-done((f32[12,12,8,128]{3,2,1,0:T(8,128)S(1)}, f32[12,12,8,128]{3,2,1,0:T(8,128)S(1)}, u32[]{:S(2)}, u32[]{:S(2)}) %collective-permute-start.9) | collective-permute-done | bytes 589856 | tf_op jit(solution)/shard_map/ppermute | solution.py:337
  31.7 3.1 %collective-permute-done.8.refs_2_ = f32[12,12,8,128]{3,2,1,0:T(8,128)S(1)} collective-permute-done((f32[12,12,8,128]{3,2,1,0:T(8,128)S(1)}, f32[12,12,8,128]{3,2,1,0:T(8,128)S(1)}, u32[]{:S(2)}, u32[]{:S(2)}) %collective-permute-start.8) | collective-permute-done | bytes 589856 | tf_op jit(solution)/shard_map/ppermute | solution.py:337
  34.8 0.8 shard_map.53.refs_1_
  35.6 0.0 collective-permute-done.10.refs_2_
  35.7 0.0 collective-permute-done.11.refs_3_
  35.7 0.7 shard_map.54
  36.4 1.5 %collective-permute-start.13 = (f32[12,12,8,128]{3,2,1,0:T(8,128)S(1)}, f32[12,12,8,128]{3,2,1,0:T(8,128)S(1)}, u32[]{:S(2)}, u32[]{:S(2)}) collective-permute-start(f32[12,12,8,128]{3,2,1,0:T(8,128)S(1)} %get-tuple-element.24.refs_0_), channel_id=1, source_target_pairs={{0,14},{2,0},{4,2},{6,4},{8,6},{10,8},{12,10},{14,12},{1,15},{3,1}... | collective-permute-start | bytes 1769480 | tf_op jit(solution)/shard_map/ppermute | solution.py:337
  37.9 0.0 collective-permute-start.12
  37.9 0.5 collective-permute-start.14
  38.4 2.7 %collective-permute-start.15 = (f32[6,12,8,128]{3,2,1,0:T(8,128)S(1)}, f32[6,12,8,128]{3,2,1,0:T(8,128)S(1)}, u32[]{:S(2)}, u32[]{:S(2)}) collective-permute-start(f32[6,12,8,128]{3,2,1,0:T(8,128)S(1)} %get-tuple-element.26), channel_id=1, source_target_pairs={{0,224},{32,0},{64,32},{96,64},{128,96},{160,128},{192,160},{224,1... | collective-permute-start | bytes 884744 | tf_op jit(solution)/shard_map/ppermute | solution.py:332
  41.1 1.1 %shard_map.55.refs_1_ = f32[12,12,8,128]{3,2,1,0:T(8,128)S(1)} custom-call(f32[12,12,8,128]{3,2,1,0:T(8,128)S(1)} %get-tuple-element.24.refs_0_, f32[12,6,8,128]{3,2,1,0:T(8,128)S(1)} %get-tuple-element.20.refs_1_, f32[12,12,8,128]{3,2,1,0:T(8,128)S(1)} %get-tuple-element.21.refs_0_.refs_2_), custom_call_target="tpu_custom_call" | custom-call | flops 400000000 | bytes 2000000 | tf_op jit(solution)/shard_map/pallas_call | solution.py:32
  42.3 3.0 %collective-permute-done.13.refs_3_ = f32[12,12,8,128]{3,2,1,0:T(8,128)S(1)} collective-permute-done((f32[12,12,8,128]{3,2,1,0:T(8,128)S(1)}, f32[12,12,8,128]{3,2,1,0:T(8,128)S(1)}, u32[]{:S(2)}, u32[]{:S(2)}) %collective-permute-start.13) | collective-permute-done | bytes 589856 | tf_op jit(solution)/shard_map/ppermute | solution.py:337
  45.3 3.1 %collective-permute-done.12.refs_2_ = f32[12,12,8,128]{3,2,1,0:T(8,128)S(1)} collective-permute-done((f32[12,12,8,128]{3,2,1,0:T(8,128)S(1)}, f32[12,12,8,128]{3,2,1,0:T(8,128)S(1)}, u32[]{:S(2)}, u32[]{:S(2)}) %collective-permute-start.12) | collective-permute-done | bytes 589856 | tf_op jit(solution)/shard_map/ppermute | solution.py:337
  48.4 0.8 shard_map.56.refs_1_
  49.2 0.0 collective-permute-done.14.refs_2_
  49.3 0.7 shard_map.57
  50.0 1.3 %collective-permute-start.18 = (f32[6,12,8,128]{3,2,1,0:T(8,128)S(1)}, f32[6,12,8,128]{3,2,1,0:T(8,128)S(1)}, u32[]{:S(2)}, u32[]{:S(2)}) collective-permute-start(f32[6,12,8,128]{3,2,1,0:T(8,128)S(1)} %get-tuple-element.28.high), channel_id=1, source_target_pairs={{0,32},{32,64},{64,96},{96,128},{128,160},{160,192},{192,224},{224... | collective-permute-start | bytes 884744 | tf_op jit(solution)/shard_map/ppermute | solution.py:331
  51.3 0.3 collective-permute-start.16
  51.6 1.7 %collective-permute-start.17 = (f32[12,12,8,128]{3,2,1,0:T(8,128)S(1)}, f32[12,12,8,128]{3,2,1,0:T(8,128)S(1)}, u32[]{:S(2)}, u32[]{:S(2)}) collective-permute-start(f32[12,12,8,128]{3,2,1,0:T(8,128)S(1)} %get-tuple-element.31.refs_0_), channel_id=1, source_target_pairs={{0,16},{16,1},{1,17},{17,0},{2,18},{18,3},{3,19},{19,2},{4,20},{20... | collective-permute-start | bytes 1769480 | tf_op jit(solution)/shard_map/ppermute | solution.py:352
  53.3 0.0 collective-permute-start.19
  53.3 1.0 shard_map.59.refs_1_
  54.3 3.9 %collective-permute-done.18.refs_2_ = f32[6,12,8,128]{3,2,1,0:T(8,128)S(1)} collective-permute-done((f32[6,12,8,128]{3,2,1,0:T(8,128)S(1)}, f32[6,12,8,128]{3,2,1,0:T(8,128)S(1)}, u32[]{:S(2)}, u32[]{:S(2)}) %collective-permute-start.18) | collective-permute-done | bytes 294944 | tf_op jit(solution)/shard_map/ppermute | solution.py:331
  58.2 2.7 %collective-permute-start.20 = (f32[12,12,8,128]{3,2,1,0:T(8,128)S(1)}, f32[12,12,8,128]{3,2,1,0:T(8,128)S(1)}, u32[]{:S(2)}, u32[]{:S(2)}) collective-permute-start(f32[12,12,8,128]{3,2,1,0:T(8,128)S(1)} %get-tuple-element.31.refs_0_), channel_id=1, source_target_pairs={{0,14},{2,0},{4,2},{6,4},{8,6},{10,8},{12,10},{14,12},{1,15},{3,1}... | collective-permute-start | bytes 1769480 | tf_op jit(solution)/shard_map/ppermute | solution.py:337
  60.9 1.5 %collective-permute-start.21 = (f32[6,12,8,128]{3,2,1,0:T(8,128)S(1)}, f32[6,12,8,128]{3,2,1,0:T(8,128)S(1)}, u32[]{:S(2)}, u32[]{:S(2)}) collective-permute-start(f32[6,12,8,128]{3,2,1,0:T(8,128)S(1)} %get-tuple-element.27.low), channel_id=1, source_target_pairs={{0,224},{32,0},{64,32},{96,64},{128,96},{160,128},{192,160},{224,1... | collective-permute-start | bytes 884744 | tf_op jit(solution)/shard_map/ppermute | solution.py:332
  62.5 2.8 %collective-permute-done.16.following = f32[12,12,8,128]{3,2,1,0:T(8,128)S(1)} collective-permute-done((f32[12,12,8,128]{3,2,1,0:T(8,128)S(1)}, f32[12,12,8,128]{3,2,1,0:T(8,128)S(1)}, u32[]{:S(2)}, u32[]{:S(2)}) %collective-permute-start.16) | collective-permute-done | bytes 589856 | tf_op jit(solution)/shard_map/ppermute | solution.py:351
  65.3 0.4 collective-permute-start.23
  65.6 0.0 collective-permute-done.17.preceding
  65.7 1.8 %collective-permute-start.22 = (f32[6,12,8,128]{3,2,1,0:T(8,128)S(1)}, f32[6,12,8,128]{3,2,1,0:T(8,128)S(1)}, u32[]{:S(2)}, u32[]{:S(2)}) collective-permute-start(f32[6,12,8,128]{3,2,1,0:T(8,128)S(1)} %slice.8), channel_id=1, source_target_pairs={{0,16},{16,1},{1,17},{17,0},{2,18},{18,3},{3,19},{19,2},{4,20},{20... | collective-permute-start | bytes 884744 | tf_op jit(solution)/shard_map/ppermute | solution.py:354
  67.5 1.4 %shard_map.58 = f32[1152,128]{1,0:T(8,128)} custom-call(s32[2]{0:T(128)S(1)} %pad_add_fusion.place, f32[6,12,8,128]{3,2,1,0:T(8,128)S(1)} %get-tuple-element.27.low, f32[6,12,8,128]{3,2,1,0:T(8,128)S(1)} %get-tuple-element.28.high, f32[12,12,8,128]{3,2,1,0:T(8,128)S(1)} %collective-permute-done.16.following, ...), custom_call_target="tpu_custom_call" | custom-call | flops 400000000 | bytes 2000000 | tf_op jit(solution)/shard_map/pallas_call | solution.py:32
  68.9 0.0 collective-permute-done.20.refs_3_
  68.9 0.8 shard_map.60.refs_1_
  69.8 0.0 collective-permute-done.21.refs_3_
  69.8 0.7 shard_map.61.applied
  70.5 1.5 %shard_map.62.near = f32[32,128]{1,0:T(8,128)S(1)} custom-call(f32[6,12,8,128]{3,2,1,0:T(8,128)S(1)} %get-tuple-element.27.low, f32[6,12,8,128]{3,2,1,0:T(8,128)S(1)} %get-tuple-element.28.high, f32[12,12,8,128]{3,2,1,0:T(8,128)S(1)} %shard_map.61.applied, f32[12,12,8,128]{3,2,1,0:T(8,128)S(1)} %collective-permute-done.16.following, ...), custom_call_target="tpu_custom_call" | custom-call | flops 400000000 | bytes 2000000 | tf_op jit(solution)/shard_map/pallas_call | solution.py:32
  72.0 0.2 collective-permute-done.23.far_low
  72.1 0.6 shard_map.63.far_part
  72.7 0.0 collective-permute-done.22.far_high
  72.7 1.3 %shard_map.64 = f32[16,16,128]{2,1,0:T(8,128)S(1)} custom-call(s32[2]{0:T(128)S(1)} %pad_add_fusion.place, f32[6,12,8,128]{3,2,1,0:T(8,128)S(1)} %get-tuple-element.27.low, f32[6,12,8,128]{3,2,1,0:T(8,128)S(1)} %get-tuple-element.28.high, f32[12,12,8,128]{3,2,1,0:T(8,128)S(1)} %shard_map.61.applied, f32[6,12,8,128]{3,2,1,0:T(8,128)S(1)} %collective-permute-done.22.far_high, ...), custom_call_target="tpu_custom_call" | custom-call | flops 1000000 | bytes 2000000 | tf_op jit(solution)/shard_map/pallas_call | solution.py:32
  74.0 15.1 %all_to_all.10.parts = f32[16,16,128]{2,1,0:T(8,128)S(1)} all-to-all(f32[16,16,128]{2,1,0:T(8,128)S(1)} %shard_map.64), channel_id=1, replica_groups=mesh['z'=8,'xl'=2,'y'=4,'core'=2,'xh'=2] {'xl','y','core'}, dimensions={0} | all-to-all | bytes 262144 | tf_op jit(solution)/shard_map/all_to_all | solution.py:384
  89.1 14.0 %all_to_all.11.parts = f32[8,32,128]{2,1,0:T(8,128)S(1)} all-to-all(f32[8,32,128]{2,1,0:T(8,128)S(1)} %shard_map.65), channel_id=1, replica_groups=mesh['z'=8,'xl'=2,'y'=4,'core'=2,'xh'=2] {'z'}, dimensions={0} | all-to-all | bytes 262144 | tf_op jit(solution)/shard_map/all_to_all | solution.py:386
  103.1 0.7 shard_map.66
  (13 shorter events, 0.1 us)
Async XLA Ops:
  0.6 8.3 %copy-start = (f32[1,6,6,128]{3,0,2,1:T(1,128)S(1)}, f32[1,6,6,128]{3,0,2,1:T(1,128)}, u32[]{:S(2)}) copy-start(f32[1,6,6,128]{3,0,2,1:T(1,128)} %param.3) | copy-start | bytes 55300
  1.7 9.2 %collective-permute-start = (f32[576,128]{1,0:T(8,128)S(1)}, f32[576,128]{1,0:T(8,128)S(1)}, u32[]{:S(2)}, u32[]{:S(2)}) collective-permute-start(f32[576,128]{1,0:T(8,128)S(1)} %get-tuple-element.41), channel_id=1, source_target_pairs={{0,16},{16,0},{1,17},{17,1},{2,18},{18,2},{3,19},{19,3},{4,20},{20... | collective-permute-start | bytes 884744 | tf_op jit(solution)/shard_map/ppermute | solution.py:290
  3.0 11.8 %collective-permute-start.6 = (f32[576,128]{1,0:T(8,128)S(1)}, f32[576,128]{1,0:T(8,128)S(1)}, u32[]{:S(2)}, u32[]{:S(2)}) collective-permute-start(f32[576,128]{1,0:T(8,128)S(1)} %get-tuple-element.42.keep), channel_id=1, source_target_pairs={{0,224},{16,48},{32,0},{48,80},{64,32},{80,112},{96,64},{112,144},... | collective-permute-start | bytes 884744 | tf_op jit(solution)/shard_map/ppermute | solution.py:297
  9.0 3.9 %collective-permute-start.1 = (f32[36,128]{1,0:T(8,128)S(1)}, f32[36,128]{1,0:T(8,128)S(1)}, u32[]{:S(2)}, u32[]{:S(2)}) collective-permute-start(f32[36,128]{1,0:T(8,128)S(1)} %reshape.16.own_field), channel_id=1, source_target_pairs={{0,16},{16,0},{1,17},{17,1},{2,18},{18,2},{3,19},{19,3},{4,20},{20... | collective-permute-start | bytes 55304 | tf_op jit(solution)/shard_map/ppermute | solution.py:291
  9.1 7.7 %collective-permute-start.3 = (f32[576,128]{1,0:T(8,128)S(1)}, f32[576,128]{1,0:T(8,128)S(1)}, u32[]{:S(2)}, u32[]{:S(2)}) collective-permute-start(f32[576,128]{1,0:T(8,128)S(1)} %get-tuple-element.42.keep), channel_id=1, source_target_pairs={{0,14},{2,0},{4,2},{6,4},{8,6},{10,8},{12,10},{14,12},{1,15},{3,1}... | collective-permute-start | bytes 884744 | tf_op jit(solution)/shard_map/ppermute | solution.py:299
  11.0 7.4 %collective-permute-start.2 = (f32[576,128]{1,0:T(8,128)S(1)}, f32[576,128]{1,0:T(8,128)S(1)}, u32[]{:S(2)}, u32[]{:S(2)}) collective-permute-start(f32[576,128]{1,0:T(8,128)S(1)} %get-tuple-element.42.keep), channel_id=1, source_target_pairs={{0,2},{2,4},{4,6},{6,8},{8,10},{10,12},{12,14},{14,0},{1,3},{3,5},... | collective-permute-start | bytes 884744 | tf_op jit(solution)/shard_map/ppermute | solution.py:298
  11.0 11.6 %collective-permute-start.7 = (f32[576,128]{1,0:T(8,128)S(1)}, f32[576,128]{1,0:T(8,128)S(1)}, u32[]{:S(2)}, u32[]{:S(2)}) collective-permute-start(f32[576,128]{1,0:T(8,128)S(1)} %collective-permute-done.received), channel_id=1, source_target_pairs={{0,32},{16,240},{32,64},{48,16},{64,96},{80,48},{96,128},{112,80},... | collective-permute-start | bytes 884744 | tf_op jit(solution)/shard_map/ppermute | solution.py:297
  12.8 9.8 %collective-permute-start.5 = (f32[576,128]{1,0:T(8,128)S(1)}, f32[576,128]{1,0:T(8,128)S(1)}, u32[]{:S(2)}, u32[]{:S(2)}) collective-permute-start(f32[576,128]{1,0:T(8,128)S(1)} %collective-permute-done.received), channel_id=1, source_target_pairs={{0,14},{2,0},{4,2},{6,4},{8,6},{10,8},{12,10},{14,12},{1,15},{3,1}... | collective-permute-start | bytes 884744 | tf_op jit(solution)/shard_map/ppermute | solution.py:299
  14.9 7.7 %collective-permute-start.4 = (f32[576,128]{1,0:T(8,128)S(1)}, f32[576,128]{1,0:T(8,128)S(1)}, u32[]{:S(2)}, u32[]{:S(2)}) collective-permute-start(f32[576,128]{1,0:T(8,128)S(1)} %collective-permute-done.received), channel_id=1, source_target_pairs={{0,2},{2,4},{4,6},{6,8},{8,10},{10,12},{12,14},{14,0},{1,3},{3,5},... | collective-permute-start | bytes 884744 | tf_op jit(solution)/shard_map/ppermute | solution.py:298
  23.6 8.1 %collective-permute-start.9 = (f32[12,12,8,128]{3,2,1,0:T(8,128)S(1)}, f32[12,12,8,128]{3,2,1,0:T(8,128)S(1)}, u32[]{:S(2)}, u32[]{:S(2)}) collective-permute-start(f32[12,12,8,128]{3,2,1,0:T(8,128)S(1)} %get-tuple-element.21.refs_0_.refs_2_), channel_id=1, source_target_pairs={{0,14},{2,0},{4,2},{6,4},{8,6},{10,8},{12,10},{14,12},{1,15},{3,1}... | collective-permute-start | bytes 1769480 | tf_op jit(solution)/shard_map/ppermute | solution.py:337
  24.3 10.5 %collective-permute-start.8 = (f32[12,12,8,128]{3,2,1,0:T(8,128)S(1)}, f32[12,12,8,128]{3,2,1,0:T(8,128)S(1)}, u32[]{:S(2)}, u32[]{:S(2)}) collective-permute-start(f32[12,12,8,128]{3,2,1,0:T(8,128)S(1)} %get-tuple-element.21.refs_0_.refs_2_), channel_id=1, source_target_pairs={{0,2},{2,4},{4,6},{6,8},{8,10},{10,12},{12,14},{14,0},{1,3},{3,5},... | collective-permute-start | bytes 1769480 | tf_op jit(solution)/shard_map/ppermute | solution.py:337
  24.3 11.3 %collective-permute-start.10 = (f32[6,12,8,128]{3,2,1,0:T(8,128)S(1)}, f32[6,12,8,128]{3,2,1,0:T(8,128)S(1)}, u32[]{:S(2)}, u32[]{:S(2)}) collective-permute-start(f32[6,12,8,128]{3,2,1,0:T(8,128)S(1)} %get-tuple-element.22), channel_id=1, source_target_pairs={{0,32},{32,64},{64,96},{96,128},{128,160},{160,192},{192,224},{224... | collective-permute-start | bytes 884744 | tf_op jit(solution)/shard_map/ppermute | solution.py:331
  24.6 11.1 %collective-permute-start.11 = (f32[6,12,8,128]{3,2,1,0:T(8,128)S(1)}, f32[6,12,8,128]{3,2,1,0:T(8,128)S(1)}, u32[]{:S(2)}, u32[]{:S(2)}) collective-permute-start(f32[6,12,8,128]{3,2,1,0:T(8,128)S(1)} %get-tuple-element.23), channel_id=1, source_target_pairs={{0,224},{32,0},{64,32},{96,64},{128,96},{160,128},{192,160},{224,1... | collective-permute-start | bytes 884744 | tf_op jit(solution)/shard_map/ppermute | solution.py:332
  36.4 8.9 %collective-permute-start.13 = (f32[12,12,8,128]{3,2,1,0:T(8,128)S(1)}, f32[12,12,8,128]{3,2,1,0:T(8,128)S(1)}, u32[]{:S(2)}, u32[]{:S(2)}) collective-permute-start(f32[12,12,8,128]{3,2,1,0:T(8,128)S(1)} %get-tuple-element.24.refs_0_), channel_id=1, source_target_pairs={{0,14},{2,0},{4,2},{6,4},{8,6},{10,8},{12,10},{14,12},{1,15},{3,1}... | collective-permute-start | bytes 1769480 | tf_op jit(solution)/shard_map/ppermute | solution.py:337
  37.9 10.5 %collective-permute-start.12 = (f32[12,12,8,128]{3,2,1,0:T(8,128)S(1)}, f32[12,12,8,128]{3,2,1,0:T(8,128)S(1)}, u32[]{:S(2)}, u32[]{:S(2)}) collective-permute-start(f32[12,12,8,128]{3,2,1,0:T(8,128)S(1)} %get-tuple-element.24.refs_0_), channel_id=1, source_target_pairs={{0,2},{2,4},{4,6},{6,8},{8,10},{10,12},{12,14},{14,0},{1,3},{3,5},... | collective-permute-start | bytes 1769480 | tf_op jit(solution)/shard_map/ppermute | solution.py:337
  37.9 11.3 %collective-permute-start.14 = (f32[6,12,8,128]{3,2,1,0:T(8,128)S(1)}, f32[6,12,8,128]{3,2,1,0:T(8,128)S(1)}, u32[]{:S(2)}, u32[]{:S(2)}) collective-permute-start(f32[6,12,8,128]{3,2,1,0:T(8,128)S(1)} %get-tuple-element.25), channel_id=1, source_target_pairs={{0,32},{32,64},{64,96},{96,128},{128,160},{160,192},{192,224},{224... | collective-permute-start | bytes 884744 | tf_op jit(solution)/shard_map/ppermute | solution.py:331
  38.4 10.8 %collective-permute-start.15 = (f32[6,12,8,128]{3,2,1,0:T(8,128)S(1)}, f32[6,12,8,128]{3,2,1,0:T(8,128)S(1)}, u32[]{:S(2)}, u32[]{:S(2)}) collective-permute-start(f32[6,12,8,128]{3,2,1,0:T(8,128)S(1)} %get-tuple-element.26), channel_id=1, source_target_pairs={{0,224},{32,0},{64,32},{96,64},{128,96},{160,128},{192,160},{224,1... | collective-permute-start | bytes 884744 | tf_op jit(solution)/shard_map/ppermute | solution.py:332
  50.0 8.3 %collective-permute-start.18 = (f32[6,12,8,128]{3,2,1,0:T(8,128)S(1)}, f32[6,12,8,128]{3,2,1,0:T(8,128)S(1)}, u32[]{:S(2)}, u32[]{:S(2)}) collective-permute-start(f32[6,12,8,128]{3,2,1,0:T(8,128)S(1)} %get-tuple-element.28.high), channel_id=1, source_target_pairs={{0,32},{32,64},{64,96},{96,128},{128,160},{160,192},{192,224},{224... | collective-permute-start | bytes 884744 | tf_op jit(solution)/shard_map/ppermute | solution.py:331
  51.3 14.0 %collective-permute-start.16 = (f32[12,12,8,128]{3,2,1,0:T(8,128)S(1)}, f32[12,12,8,128]{3,2,1,0:T(8,128)S(1)}, u32[]{:S(2)}, u32[]{:S(2)}) collective-permute-start(f32[12,12,8,128]{3,2,1,0:T(8,128)S(1)} %get-tuple-element.31.refs_0_), channel_id=1, source_target_pairs={{0,17},{16,0},{1,16},{17,1},{2,19},{18,2},{3,18},{19,3},{4,21},{20... | collective-permute-start | bytes 1769480 | tf_op jit(solution)/shard_map/ppermute | solution.py:351
  51.6 14.1 %collective-permute-start.17 = (f32[12,12,8,128]{3,2,1,0:T(8,128)S(1)}, f32[12,12,8,128]{3,2,1,0:T(8,128)S(1)}, u32[]{:S(2)}, u32[]{:S(2)}) collective-permute-start(f32[12,12,8,128]{3,2,1,0:T(8,128)S(1)} %get-tuple-element.31.refs_0_), channel_id=1, source_target_pairs={{0,16},{16,1},{1,17},{17,0},{2,18},{18,3},{3,19},{19,2},{4,20},{20... | collective-permute-start | bytes 1769480 | tf_op jit(solution)/shard_map/ppermute | solution.py:352
  53.3 15.6 %collective-permute-start.19 = (f32[12,12,8,128]{3,2,1,0:T(8,128)S(1)}, f32[12,12,8,128]{3,2,1,0:T(8,128)S(1)}, u32[]{:S(2)}, u32[]{:S(2)}) collective-permute-start(f32[12,12,8,128]{3,2,1,0:T(8,128)S(1)} %get-tuple-element.31.refs_0_), channel_id=1, source_target_pairs={{0,2},{2,4},{4,6},{6,8},{8,10},{10,12},{12,14},{14,0},{1,3},{3,5},... | collective-permute-start | bytes 1769480 | tf_op jit(solution)/shard_map/ppermute | solution.py:337
  58.2 10.7 %collective-permute-start.20 = (f32[12,12,8,128]{3,2,1,0:T(8,128)S(1)}, f32[12,12,8,128]{3,2,1,0:T(8,128)S(1)}, u32[]{:S(2)}, u32[]{:S(2)}) collective-permute-start(f32[12,12,8,128]{3,2,1,0:T(8,128)S(1)} %get-tuple-element.31.refs_0_), channel_id=1, source_target_pairs={{0,14},{2,0},{4,2},{6,4},{8,6},{10,8},{12,10},{14,12},{1,15},{3,1}... | collective-permute-start | bytes 1769480 | tf_op jit(solution)/shard_map/ppermute | solution.py:337
  60.9 8.8 %collective-permute-start.21 = (f32[6,12,8,128]{3,2,1,0:T(8,128)S(1)}, f32[6,12,8,128]{3,2,1,0:T(8,128)S(1)}, u32[]{:S(2)}, u32[]{:S(2)}) collective-permute-start(f32[6,12,8,128]{3,2,1,0:T(8,128)S(1)} %get-tuple-element.27.low), channel_id=1, source_target_pairs={{0,224},{32,0},{64,32},{96,64},{128,96},{160,128},{192,160},{224,1... | collective-permute-start | bytes 884744 | tf_op jit(solution)/shard_map/ppermute | solution.py:332
  65.3 6.8 %collective-permute-start.23 = (f32[6,12,8,128]{3,2,1,0:T(8,128)S(1)}, f32[6,12,8,128]{3,2,1,0:T(8,128)S(1)}, u32[]{:S(2)}, u32[]{:S(2)}) collective-permute-start(f32[6,12,8,128]{3,2,1,0:T(8,128)S(1)} %slice.9), channel_id=1, source_target_pairs={{0,17},{16,0},{1,16},{17,1},{2,19},{18,2},{3,18},{19,3},{4,21},{20... | collective-permute-start | bytes 884744 | tf_op jit(solution)/shard_map/ppermute | solution.py:353
  65.7 7.1 %collective-permute-start.22 = (f32[6,12,8,128]{3,2,1,0:T(8,128)S(1)}, f32[6,12,8,128]{3,2,1,0:T(8,128)S(1)}, u32[]{:S(2)}, u32[]{:S(2)}) collective-permute-start(f32[6,12,8,128]{3,2,1,0:T(8,128)S(1)} %slice.8), channel_id=1, source_target_pairs={{0,16},{16,1},{1,17},{17,0},{2,18},{18,3},{3,19},{19,2},{4,20},{20... | collective-permute-start | bytes 884744 | tf_op jit(solution)/shard_map/ppermute | solution.py:354
